TPU v7x, 32 devices: a whole 2x2x4 slice. The times are simulated.
32 devices in a mesh: tile: 4 (over y, x), proj: 2 (over core), cuts: 4 (over z).
Axes of the slice: x: 2, y: 2, z: 4, core: 2. Of those that a mesh axis runs over, the one named last changes fastest.
Arguments:
- object_field: float32 [8, 2, 384, 2048], P(('proj', 'cuts'), None, None, 'tile'), may hold values from -5 to 5
- probe_field: float32 [2, 256, 256], replicated, may hold values from -6 to 6
- amplitudes: bfloat16 [8, 4, 6, 256, 256], P(('proj', 'cuts'), 'tile'), may hold values from 0 to 16
- pos_rows: int32 [8, 4, 6], P(('proj', 'cuts'), 'tile'), may hold values from 0 to 128
- pos_cols: int32 [8, 4, 6], P(('proj', 'cuts'), 'tile'), may hold values from 0 to 512
- counts: int32 [8, 4], P(('proj', 'cuts'), 'tile'), may hold values from 1 to 6, as said below
- admm_dual: float32 [8, 32, 2048], P(('proj', 'cuts'), None, 'tile'), may hold values from -4 to 4
- volume: float32 [32, 2048, 2048], P('cuts', ('tile', 'proj')), may hold values from -6 to 6
- proj_weights: bfloat16 [16, 2048, 2048], P(None, ('tile', 'proj')), may hold values from -0.125 to 0.125
- ray_weights: float32 [16, 2048], replicated, may hold values from -0.125 to 0.125
- angle_ids: int32 [8], replicated, may hold values from 0 to 15
Outputs:
- new_object: float32 [8, 2, 384, 2048], P(('proj', 'cuts'), None, None, 'tile')
- new_probe: float32 [2, 256, 256], replicated
- new_volume: float32 [32, 2048, 2048], P('cuts', ('tile', 'proj'))
Inputs may be any that keep to these rules, and one draw needn't show every extreme that they name: `counts`: every tile holds at least one live position and at most 6; exactly one tile of one projection holds 6, every other holds at most 3.
All inputs are finite; a program needn't handle non-finite values.
Results may differ from a plain program's by a relative error of at most 0.00095.
The roundings to bfloat16 on the way count: a program that leaves them out, or rounds other values in their place, can miss the bound.
Values may be sent and summed in bfloat16 or wider, within the bound.
No kernel may reach another device: no remote copies, remote signals or barrier semaphores. Data moves between devices by JAX's collectives and lax.ppermute only.
A program may use at most 128 MiB of HBM per device.

v0:
```python
import math

import jax
import jax.numpy as jnp
import numpy as np
from jax import lax
from jax.experimental import pallas as pl
from jax.experimental.pallas import tpu as pltpu
from jax.sharding import PartitionSpec as P

MIB = 1024 * 1024
VMEM = pltpu.VMEM
F32 = jnp.float32
BF16 = jnp.bfloat16
LANES = 128
SUBLANES = 8
ENERGY_ROWS = 8

tomo_step = 1.0


def shifted(value, axis, steps):
    count = lax.axis_size(axis)
    leading, last = (max(0, -steps), min(count, count - steps))
    return lax.ppermute(value, axis, [(source, source + steps) for source in range(leading, last)])


def dft_blocks(side):
    indices = np.arange(side)
    products = (indices[:, None] * indices[None, :]) % side
    phase = products.astype(np.float32) * np.float32(2.0 * math.pi / side)
    norm = np.float32(1.0 / math.sqrt(side))
    real = np.cos(phase).astype(np.float32) * norm
    imag = -np.sin(phase).astype(np.float32) * norm
    left = np.block([[real, -imag], [imag, real]])
    right = np.block([[real, imag], [-imag, real]])
    return left.astype(jnp.bfloat16), right.astype(jnp.bfloat16)


def dot(left, right):
    return jnp.dot(left, right, preferred_element_type=F32)


def split_bf16(values):
    high = values.astype(BF16).astype(F32)
    low = (values - high).astype(BF16).astype(F32)
    return high, low


def forward_kernel(ids_ref, volume_ref, weights_ref, rays_ref, out_ref, table_ref, sums_ref):
    step = pl.program_id(0)
    depth, projections, _ = sums_ref.shape
    lanes = table_ref.shape[1]
    parts, _, _, share = out_ref.shape

    @pl.when(step == 0)
    def _():
        rows = jnp.concatenate(
            [rays_ref[pl.ds(ids_ref[a], 1), :] for a in range(projections)], axis=0
        )
        high, low = split_bf16(rows)
        stacked = [high, low]
        if lanes > 2 * projections:
            stacked.append(jnp.zeros((lanes - 2 * projections, rows.shape[1]), F32))
        table_ref[...] = jnp.concatenate(stacked, axis=0).T.astype(BF16)

    @pl.when(step < depth)
    def _():
        block = volume_ref[0]
        high = block.astype(BF16)
        low = (block - high.astype(F32)).astype(BF16)
        first = dot(high, table_ref[...]).T
        second = dot(low, table_ref[...]).T
        sums_ref[step] = first[:projections] + (
            first[projections : 2 * projections] + second[:projections]
        )

    @pl.when(step >= depth)
    def _():
        a = step - depth
        rows = sums_ref[:, pl.ds(a, 1), :].reshape(depth, sums_ref.shape[2])
        result = dot(rows.astype(BF16), weights_ref[0])
        for part in range(parts):
            out_ref[part, a] = result[:, part * share : (part + 1) * share]


def forward_parts(angle_ids, volume, proj_weights, ray_weights, parts):
    depth, rows, width = volume.shape
    projections = angle_ids.shape[0]
    angles = ray_weights.shape[0]
    lanes = -(-2 * projections // LANES) * LANES
    share = width // parts
    return pl.pallas_call(
        forward_kernel,
        grid_spec=pltpu.PrefetchScalarGridSpec(
            num_scalar_prefetch=1,
            grid=(depth + projections,),
            in_specs=[
                pl.BlockSpec((1, rows, width), lambda i, ids: (jnp.minimum(i, depth - 1), 0, 0)),
                pl.BlockSpec(
                    (1, rows, width), lambda i, ids: (ids[jnp.maximum(i - depth, 0)], 0, 0)
                ),
                pl.BlockSpec((angles, width), lambda i, ids: (0, 0)),
            ],
            out_specs=pl.BlockSpec((parts, projections, depth, share), lambda i, ids: (0, 0, 0, 0)),
            scratch_shapes=[
                VMEM((width, lanes), BF16),
                VMEM((depth, projections, rows), F32),
            ],
        ),
        out_shape=jax.ShapeDtypeStruct((parts, projections, depth, share), F32),
        compiler_params=pltpu.CompilerParams(vmem_limit_bytes=40 * MIB),
        cost_estimate=pl.CostEstimate(
            flops=4 * depth * rows * width * lanes,
            bytes_accessed=depth * rows * width * 4 + projections * rows * width * 2,
            transcendentals=0,
        ),
        name="forward",
    )(angle_ids, volume, proj_weights, ray_weights)


def placed(values, down, across):
    rows, cols = values.shape
    tall = jnp.concatenate([values, jnp.zeros((SUBLANES, cols), F32)], axis=0)
    tall = pltpu.roll(tall, down, axis=0)
    wide = jnp.concatenate([tall, jnp.zeros((rows + SUBLANES, LANES), F32)], axis=1)
    return pltpu.roll(wide, across, axis=1)


def patch_kernel(
    rows_ref,
    cols_ref,
    count_ref,
    own_ref,
    left_ref,
    right_ref,
    probe_ref,
    amp_ref,
    dft_a_ref,
    dft_b_ref,
    dual_ref,
    new_ref,
    edge_left_ref,
    edge_right_ref,
    slab_ref,
    slab_left_ref,
    slab_right_ref,
    grad_ref,
    ext_ref,
    sum_ref,
    patch_ref,
    wave_ref,
    half_ref,
    far_ref,
    energy_ref,
):
    side = probe_ref.shape[1]
    margin = left_ref.shape[2]
    tile_cols = own_ref.shape[2]
    window = side + LANES
    chunk = 32
    tall = chunk + SUBLANES
    height = own_ref.shape[1]

    for c in range(2):
        ext_ref[c, :height, :margin] = left_ref[c]
        ext_ref[c, :height, margin : margin + tile_cols] = own_ref[c]
        ext_ref[c, :height, margin + tile_cols : 2 * margin + tile_cols] = right_ref[c]
    sum_ref[...] = jnp.zeros(sum_ref.shape, F32)
    grad_ref[...] = jnp.zeros(grad_ref.shape, F32)
    energy_ref[...] = jnp.zeros(energy_ref.shape, F32)

    def slot_step(slot, carry):
        row = rows_ref[slot]
        col = cols_ref[slot]
        lane = lax.rem(col, LANES)
        base = pl.multiple_of(col - lane, LANES)
        back_shift = lax.rem(window - lane, window)
        notch = lax.rem(row, SUBLANES)
        top = pl.multiple_of(row - notch, SUBLANES)
        up_shift = lax.rem(tall - notch, tall)
        for r in range(0, side, chunk):
            cells = pl.ds(top + r, tall)
            here = slice(r, r + chunk)
            below = slice(side + r, side + r + chunk)
            x_re = pltpu.roll(ext_ref[0, cells, pl.ds(base, window)], back_shift, axis=1)[:, :side]
            x_im = pltpu.roll(ext_ref[1, cells, pl.ds(base, window)], back_shift, axis=1)[:, :side]
            x_re = pltpu.roll(x_re, up_shift, axis=0)[:chunk]
            x_im = pltpu.roll(x_im, up_shift, axis=0)[:chunk]
            p_re = probe_ref[0, here, :]
            p_im = probe_ref[1, here, :]
            patch_ref[here, :] = x_re
            patch_ref[below, :] = x_im
            wave_ref[here, :] = (p_re * x_re - p_im * x_im).astype(BF16)
            wave_ref[below, :] = (p_re * x_im + p_im * x_re).astype(BF16)
            power = x_re * x_re + x_im * x_im
            energy_ref[...] += jnp.sum(power.reshape(chunk // 8, 8, side), axis=0)
        half_ref[:, :side] = dot(dft_a_ref[:side, :], wave_ref[...]).astype(BF16)
        half_ref[:, side:] = dot(dft_a_ref[side:, :], wave_ref[...]).astype(BF16)
        far_ref[...] = dot(half_ref[...], dft_b_ref[...])
        for r in range(0, side, chunk):
            here = slice(r, r + chunk)
            below = slice(side + r, side + r + chunk)
            f_re = far_ref[here, :side]
            f_im = far_ref[here, side:]
            inverse = lax.rsqrt(f_re * f_re + f_im * f_im + 0.25)
            factor = amp_ref[slot, here, :].astype(F32) * inverse - 1.0
            wave_ref[here, :] = (f_re * factor).astype(BF16)
            wave_ref[below, :] = (f_im * factor).astype(BF16)
        half_ref[:, :side] = dot(dft_b_ref[:side, :], wave_ref[...]).astype(BF16)
        half_ref[:, side:] = dot(dft_b_ref[side:, :], wave_ref[...]).astype(BF16)
        far_ref[...] = dot(half_ref[...], dft_a_ref[...])
        for r in range(0, side, chunk):
            cells = pl.ds(top + r, tall)
            here = slice(r, r + chunk)
            below = slice(side + r, side + r + chunk)
            b_re = far_ref[here, :side]
            b_im = far_ref[here, side:]
            p_re = probe_ref[0, here, :]
            p_im = probe_ref[1, here, :]
            x_re = patch_ref[here, :]
            x_im = patch_ref[below, :]
            o_re = p_re * b_re + p_im * b_im
            o_im = p_re * b_im - p_im * b_re
            sum_ref[0, cells, pl.ds(base, window)] += placed(o_re, notch, lane)
            sum_ref[1, cells, pl.ds(base, window)] += placed(o_im, notch, lane)
            grad_ref[here, :] += x_re * b_re + x_im * b_im
            grad_ref[below, :] += x_re * b_im - x_im * b_re
        return carry

    lax.fori_loop(0, count_ref[0], slot_step, 0)

    grad_ref[2 * side :, :] = energy_ref[...]
    p_re = probe_ref[0]
    p_im = probe_ref[1]
    peak = jnp.max(p_re * p_re + p_im * p_im)
    scale = 1.0 / (jnp.full((1, LANES), peak, F32) + 1e-05)
    wide = jnp.tile(scale, (1, tile_cols // LANES))
    for c in range(2):
        new_ref[c] = own_ref[c] + sum_ref[c, :height, margin : margin + tile_cols] * wide
        edge_left_ref[c] = sum_ref[c, :height, :margin] * scale
        edge_right_ref[c] = sum_ref[c, :height, margin + tile_cols : 2 * margin + tile_cols] * scale
    slab_rows = dual_ref.shape[0]
    first = (own_ref.shape[1] - slab_rows) // 2
    slab_ref[...] = new_ref[1, first : first + slab_rows, :] + dual_ref[...]
    slab_left_ref[...] = edge_left_ref[1, first : first + slab_rows, :]
    slab_right_ref[...] = edge_right_ref[1, first : first + slab_rows, :]


def patch_updates(rows, cols, count, own, left, right, probe, amplitudes, dual):
    side = probe.shape[1]
    _, height, tile_cols = own.shape
    margin = left.shape[2]
    slots = amplitudes.shape[0]
    slab_rows = dual.shape[0]
    dft_a, dft_b = dft_blocks(side)
    full = pl.BlockSpec(memory_space=VMEM)
    scalars = pl.BlockSpec(memory_space=pltpu.SMEM)
    extent = tile_cols + 2 * margin + LANES
    shape = jax.ShapeDtypeStruct
    return pl.pallas_call(
        patch_kernel,
        in_specs=[scalars] * 3 + [full] * 8,
        out_specs=[full] * 7,
        out_shape=[
            shape((2, height, tile_cols), F32),
            shape((2, height, margin), F32),
            shape((2, height, margin), F32),
            shape((slab_rows, tile_cols), F32),
            shape((slab_rows, margin), F32),
            shape((slab_rows, margin), F32),
            shape((2 * side + ENERGY_ROWS, side), F32),
        ],
        scratch_shapes=[
            VMEM((2, height + SUBLANES, extent), F32),
            VMEM((2, height + SUBLANES, extent), F32),
            VMEM((2 * side, side), F32),
            VMEM((2 * side, side), BF16),
            VMEM((side, 2 * side), BF16),
            VMEM((side, 2 * side), F32),
            VMEM((ENERGY_ROWS, side), F32),
        ],
        compiler_params=pltpu.CompilerParams(vmem_limit_bytes=40 * MIB),
        cost_estimate=pl.CostEstimate(
            flops=slots * 32 * side**3,
            bytes_accessed=8 * height * tile_cols * 4,
            transcendentals=slots * side * side,
        ),
        name="patches",
    )(
        rows,
        cols,
        count,
        own,
        left,
        right,
        probe,
        amplitudes,
        jnp.asarray(dft_a),
        jnp.asarray(dft_b),
        dual,
    )


def update_kernel(
    ids_ref, residual_ref, weights_ref, rays_ref, volume_ref, out_ref, turned_ref, total_ref, stack_ref, rays_bf_ref
):
    step = pl.program_id(0)
    parts, projections, depth, share = residual_ref.shape
    both = projections * depth

    @pl.when(step == 0)
    def _():
        for part in range(parts):
            block = residual_ref[part].astype(F32).reshape(both, share)
            turned_ref[part * share : (part + 1) * share, :] = block.T
        total_ref[...] = jnp.zeros(total_ref.shape, F32)
        width = rays_ref.shape[1]
        rows = jnp.concatenate(
            [
                jnp.broadcast_to(rays_ref[pl.ds(ids_ref[a], 1), :], (depth, width))
                for a in range(projections)
            ],
            axis=0,
        )
        high, low = split_bf16(rows)
        for place, block in enumerate((high, high, low, low)):
            rays_bf_ref[place * both : (place + 1) * both, :] = block.astype(BF16)

    @pl.when(step < projections)
    def _():
        lane = lax.broadcasted_iota(jnp.int32, turned_ref.shape, 1)
        begin = step * depth
        kept = jnp.logical_and(lane >= begin, lane < begin + depth)
        chosen = jnp.where(kept, turned_ref[...], 0.0).astype(BF16)
        total_ref[...] += dot(weights_ref[0], chosen)

    @pl.when(step == projections)
    def _():
        high, low = split_bf16(total_ref[...])
        stack_ref[...] = jnp.concatenate([high, low, high, low], axis=1)

    @pl.when(step >= projections)
    def _():
        lane = lax.broadcasted_iota(jnp.int32, stack_ref.shape, 1)
        kept = lax.rem(lane, depth) == step - projections
        chosen = jnp.where(kept, stack_ref[...], 0.0).astype(BF16)
        out_ref[0] = volume_ref[0] - tomo_step * dot(chosen, rays_bf_ref[...])


def volume_update(angle_ids, residual, proj_weights, ray_weights, volume):
    depth, rows, width = volume.shape
    projections = angle_ids.shape[0]
    angles = ray_weights.shape[0]
    parts, _, _, share = residual.shape
    both = projections * depth
    return pl.pallas_call(
        update_kernel,
        grid_spec=pltpu.PrefetchScalarGridSpec(
            num_scalar_prefetch=1,
            grid=(projections + depth,),
            in_specs=[
                pl.BlockSpec((parts, projections, depth, share), lambda i, ids: (0, 0, 0, 0)),
                pl.BlockSpec(
                    (1, rows, width), lambda i, ids: (ids[jnp.minimum(i, projections - 1)], 0, 0)
                ),
                pl.BlockSpec((angles, width), lambda i, ids: (0, 0)),
                pl.BlockSpec(
                    (1, rows, width), lambda i, ids: (jnp.maximum(i - projections, 0), 0, 0)
                ),
            ],
            out_specs=pl.BlockSpec(
                (1, rows, width), lambda i, ids: (jnp.maximum(i - projections, 0), 0, 0)
            ),
            scratch_shapes=[
                VMEM((width, both), F32),
                VMEM((rows, both), F32),
                VMEM((rows, 4 * both), F32),
                VMEM((4 * both, width), BF16),
            ],
        ),
        out_shape=jax.ShapeDtypeStruct((depth, rows, width), F32),
        compiler_params=pltpu.CompilerParams(vmem_limit_bytes=48 * MIB),
        cost_estimate=pl.CostEstimate(
            flops=2 * rows * width * both * (projections + 4 * depth),
            bytes_accessed=2 * depth * rows * width * 4 + projections * rows * width * 2,
            transcendentals=0,
        ),
        name="update",
    )(angle_ids, residual, proj_weights, ray_weights, volume)


def probe_update(grad, probe):
    side = probe.shape[1]
    flat_axes = ("tile", "proj")
    plane = lax.axis_size("tile") * lax.axis_size("proj")
    layers = lax.axis_size("cuts")
    plane_rows = 2 * side // plane
    layer_rows = plane_rows // layers
    values = grad[: 2 * side].reshape(plane, plane_rows, side)
    energy = jnp.broadcast_to(grad[2 * side :][None], (plane, ENERGY_ROWS, side))
    sent = jnp.concatenate([values, energy], axis=1)
    summed = jnp.sum(lax.all_to_all(sent, flat_axes, 0, 0, tiled=True), axis=0)
    values = summed[:plane_rows].reshape(layers, layer_rows, side)
    energy = jnp.broadcast_to(summed[plane_rows:][None], (layers, ENERGY_ROWS, side))
    sent = jnp.concatenate([values, energy], axis=1)
    summed = jnp.sum(lax.all_to_all(sent, "cuts", 0, 0, tiled=True), axis=0)
    energy = jnp.sum(summed[layer_rows:]) / (side * side)
    part = lax.axis_index(flat_axes) * layers + lax.axis_index("cuts")
    own = lax.dynamic_slice(
        probe.reshape(2 * side, side), (part * layer_rows, jnp.zeros((), jnp.int32)), (layer_rows, side)
    )
    new_rows = own + summed[:layer_rows] / (energy + 1e-05)
    new_rows = lax.all_gather(new_rows, "cuts", axis=0, tiled=True)
    new_rows = lax.all_gather(new_rows, flat_axes, axis=0, tiled=True)
    return new_rows.reshape(2, side, side)


def on_device(
    object_field,
    probe_field,
    amplitudes,
    pos_rows,
    pos_cols,
    counts,
    admm_dual,
    volume,
    proj_weights,
    ray_weights,
    angle_ids,
):
    margin = probe_field.shape[1] // 2
    own = object_field[0]
    tile_cols = own.shape[2]
    flat_axes = ("tile", "proj")
    plane = lax.axis_size("tile") * lax.axis_size("proj")
    proj_count = lax.axis_size("proj")
    layers = lax.axis_size("cuts")
    from_left = shifted(own[:, :, tile_cols - margin :], "tile", 1)
    from_right = shifted(own[:, :, :margin], "tile", -1)
    forward = forward_parts(angle_ids, volume, proj_weights, ray_weights, plane)
    arrived = lax.all_to_all(forward, flat_axes, 0, 0, tiled=True)
    partial_new, edge_left, edge_right, slab, slab_left, slab_right, grad = patch_updates(
        pos_rows[0, 0],
        pos_cols[0, 0],
        counts[0],
        own,
        from_left,
        from_right,
        probe_field,
        amplitudes[0, 0],
        admm_dual[0],
    )
    slab_from_right = shifted(slab_left, "tile", -1)
    slab_from_left = shifted(slab_right, "tile", 1)
    edge_from_right = shifted(edge_left, "tile", -1)
    edge_from_left = shifted(edge_right, "tile", 1)
    slab = slab + jnp.pad(slab_from_left, ((0, 0), (0, tile_cols - margin)))
    slab = slab + jnp.pad(slab_from_right, ((0, 0), (tile_cols - margin, 0)))
    slab_rows = slab.shape[0]
    depth = slab_rows // layers
    share = tile_cols // proj_count
    pieces = slab.reshape(layers, depth, proj_count, share).transpose(2, 0, 1, 3)
    pieces = pieces.reshape(proj_count * layers, depth, share)
    target = lax.all_to_all(pieces, ("proj", "cuts"), 0, 0, tiled=True)
    residual = (jnp.sum(arrived, axis=0) - target).astype(BF16)
    residual = lax.all_gather(residual[None], flat_axes, axis=0, tiled=True)
    new_volume = volume_update(angle_ids, residual, proj_weights, ray_weights, volume)
    new_object = partial_new.at[:, :, :margin].add(edge_from_left)
    new_object = new_object.at[:, :, tile_cols - margin :].add(edge_from_right)
    new_probe = probe_update(grad, probe_field)
    return (new_object[None], new_probe, new_volume)


def solution(mesh):
    in_specs = (
        P(("proj", "cuts"), None, None, "tile"),
        P(),
        P(("proj", "cuts"), "tile", None, None, None),
        P(("proj", "cuts"), "tile", None),
        P(("proj", "cuts"), "tile", None),
        P(("proj", "cuts"), "tile"),
        P(("proj", "cuts"), None, "tile"),
        P("cuts", ("tile", "proj"), None),
        P(None, ("tile", "proj"), None),
        P(),
        P(),
    )
    out_specs = (P(("proj", "cuts"), None, None, "tile"), P(), P("cuts", ("tile", "proj"), None))
    return jax.shard_map(
        on_device, mesh=mesh, in_specs=in_specs, out_specs=out_specs, check_vma=False
    )
```

profile of v0, /device:TPU:0, one launch (start us, length us, event | category | flops | bytes accessed | tf_op | source)
XLA Modules:
  0.0 153.8 jit_solution(12628402312802541145)
XLA Ops:
  0.7 1.2 fusion.3
  1.9 1.3 collective-permute-start.1
  3.2 0.0 copy-start.3
  3.2 0.0 copy-start.10
  3.2 0.0 copy-start.11
  3.2 0.0 copy-start.12
  3.2 5.6 %collective-permute-start = (f32[2,384,128]{2,1,0:T(8,128)S(1)}, f32[2,384,128]{2,1,0:T(8,128)S(1)}, u32[]{:S(2)}, u32[]{:S(2)}) collective-permute-start(f32[2,384,128]{2,1,0:T(8,128)S(1)} %get-tuple-element.42), channel_id=1, source_target_pairs={{0,8},{8,16},{16,24},{1,9},{9,17},{17,25},{2,10},{10,18},{18,26},{... | collective-permute-start | bytes 1179656 | tf_op jit(solution)/shard_map/ppermute | solution.py:25
  8.9 18.4 %forward.1 = f32[8,8,8,256]{3,2,1,0:T(8,128)} custom-call(s32[8]{0:T(128)S(1)} %copy-done.2, f32[8,256,2048]{2,1,0:T(8,128)} %volume_ref.3, bf16[16,256,2048]{2,1,0:T(8,128)(2,1)} %weights_ref.3, f32[16,2048]{1,0:T(8,128)S(1)} %copy-done), custom_call_target="tpu_custom_call" | custom-call | flops 2147483648 | bytes 25165824 | tf_op jit(solution)/shard_map/forward/pallas_call | solution.py:93
  27.2 4.2 %all-to-all-start.2 = ((f32[8,8,8,256]{3,2,1,0:T(8,128)}), f32[8,8,8,256]{3,2,1,0:T(8,128)}, u32[]{:S(2)}, u32[]{:S(2)}) async-start(f32[8,8,8,256]{3,2,1,0:T(8,128)} %forward.1), calls=%async_computation.2 | async-start | bytes 1048576 | tf_op jit(solution)/shard_map/all_to_all | solution.py:442
  32.1 0.0 collective-permute-done.1.right_ref
  32.1 0.0 copy-start.6
  32.1 0.7 copy-done.6
  32.8 0.7 copy-done.8
  33.6 0.0 copy-start.1
  33.6 1.4 copy-done.1
  35.0 1.1 copy-done.4
  36.1 1.0 copy-done.7
  37.1 1.0 copy-done.9
  38.1 1.0 copy-done.13
  39.2 1.0 copy-done.14
  40.2 6.6 %patches.1 = (f32[2,384,512]{2,1,0:T(8,128)S(1)}, f32[2,384,128]{2,1,0:T(8,128)S(1)}, f32[2,384,128]{2,1,0:T(8,128)S(1)}, f32[32,512]{1,0:T(8,128)S(1)}, f32[32,...) custom-call(s32[6]{0:T(128)S(1)} %bitcast.28, s32[6]{0:T(128)S(1)} %bitcast.29, ...), custom_call_target="tpu_custom_call" | custom-call | flops 3221225472 | bytes 6291456 | tf_op jit(solution)/shard_map/patches/pallas_call | solution.py:261
  46.8 0.7 copy-done.5
  47.6 3.0 %collective-permute-start.4 = (f32[32,128]{1,0:T(8,128)S(1)}, f32[32,128]{1,0:T(8,128)S(1)}, u32[]{:S(2)}, u32[]{:S(2)}) collective-permute-start(f32[32,128]{1,0:T(8,128)S(1)} %get-tuple-element.39), channel_id=1, source_target_pairs={{0,8},{8,16},{16,24},{1,9},{9,17},{17,25},{2,10},{10,18},{18,26},{... | collective-permute-start | bytes 49160 | tf_op jit(solution)/shard_map/ppermute | solution.py:25
  50.6 1.3 collective-permute-start.5
  51.9 0.8 slice.76
  52.7 10.9 %collective-permute-start.2 = (f32[2,384,128]{2,1,0:T(8,128)}, f32[2,384,128]{2,1,0:T(8,128)}, u32[]{:S(2)}, u32[]{:S(2)}) collective-permute-start(f32[2,384,128]{2,1,0:T(8,128)} %copy-done.5), channel_id=1, source_target_pairs={{0,8},{8,16},{16,24},{1,9},{9,17},{17,25},{2,10},{10,18},{18,26},{... | collective-permute-start | bytes 1179656 | tf_op jit(solution)/shard_map/ppermute | solution.py:25
  63.6 1.3 collective-permute-start.3
  64.9 0.0 collective-permute-done.4
  64.9 0.0 collective-permute-done.5
  64.9 0.6 copy.18
  65.5 3.4 %all-to-all-start.3 = ((f32[8,8,256]{2,1,0:T(8,128)}), f32[8,8,256]{2,1,0:T(8,128)S(1)}, u32[]{:S(2)}, u32[]{:S(2)}) async-start(f32[8,8,256]{2,1,0:T(8,128)} %bitcast.14), calls=%async_computation.3 | async-start | bytes 131072 | tf_op jit(solution)/shard_map/all_to_all | solution.py:465
  68.9 1.9 %pad_maximum_fusion = f32[8,72,256]{2,1,0:T(8,128)} fusion(f32[8,8,256]{2,1,0:T(8,128)S(1)} %broadcast_in_dim.22, f32[8,64,256]{2,1,0:T(8,128)} %bitcast.30), kind=kLoop, calls=%fused_computation | loop fusion | flops 147456 | bytes 1179648 | tf_op jit(solution)/shard_map/concatenate | solution.py:402
  70.8 1.1 reduce_sum.39
  71.9 2.9 %all-to-all-done.3 = f32[8,8,256]{2,1,0:T(8,128)S(1)} async-done(((f32[8,8,256]{2,1,0:T(8,128)}), f32[8,8,256]{2,1,0:T(8,128)S(1)}, u32[]{:S(2)}, u32[]{:S(2)}) %all-to-all-start.3) | async-done | bytes 65568 | tf_op jit(solution)/shard_map/all_to_all | solution.py:465
  74.8 5.5 %all-to-all-start = ((f32[8,72,256]{2,1,0:T(8,128)}), f32[8,72,256]{2,1,0:T(8,128)S(1)}, u32[]{:S(2)}, u32[]{:S(2)}) async-start(f32[8,72,256]{2,1,0:T(8,128)} %pad_maximum_fusion), calls=%async_computation | async-start | bytes 1179648 | tf_op jit(solution)/shard_map/all_to_all | solution.py:403
  80.4 14.1 %all-gather = bf16[64,8,256]{2,1,0:T(8,128)(2,1)S(1)} all-gather(bf16[8,8,256]{2,1,0:T(8,128)(2,1)S(1)} %subtract_convert_fusion), channel_id=2, replica_groups=mesh['tile'=4,'proj'=2,'cuts'=4] {'tile','proj'}, dimensions={0}, use_global_device_ids=true | all-gather | bytes 294912 | tf_op jit(solution)/shard_map/all_gather | solution.py:467
  94.4 22.8 %update.1 = f32[8,256,2048]{2,1,0:T(8,128)} custom-call(s32[8]{0:T(128)S(1)} %copy-done.2, bf16[8,8,8,256]{3,2,1,0:T(8,128)(2,1)S(1)} %bitcast.22, bf16[16,256,2048]{2,1,0:T(8,128)(2,1)} %weights_ref.3, f32[16,2048]{1,0:T(8,128)S(1)} %copy-done, f32[8,256,2048]{2,1,0:T(8,128)} %volume_ref.3), custom_call_target="tpu_custom_call" | custom-call | flops 2684354560 | bytes 41943040 | tf_op jit(solution)/shard_map/update/pallas_call | solution.py:357
  117.2 1.1 add_dynamic-update-slice_fusion
  118.3 1.1 copy.20
  119.5 0.7 pad_maximum_fusion.1
  120.2 3.3 %all-to-all-start.1 = ((f32[4,24,256]{2,1,0:T(8,128)}), f32[4,24,256]{2,1,0:T(8,128)S(1)}, u32[]{:S(2)}, u32[]{:S(2)}) async-start(f32[4,24,256]{2,1,0:T(8,128)} %pad_maximum_fusion.1), calls=%async_computation.1 | async-start | bytes 196608 | tf_op jit(solution)/shard_map/all_to_all | solution.py:407
  123.5 0.0 collective-permute-done.3
  123.5 1.8 %fusion.1 = f32[1,2,384,512]{3,2,1,0:T(8,128)} fusion(f32[1,2,384,512]{3,2,1,0:T(8,128)} %copy.20, f32[2,384,128]{2,1,0:T(8,128)} %collective-permute-done.3, f32[2,384,512]{2,1,0:T(8,128)S(1)} %add_dynamic-update-slice_fusion), kind=kLoop, calls=%fused_computation.3 | loop fusion | flops 98304 | bytes 1179648 | tf_op jit(solution)/shard_map/scatter-add | solution.py:470
  125.3 4.1 %all-to-all-done.1 = f32[4,24,256]{2,1,0:T(8,128)S(1)} async-done(((f32[4,24,256]{2,1,0:T(8,128)}), f32[4,24,256]{2,1,0:T(8,128)S(1)}, u32[]{:S(2)}, u32[]{:S(2)}) %all-to-all-start.1) | async-done | bytes 98336 | tf_op jit(solution)/shard_map/all_to_all | solution.py:407
  129.5 0.6 slice_reduce_fusion
  130.8 13.2 %all_gather.9 = f32[64,256]{1,0:T(8,128)S(1)} all-gather(f32[16,256]{1,0:T(8,128)S(1)} %fusion.2), channel_id=1, replica_groups=mesh['tile'=4,'proj'=2,'cuts'=4] {'cuts'}, dimensions={0}, use_global_device_ids=true | all-gather | bytes 81920 | tf_op jit(solution)/shard_map/all_gather | solution.py:414
  144.0 9.1 %all_gather.10 = f32[512,256]{1,0:T(8,128)S(1)} all-gather(f32[64,256]{1,0:T(8,128)S(1)} %all_gather.9), channel_id=1, replica_groups=mesh['tile'=4,'proj'=2,'cuts'=4] {'tile','proj'}, dimensions={0}, use_global_device_ids=true | all-gather | bytes 589824 | tf_op jit(solution)/shard_map/all_gather | solution.py:415
  153.0 0.8 copy.23
  (29 shorter events, 0.1 us)
Async XLA Ops:
  0.6 8.2 %copy-start.2 = (s32[8]{0:T(128)S(1)}, s32[8]{0:T(128)}, u32[]{:S(2)}) copy-start(s32[8]{0:T(128)} %ids_ref.3) | copy-start | bytes 100
  0.6 8.2 %copy-start = (f32[16,2048]{1,0:T(8,128)S(1)}, f32[16,2048]{1,0:T(8,128)}, u32[]{:S(2)}) copy-start(f32[16,2048]{1,0:T(8,128)} %rays_ref.3) | copy-start | bytes 393220
  1.9 30.2 %collective-permute-start.1 = (f32[2,384,128]{2,1,0:T(8,128)S(1)}, f32[2,384,128]{2,1,0:T(8,128)S(1)}, u32[]{:S(2)}, u32[]{:S(2)}) collective-permute-start(f32[2,384,128]{2,1,0:T(8,128)S(1)} %get-tuple-element.41), channel_id=1, source_target_pairs={{8,0},{16,8},{24,16},{9,1},{17,9},{25,17},{10,2},{18,10},{26,18},{... | collective-permute-start | bytes 1179656 | tf_op jit(solution)/shard_map/ppermute | solution.py:25
  3.2 30.4 %copy-start.3 = (f32[2,256,256]{2,1,0:T(8,128)S(1)}, f32[2,256,256]{2,1,0:T(8,128)}, u32[]{:S(2)}) copy-start(f32[2,256,256]{2,1,0:T(8,128)} %probe_ref.1) | copy-start | bytes 1572868
  3.2 30.4 %copy-start.10 = (f32[1,32,512]{2,1,0:T(8,128)S(1)}, f32[1,32,512]{2,1,0:T(8,128)}, u32[]{:S(2)}) copy-start(f32[1,32,512]{2,1,0:T(8,128)} %param.23) | copy-start | bytes 196612
  3.2 30.4 %copy-start.11 = (s32[1,1,6]{2,1,0:T(1,128)S(1)}, s32[1,1,6]{2,1,0:T(1,128)}, u32[]{:S(2)}) copy-start(s32[1,1,6]{2,1,0:T(1,128)} %param.20) | copy-start | bytes 76
  3.2 30.4 %copy-start.12 = (s32[1,1,6]{2,1,0:T(1,128)S(1)}, s32[1,1,6]{2,1,0:T(1,128)}, u32[]{:S(2)}) copy-start(s32[1,1,6]{2,1,0:T(1,128)} %param.21) | copy-start | bytes 76
  3.2 29.6 %collective-permute-start = (f32[2,384,128]{2,1,0:T(8,128)S(1)}, f32[2,384,128]{2,1,0:T(8,128)S(1)}, u32[]{:S(2)}, u32[]{:S(2)}) collective-permute-start(f32[2,384,128]{2,1,0:T(8,128)S(1)} %get-tuple-element.42), channel_id=1, source_target_pairs={{0,8},{8,16},{16,24},{1,9},{9,17},{17,25},{2,10},{10,18},{18,26},{... | collective-permute-start | bytes 1179656 | tf_op jit(solution)/shard_map/ppermute | solution.py:25
  27.2 38.3 %all-to-all-start.2 = ((f32[8,8,8,256]{3,2,1,0:T(8,128)}), f32[8,8,8,256]{3,2,1,0:T(8,128)}, u32[]{:S(2)}, u32[]{:S(2)}) async-start(f32[8,8,8,256]{3,2,1,0:T(8,128)} %forward.1), calls=%async_computation.2 | async-start | bytes 1048576 | tf_op jit(solution)/shard_map/all_to_all | solution.py:442
  32.1 0.7 copy-start.6
  32.8 0.7 copy-start.8
  33.6 1.4 copy-start.1
  35.0 1.1 copy-start.4
  36.1 1.0 copy-start.7
  37.1 1.0 copy-start.9
  38.1 1.0 copy-start.13
  39.2 1.0 copy-start.14
  46.8 0.7 copy-start.5
  47.6 17.3 %collective-permute-start.4 = (f32[32,128]{1,0:T(8,128)S(1)}, f32[32,128]{1,0:T(8,128)S(1)}, u32[]{:S(2)}, u32[]{:S(2)}) collective-permute-start(f32[32,128]{1,0:T(8,128)S(1)} %get-tuple-element.39), channel_id=1, source_target_pairs={{0,8},{8,16},{16,24},{1,9},{9,17},{17,25},{2,10},{10,18},{18,26},{... | collective-permute-start | bytes 49160 | tf_op jit(solution)/shard_map/ppermute | solution.py:25
  50.6 14.3 %collective-permute-start.5 = (f32[32,128]{1,0:T(8,128)S(1)}, f32[32,128]{1,0:T(8,128)S(1)}, u32[]{:S(2)}, u32[]{:S(2)}) collective-permute-start(f32[32,128]{1,0:T(8,128)S(1)} %get-tuple-element.40), channel_id=1, source_target_pairs={{8,0},{16,8},{24,16},{9,1},{17,9},{25,17},{10,2},{18,10},{26,18},{... | collective-permute-start | bytes 49160 | tf_op jit(solution)/shard_map/ppermute | solution.py:25
  52.7 64.5 %collective-permute-start.2 = (f32[2,384,128]{2,1,0:T(8,128)}, f32[2,384,128]{2,1,0:T(8,128)}, u32[]{:S(2)}, u32[]{:S(2)}) collective-permute-start(f32[2,384,128]{2,1,0:T(8,128)} %copy-done.5), channel_id=1, source_target_pairs={{0,8},{8,16},{16,24},{1,9},{9,17},{17,25},{2,10},{10,18},{18,26},{... | collective-permute-start | bytes 1179656 | tf_op jit(solution)/shard_map/ppermute | solution.py:25
  63.6 59.9 %collective-permute-start.3 = (f32[2,384,128]{2,1,0:T(8,128)S(1)}, f32[2,384,128]{2,1,0:T(8,128)}, u32[]{:S(2)}, u32[]{:S(2)}) collective-permute-start(f32[2,384,128]{2,1,0:T(8,128)S(1)} %get-tuple-element.36), channel_id=1, source_target_pairs={{8,0},{16,8},{24,16},{9,1},{17,9},{25,17},{10,2},{18,10},{26,18},{... | collective-permute-start | bytes 1179656 | tf_op jit(solution)/shard_map/ppermute | solution.py:25
  65.5 9.3 %all-to-all-start.3 = ((f32[8,8,256]{2,1,0:T(8,128)}), f32[8,8,256]{2,1,0:T(8,128)S(1)}, u32[]{:S(2)}, u32[]{:S(2)}) async-start(f32[8,8,256]{2,1,0:T(8,128)} %bitcast.14), calls=%async_computation.3 | async-start | bytes 131072 | tf_op jit(solution)/shard_map/all_to_all | solution.py:465
  74.8 44.6 %all-to-all-start = ((f32[8,72,256]{2,1,0:T(8,128)}), f32[8,72,256]{2,1,0:T(8,128)S(1)}, u32[]{:S(2)}, u32[]{:S(2)}) async-start(f32[8,72,256]{2,1,0:T(8,128)} %pad_maximum_fusion), calls=%async_computation | async-start | bytes 1179648 | tf_op jit(solution)/shard_map/all_to_all | solution.py:403
  120.2 9.3 %all-to-all-start.1 = ((f32[4,24,256]{2,1,0:T(8,128)}), f32[4,24,256]{2,1,0:T(8,128)S(1)}, u32[]{:S(2)}, u32[]{:S(2)}) async-start(f32[4,24,256]{2,1,0:T(8,128)} %pad_maximum_fusion.1), calls=%async_computation.1 | async-start | bytes 196608 | tf_op jit(solution)/shard_map/all_to_all | solution.py:407
where the time goes:
time: 154 us
  Pallas kernels  47.7 us (31%)
  starting transfers between devices  39.7 us (26%)
  blocking collectives  36.4 us (24%)
  local copies, waits for them, and re-layouts  13.5 us (9%)
  other arithmetic  7.25 us (5%)
  waiting for transfers between devices  7.05 us (5%)
  between operations  2.22 us (1%)
    ppermute x6, starting transfers between devices, shifted(): lax.ppermute(value, axis, [(source, source + steps) for source in range(l...  23.3 us
    pallas_call x1, Pallas kernels, volume_update(): pl.pallas_call(update_kernel, grid_spec=pltpu.PrefetchScalarGridSpec(num_...  22.8 us
    pallas_call x1, Pallas kernels, forward_parts(): pl.pallas_call(forward_kernel, grid_spec=pltpu.PrefetchScalarGridSpec(num...  18.4 us
    all_gather x1, blocking collectives, on_device(): residual = lax.all_gather(residual[None], flat_axes, axis=0, tiled=True)  14.1 us
    all_gather x1, blocking collectives, probe_update(): new_rows = lax.all_gather(new_rows, 'cuts', axis=0, tiled=True)  13.2 us
    unnamed x32, local copies, waits for them, and re-layouts  10.8 us
    all_gather x1, blocking collectives, probe_update(): new_rows = lax.all_gather(new_rows, flat_axes, axis=0, tiled=True)  9.08 us
    pallas_call x1, Pallas kernels, patch_updates(): pl.pallas_call(patch_kernel, in_specs=[scalars] * 3 + [full] * 8, out_spe...  6.59 us
  transfers between devices with their start and end apart: 10, of which 2 were waited for; matrix products, arithmetic and copies ran while one was open for 6% of the time, Pallas kernels for 31%

commit v1 on v0

v1 whole, which is shorter than its diff:
```python
import math

import jax
import jax.numpy as jnp
import numpy as np
from jax import lax
from jax.experimental import pallas as pl
from jax.experimental.pallas import tpu as pltpu
from jax.sharding import PartitionSpec as P

MIB = 1024 * 1024
VMEM = pltpu.VMEM
F32 = jnp.float32
BF16 = jnp.bfloat16
LANES = 128
SUBLANES = 8
ENERGY_ROWS = 8
AHEAD = 4

tomo_step = 1.0


def shifted(value, axis, steps):
    count = lax.axis_size(axis)
    leading, last = (max(0, -steps), min(count, count - steps))
    return lax.ppermute(value, axis, [(source, source + steps) for source in range(leading, last)])


def dft_blocks(side):
    indices = np.arange(side)
    products = (indices[:, None] * indices[None, :]) % side
    phase = products.astype(np.float32) * np.float32(2.0 * math.pi / side)
    norm = np.float32(1.0 / math.sqrt(side))
    real = np.cos(phase).astype(np.float32) * norm
    imag = -np.sin(phase).astype(np.float32) * norm
    left = np.block([[real, -imag], [imag, real]])
    right = np.block([[real, imag], [-imag, real]])
    return left.astype(jnp.bfloat16), right.astype(jnp.bfloat16)


def dot(left, right):
    return jnp.dot(left, right, preferred_element_type=F32)


def split_bf16(values):
    high = values.astype(BF16).astype(F32)
    low = (values - high).astype(BF16).astype(F32)
    return high, low


def forward_kernel(
    ids_ref,
    rays_ref,
    volume_ref,
    weights_ref,
    out_ref,
    volume_keep,
    weights_keep,
    rays_keep,
    table_ref,
    sums_ref,
    volume_sem,
    weights_sem,
):
    depth, projections, _ = sums_ref.shape
    width, lanes = table_ref.shape
    parts, _, _, share = out_ref.shape
    both = projections * depth

    def volume_copy(z):
        return pltpu.make_async_copy(volume_ref.at[z], volume_keep.at[z], volume_sem.at[z])

    def weights_copy(a):
        return pltpu.make_async_copy(
            weights_ref.at[ids_ref[a]], weights_keep.at[a], weights_sem.at[a]
        )

    for z in range(min(AHEAD, depth)):
        volume_copy(z).start()
    for a in range(min(max(AHEAD - depth, 0), projections)):
        weights_copy(a).start()

    rows = jnp.concatenate([rays_ref[pl.ds(ids_ref[a], 1), :] for a in range(projections)], axis=0)
    high, low = split_bf16(rows)
    stacked = [high, low]
    if lanes > 2 * projections:
        stacked.append(jnp.zeros((lanes - 2 * projections, width), F32))
    table_ref[...] = jnp.concatenate(stacked, axis=0).T.astype(BF16)
    spread = [jnp.broadcast_to(rows[a : a + 1], (depth, width)) for a in range(projections)]
    high, low = split_bf16(jnp.concatenate(spread, axis=0))
    for place, block in enumerate((high, high, low, low)):
        rays_keep[place * both : (place + 1) * both, :] = block.astype(BF16)

    @pl.loop(0, depth)
    def _(z):
        volume_copy(z).wait()

        @pl.when(z + AHEAD < depth)
        def _():
            volume_copy(z + AHEAD).start()

        @pl.when(jnp.logical_and(z + AHEAD >= depth, z + AHEAD - depth < projections))
        def _():
            weights_copy(z + AHEAD - depth).start()

        piece = min(512, width)
        first = second = None
        for k in range(0, width, piece):
            block = volume_keep[z, :, k : k + piece]
            high = block.astype(BF16)
            low = (block - high.astype(F32)).astype(BF16)
            of_high = dot(high, table_ref[k : k + piece, :])
            of_low = dot(low, table_ref[k : k + piece, :])
            first = of_high if first is None else first + of_high
            second = of_low if second is None else second + of_low
        first = first.T
        second = second.T
        sums_ref[z] = first[:projections] + (
            first[projections : 2 * projections] + second[:projections]
        )

    @pl.loop(0, projections)
    def _(a):
        weights_copy(a).wait()

        @pl.when(a + AHEAD < projections)
        def _():
            weights_copy(a + AHEAD).start()

        rows = sums_ref[:, pl.ds(a, 1), :].reshape(depth, sums_ref.shape[2])
        result = dot(rows.astype(BF16), weights_keep[a])
        for part in range(parts):
            out_ref[part, a] = result[:, part * share : (part + 1) * share]


def forward_parts(angle_ids, volume, proj_weights, ray_weights, parts):
    depth, rows, width = volume.shape
    projections = angle_ids.shape[0]
    lanes = -(-2 * projections // LANES) * LANES
    share = width // parts
    full = pl.BlockSpec(memory_space=VMEM)
    shape = jax.ShapeDtypeStruct
    return pl.pallas_call(
        forward_kernel,
        in_specs=[
            pl.BlockSpec(memory_space=pltpu.SMEM),
            full,
            pl.BlockSpec(memory_space=pl.ANY),
            pl.BlockSpec(memory_space=pl.ANY),
        ],
        out_specs=[full] * 4,
        out_shape=[
            shape((parts, projections, depth, share), F32),
            shape((depth, rows, width), F32),
            shape((projections, rows, width), BF16),
            shape((4 * projections * depth, width), BF16),
        ],
        scratch_shapes=[
            VMEM((width, lanes), BF16),
            VMEM((depth, projections, rows), F32),
            pltpu.SemaphoreType.DMA((depth,)),
            pltpu.SemaphoreType.DMA((projections,)),
        ],
        compiler_params=pltpu.CompilerParams(vmem_limit_bytes=14 * MIB),
        cost_estimate=pl.CostEstimate(
            flops=4 * depth * rows * width * lanes,
            bytes_accessed=depth * rows * width * 4 + projections * rows * width * 2,
            transcendentals=0,
        ),
        name="forward",
    )(angle_ids, ray_weights, volume, proj_weights)


def placed(values, down, across):
    rows, cols = values.shape
    tall = jnp.concatenate([values, jnp.zeros((SUBLANES, cols), F32)], axis=0)
    tall = pltpu.roll(tall, down, axis=0)
    wide = jnp.concatenate([tall, jnp.zeros((rows + SUBLANES, LANES), F32)], axis=1)
    return pltpu.roll(wide, across, axis=1)


def patch_kernel(
    rows_ref,
    cols_ref,
    count_ref,
    own_ref,
    left_ref,
    right_ref,
    probe_ref,
    amp_ref,
    dft_a_ref,
    dft_b_ref,
    dual_ref,
    new_ref,
    edge_left_ref,
    edge_right_ref,
    slab_ref,
    parts_ref,
    ext_ref,
    sum_ref,
    patch_ref,
    wave_ref,
    half_ref,
    far_ref,
    grad_ref,
    energy_ref,
):
    side = probe_ref.shape[1]
    margin = left_ref.shape[2]
    tile_cols = own_ref.shape[2]
    window = side + LANES
    chunk = 32
    tall = chunk + SUBLANES
    height = own_ref.shape[1]

    for c in range(2):
        ext_ref[c, :height, :margin] = left_ref[c]
        ext_ref[c, :height, margin : margin + tile_cols] = own_ref[c]
        ext_ref[c, :height, margin + tile_cols : 2 * margin + tile_cols] = right_ref[c]
    sum_ref[...] = jnp.zeros(sum_ref.shape, F32)
    grad_ref[...] = jnp.zeros(grad_ref.shape, F32)
    energy_ref[...] = jnp.zeros(energy_ref.shape, F32)

    def slot_step(slot, carry):
        row = rows_ref[slot]
        col = cols_ref[slot]
        lane = lax.rem(col, LANES)
        base = pl.multiple_of(col - lane, LANES)
        back_shift = lax.rem(window - lane, window)
        notch = lax.rem(row, SUBLANES)
        top = pl.multiple_of(row - notch, SUBLANES)
        up_shift = lax.rem(tall - notch, tall)
        for r in range(0, side, chunk):
            cells = pl.ds(top + r, tall)
            here = slice(r, r + chunk)
            below = slice(side + r, side + r + chunk)
            x_re = pltpu.roll(ext_ref[0, cells, pl.ds(base, window)], back_shift, axis=1)[:, :side]
            x_im = pltpu.roll(ext_ref[1, cells, pl.ds(base, window)], back_shift, axis=1)[:, :side]
            x_re = pltpu.roll(x_re, up_shift, axis=0)[:chunk]
            x_im = pltpu.roll(x_im, up_shift, axis=0)[:chunk]
            p_re = probe_ref[0, here, :]
            p_im = probe_ref[1, here, :]
            patch_ref[here, :] = x_re
            patch_ref[below, :] = x_im
            wave_ref[here, :] = (p_re * x_re - p_im * x_im).astype(BF16)
            wave_ref[below, :] = (p_re * x_im + p_im * x_re).astype(BF16)
            power = x_re * x_re + x_im * x_im
            energy_ref[...] += jnp.sum(power.reshape(chunk // 8, 8, side), axis=0)
        half_ref[:, :side] = dot(dft_a_ref[:side, :], wave_ref[...]).astype(BF16)
        half_ref[:, side:] = dot(dft_a_ref[side:, :], wave_ref[...]).astype(BF16)
        far_ref[...] = dot(half_ref[...], dft_b_ref[...])
        for r in range(0, side, chunk):
            here = slice(r, r + chunk)
            below = slice(side + r, side + r + chunk)
            f_re = far_ref[here, :side]
            f_im = far_ref[here, side:]
            inverse = lax.rsqrt(f_re * f_re + f_im * f_im + 0.25)
            factor = amp_ref[slot, here, :].astype(F32) * inverse - 1.0
            wave_ref[here, :] = (f_re * factor).astype(BF16)
            wave_ref[below, :] = (f_im * factor).astype(BF16)
        half_ref[:, :side] = dot(dft_b_ref[:side, :], wave_ref[...]).astype(BF16)
        half_ref[:, side:] = dot(dft_b_ref[side:, :], wave_ref[...]).astype(BF16)
        far_ref[...] = dot(half_ref[...], dft_a_ref[...])
        for r in range(0, side, chunk):
            cells = pl.ds(top + r, tall)
            here = slice(r, r + chunk)
            below = slice(side + r, side + r + chunk)
            b_re = far_ref[here, :side]
            b_im = far_ref[here, side:]
            p_re = probe_ref[0, here, :]
            p_im = probe_ref[1, here, :]
            x_re = patch_ref[here, :]
            x_im = patch_ref[below, :]
            o_re = p_re * b_re + p_im * b_im
            o_im = p_re * b_im - p_im * b_re
            sum_ref[0, cells, pl.ds(base, window)] += placed(o_re, notch, lane)
            sum_ref[1, cells, pl.ds(base, window)] += placed(o_im, notch, lane)
            grad_ref[here, :] += x_re * b_re + x_im * b_im
            grad_ref[below, :] += x_re * b_im - x_im * b_re
        return carry

    lax.fori_loop(0, count_ref[0], slot_step, 0)

    parts, part_rows, _ = parts_ref.shape
    part_rows -= ENERGY_ROWS
    for part in range(parts):
        parts_ref[part, :part_rows, :] = grad_ref[part * part_rows : (part + 1) * part_rows, :]
        parts_ref[part, part_rows:, :] = energy_ref[...]
    p_re = probe_ref[0]
    p_im = probe_ref[1]
    peak = jnp.max(p_re * p_re + p_im * p_im)
    scale = 1.0 / (jnp.full((1, LANES), peak, F32) + 1e-05)
    wide = jnp.tile(scale, (1, tile_cols // LANES))
    for c in range(2):
        new_ref[c] = own_ref[c] + sum_ref[c, :height, margin : margin + tile_cols] * wide
        edge_left_ref[c] = sum_ref[c, :height, :margin] * scale
        edge_right_ref[c] = sum_ref[c, :height, margin + tile_cols : 2 * margin + tile_cols] * scale
    shares, layers, depth, share = slab_ref.shape
    edge = min(share - tile_cols // shares, margin)
    share -= edge
    holders = margin // edge
    first = (height - layers * depth) // 2
    for layer in range(layers):
        rows = slice(layer * depth, (layer + 1) * depth)
        cells = slice(first + layer * depth, first + (layer + 1) * depth)
        for p in range(shares):
            cols = slice(p * share, (p + 1) * share)
            slab_ref[p, layer, :, :share] = new_ref[1, cells, cols] + dual_ref[rows, cols]
            begin = (p - shares + holders) * edge
            if p < holders:
                outgoing = edge_left_ref[1, cells, p * edge : (p + 1) * edge]
            elif p >= shares - holders:
                outgoing = edge_right_ref[1, cells, begin : begin + edge]
            else:
                outgoing = jnp.zeros((depth, edge), F32)
            slab_ref[p, layer, :, share:] = outgoing


def patch_updates(
    rows, cols, count, own, left, right, probe, amplitudes, dual, parts, shares, layers
):
    side = probe.shape[1]
    _, height, tile_cols = own.shape
    margin = left.shape[2]
    slots = amplitudes.shape[0]
    slab_rows = dual.shape[0]
    share = tile_cols // shares
    edge = min(share, margin)
    dft_a, dft_b = dft_blocks(side)
    full = pl.BlockSpec(memory_space=VMEM)
    scalars = pl.BlockSpec(memory_space=pltpu.SMEM)
    extent = tile_cols + 2 * margin + LANES
    shape = jax.ShapeDtypeStruct
    return pl.pallas_call(
        patch_kernel,
        in_specs=[scalars] * 3 + [full] * 8,
        out_specs=[full] * 5,
        out_shape=[
            shape((2, height, tile_cols), F32),
            shape((2, height, margin), F32),
            shape((2, height, margin), F32),
            shape((shares, layers, slab_rows // layers, share + edge), F32),
            shape((parts, 2 * side // parts + ENERGY_ROWS, side), F32),
        ],
        scratch_shapes=[
            VMEM((2, height + SUBLANES, extent), F32),
            VMEM((2, height + SUBLANES, extent), F32),
            VMEM((2 * side, side), F32),
            VMEM((2 * side, side), BF16),
            VMEM((side, 2 * side), BF16),
            VMEM((side, 2 * side), F32),
            VMEM((2 * side, side), F32),
            VMEM((ENERGY_ROWS, side), F32),
        ],
        compiler_params=pltpu.CompilerParams(vmem_limit_bytes=16 * MIB),
        cost_estimate=pl.CostEstimate(
            flops=slots * 32 * side**3,
            bytes_accessed=8 * height * tile_cols * 4,
            transcendentals=slots * side * side,
        ),
        name="patches",
    )(
        rows,
        cols,
        count,
        own,
        left,
        right,
        probe,
        amplitudes,
        jnp.asarray(dft_a),
        jnp.asarray(dft_b),
        dual,
    )


def backward_kernel(residual_ref, weights_ref, out_ref, turned_ref):
    parts, projections, depth, share = residual_ref.shape
    both = projections * depth
    for part in range(parts):
        block = residual_ref[part].astype(F32).reshape(both, share)
        turned_ref[part * share : (part + 1) * share, :] = block.T
    out_ref[...] = jnp.zeros(out_ref.shape, F32)

    @pl.loop(0, projections)
    def _(a):
        lane = lax.broadcasted_iota(jnp.int32, turned_ref.shape, 1)
        begin = a * depth
        kept = jnp.logical_and(lane >= begin, lane < begin + depth)
        chosen = jnp.where(kept, turned_ref[...], 0.0).astype(BF16)
        out_ref[...] += dot(weights_ref[a], chosen)


def backward_sums(residual, weights):
    projections, rows, width = weights.shape
    depth = residual.shape[2]
    full = pl.BlockSpec(memory_space=VMEM)
    return pl.pallas_call(
        backward_kernel,
        in_specs=[full] * 2,
        out_specs=full,
        out_shape=jax.ShapeDtypeStruct((rows, projections * depth), F32),
        scratch_shapes=[VMEM((width, projections * depth), F32)],
        compiler_params=pltpu.CompilerParams(vmem_limit_bytes=14 * MIB),
        cost_estimate=pl.CostEstimate(
            flops=2 * rows * width * projections * projections * depth,
            bytes_accessed=projections * rows * width * 2,
            transcendentals=0,
        ),
        name="backward",
    )(residual, weights)


def update_kernel(
    sums_ref,
    rays_ref,
    volume_ref,
    object_ref,
    from_left_ref,
    from_right_ref,
    out_ref,
    new_object_ref,
    stack_ref,
    done_ref,
    cells_ref,
    out_sem,
    object_sem,
):
    depth = volume_ref.shape[0]
    slots = done_ref.shape[0]
    margin = from_left_ref.shape[2]
    tile_cols = object_ref.shape[2]
    high, low = split_bf16(sums_ref[...])
    stack_ref[...] = jnp.concatenate([high, low, high, low], axis=1)

    def out_copy(z):
        slot = lax.rem(z, slots)
        return pltpu.make_async_copy(done_ref.at[slot], out_ref.at[z], out_sem.at[slot])

    @pl.loop(0, depth)
    def _(z):
        @pl.when(z >= slots)
        def _():
            out_copy(z - slots).wait()

        lane = lax.broadcasted_iota(jnp.int32, stack_ref.shape, 1)
        kept = lax.rem(lane, depth) == z
        chosen = jnp.where(kept, stack_ref[...], 0.0).astype(BF16)
        done_ref[lax.rem(z, slots)] = volume_ref[z] - tomo_step * dot(chosen, rays_ref[...])
        out_copy(z).start()

    cells_ref[...] = object_ref[...]
    cells_ref[:, :, :margin] += from_left_ref[...]
    cells_ref[:, :, tile_cols - margin :] += from_right_ref[...]
    object_copy = pltpu.make_async_copy(cells_ref, new_object_ref, object_sem)
    object_copy.start()
    for z in range(max(depth - slots, 0), depth):
        out_copy(z).wait()
    object_copy.wait()


def volume_update(sums, rays, volume, partial_object, from_left, from_right):
    depth, rows, width = volume.shape
    slots = min(4, depth)
    full = pl.BlockSpec(memory_space=VMEM)
    anywhere = pl.BlockSpec(memory_space=pl.ANY)
    return pl.pallas_call(
        update_kernel,
        in_specs=[full] * 6,
        out_specs=[anywhere] * 2,
        out_shape=[
            jax.ShapeDtypeStruct(volume.shape, F32),
            jax.ShapeDtypeStruct(partial_object.shape, F32),
        ],
        scratch_shapes=[
            VMEM((rows, 4 * sums.shape[1]), F32),
            VMEM((slots, rows, width), F32),
            VMEM(partial_object.shape, F32),
            pltpu.SemaphoreType.DMA((slots,)),
            pltpu.SemaphoreType.DMA,
        ],
        compiler_params=pltpu.CompilerParams(vmem_limit_bytes=18 * MIB),
        cost_estimate=pl.CostEstimate(
            flops=8 * rows * width * sums.shape[1] * depth,
            bytes_accessed=depth * rows * width * 4,
            transcendentals=0,
        ),
        name="update",
    )(sums, rays, volume, partial_object, from_left, from_right)


def spread_to(value, axes, count):
    copies = jnp.broadcast_to(value[None], (count, *value.shape))
    return lax.all_to_all(copies, axes, 0, 0, tiled=True)


def on_device(
    object_field,
    probe_field,
    amplitudes,
    pos_rows,
    pos_cols,
    counts,
    admm_dual,
    volume,
    proj_weights,
    ray_weights,
    angle_ids,
):
    margin = probe_field.shape[1] // 2
    own = object_field[0]
    tile_cols = own.shape[2]
    flat_axes = ("tile", "proj")
    plane = lax.axis_size("tile") * lax.axis_size("proj")
    proj_count = lax.axis_size("proj")
    layers = lax.axis_size("cuts")
    from_left = shifted(own[:, :, tile_cols - margin :], "tile", 1)
    from_right = shifted(own[:, :, :margin], "tile", -1)
    forward, volume_kept, weights_kept, rays_kept = forward_parts(
        angle_ids, volume, proj_weights, ray_weights, plane
    )
    arrived = lax.all_to_all(forward, flat_axes, 0, 0, tiled=True)
    partial_object, edge_left, edge_right, slab, grad_parts = patch_updates(
        pos_rows[0, 0],
        pos_cols[0, 0],
        counts[0],
        own,
        from_left,
        from_right,
        probe_field,
        amplitudes[0, 0],
        admm_dual[0],
        plane,
        proj_count,
        layers,
    )

    share = tile_cols // proj_count
    edge = slab.shape[3] - share
    holders = margin // edge
    pieces = slab.reshape(proj_count * layers, *slab.shape[2:])
    pieces = lax.all_to_all(pieces, ("proj", "cuts"), 0, 0, tiled=True)
    pairs = []
    for tile in range(lax.axis_size("tile") - 1):
        for k in range(holders):
            lower = tile * proj_count + proj_count - holders + k
            upper = (tile + 1) * proj_count + k
            pairs += [(lower, upper), (upper, lower)]
    grads_in = lax.ppermute(pieces[:, :, share:], flat_axes, pairs)
    at_start = jnp.pad(grads_in, ((0, 0), (0, 0), (0, share - edge)))
    at_end = jnp.pad(grads_in, ((0, 0), (0, 0), (share - edge, 0)))
    target = pieces[:, :, :share] + jnp.where(
        lax.axis_index("proj") < holders, at_start, at_end
    )
    residual = (jnp.sum(arrived, axis=0) - target).astype(BF16)
    residual = spread_to(residual, flat_axes, plane)
    back_sums = backward_sums(residual, weights_kept)

    edge_from_right = shifted(edge_left, "tile", -1)
    edge_from_left = shifted(edge_right, "tile", 1)

    side = probe_field.shape[1]
    part_rows = grad_parts.shape[1] - ENERGY_ROWS
    summed = jnp.sum(lax.all_to_all(grad_parts, flat_axes, 0, 0, tiled=True), axis=0)
    summed = jnp.sum(spread_to(summed, "cuts", layers), axis=0)
    energy = jnp.sum(summed[part_rows:]) / (side * side)
    begin = lax.axis_index(flat_axes) * part_rows
    own_rows = lax.dynamic_slice(
        probe_field.reshape(2 * side, side),
        (begin, jnp.zeros((), begin.dtype)),
        (part_rows, side),
    )
    new_rows = own_rows + summed[:part_rows] / (energy + 1e-05)
    new_probe = spread_to(new_rows, flat_axes, plane).reshape(2, side, side)

    new_volume, new_object = volume_update(
        back_sums, rays_kept, volume_kept, partial_object, edge_from_left, edge_from_right
    )
    return (new_object[None], new_probe, new_volume)


def solution(mesh):
    in_specs = (
        P(("proj", "cuts"), None, None, "tile"),
        P(),
        P(("proj", "cuts"), "tile", None, None, None),
        P(("proj", "cuts"), "tile", None),
        P(("proj", "cuts"), "tile", None),
        P(("proj", "cuts"), "tile"),
        P(("proj", "cuts"), None, "tile"),
        P("cuts", ("tile", "proj"), None),
        P(None, ("tile", "proj"), None),
        P(),
        P(),
    )
    out_specs = (P(("proj", "cuts"), None, None, "tile"), P(), P("cuts", ("tile", "proj"), None))
    return jax.shard_map(
        on_device, mesh=mesh, in_specs=in_specs, out_specs=out_specs, check_vma=False
    )
```

time: 154 us -> 144 us (0.935)
  local copies, waits for them, and re-layouts: 13.5 us -> 36.2 us
  blocking collectives: 36.4 us -> 14.5 us
  Pallas kernels: 47.7 us -> 30.3 us
  waiting for transfers between devices: 7.05 us -> 16.6 us
  other arithmetic: 7.25 us -> 4.65 us
  starting transfers between devices: 39.7 us -> 38.1 us
    all_gather x3 -> x0, blocking collectives: 36.4 us -> none  [the longest x1 14.1 us: on_device(): residual = lax.all_gather(residual[None], flat_axes, axis=0, tiled=True)]
    unnamed x32 -> x43, local copies, waits for them, and re-layouts: 10.8 us -> 32.7 us
    pallas_call x2 -> x3, Pallas kernels: 41.1 us -> 23.1 us  [the longest x1 11.6 us: forward_parts(): pl.pallas_call(forward_kernel, in_specs=[pl.BlockSpec(memory_space=pltpu....]
    all_to_all x0 -> x1, blocking collectives: none -> 14.5 us  [on_device(): lax.all_to_all(grad_parts, flat_axes, 0, 0, tiled=True)]
    ppermute x6 -> x4, starting transfers between devices: 23.3 us -> 13 us  [shifted(): lax.ppermute(value, axis, [(source, source + steps) for source in range(l...]
    all_to_all x3 -> x4, waiting for transfers between devices: 7.03 us -> 16.6 us  [the longest x3 11.3 us: spread_to(): return lax.all_to_all(copies, axes, 0, 0, tiled=True)]
    all_to_all x3 -> x4, starting transfers between devices: 12.2 us -> 20.3 us  [the longest x3 11 us: spread_to(): return lax.all_to_all(copies, axes, 0, 0, tiled=True)]
    scatter-add x2 -> x0, other arithmetic: 2.91 us -> none  [the longest x1 1.82 us: on_device(): new_object = new_object.at[:, :, tile_cols - margin:].add(edge_from_right)]
  transfers between devices with their start and end apart: 10 -> 10, of which waited for: 2 -> 3; matrix products, arithmetic and copies ran while one was open for 6% -> 4% of each run, Pallas kernels for 31% -> 21%
where the time goes in v1:
time: 144 us; the launch traced here: 143 us
  starting transfers between devices  38.1 us (26%)
  local copies, waits for them, and re-layouts  36.2 us (25%)
  Pallas kernels  30.3 us (21%)
  waiting for transfers between devices  16.6 us (12%)
  blocking collectives  14.5 us (10%)
  other arithmetic  4.65 us (3%)
  between operations  2.17 us (2%)
    unnamed x43, local copies, waits for them, and re-layouts  32.7 us
    all_to_all x1, blocking collectives, on_device(): lax.all_to_all(grad_parts, flat_axes, 0, 0, tiled=True)  14.5 us
    ppermute x4, starting transfers between devices, shifted(): lax.ppermute(value, axis, [(source, source + steps) for source in range(l...  13 us
    pallas_call x1, Pallas kernels, forward_parts(): pl.pallas_call(forward_kernel, in_specs=[pl.BlockSpec(memory_space=pltpu....  11.6 us
    all_to_all x3, waiting for transfers between devices, spread_to(): return lax.all_to_all(copies, axes, 0, 0, tiled=True)  11.3 us
    all_to_all x3, starting transfers between devices, spread_to(): return lax.all_to_all(copies, axes, 0, 0, tiled=True)  11 us
    all_to_all x1, starting transfers between devices, on_device(): pieces = lax.all_to_all(pieces, ('proj', 'cuts'), 0, 0, tiled=True)  9.26 us
    pallas_call x1, Pallas kernels, volume_update(): pl.pallas_call(update_kernel, in_specs=[full] * 6, out_specs=[anywhere] *...  7.88 us
  transfers between devices with their start and end apart: 10, of which 3 were waited for; matrix products, arithmetic and copies ran while one was open for 4% of the time, Pallas kernels for 21%

profile of v1, /device:TPU:0, one launch (start us, length us, event | category | flops | bytes accessed | tf_op | source)
XLA Modules:
  0.0 142.6 jit_solution(9882724095253176242)
XLA Ops:
  0.6 1.2 fusion.3
  1.8 1.3 collective-permute-start.1
  3.1 5.5 %collective-permute-start = (f32[2,384,128]{2,1,0:T(8,128)S(1)}, f32[2,384,128]{2,1,0:T(8,128)S(1)}, u32[]{:S(2)}, u32[]{:S(2)}) collective-permute-start(f32[2,384,128]{2,1,0:T(8,128)S(1)} %get-tuple-element.26), channel_id=1, source_target_pairs={{0,8},{8,16},{16,24},{1,9},{9,17},{17,25},{2,10},{10,18},{18,26},{... | collective-permute-start | bytes 1179656 | tf_op jit(solution)/shard_map/ppermute | solution.py:26
  8.6 0.0 copy-start.5
  8.6 0.9 copy-done.5
  9.5 0.7 copy-done.7
  10.2 11.6 %forward.1 = (f32[8,8,8,256]{3,2,1,0:T(8,128)}, f32[8,256,2048]{2,1,0:T(8,128)S(1)}, bf16[8,256,2048]{2,1,0:T(8,128)(2,1)S(1)}, bf16[256,2048]{1,0:T(8,128)(2,1)S(1)}) custom-call(s32[8]{0:T(128)S(1)} %copy-done.7, f32[16,2048]{1,0:T(8,128)S(1)} %copy-done.5, f32[8,256,2048]{2,1,0:T(8,128)} %volume_ref.1, bf16[16,256,2048]{2,1,0:T(8,128)(2,1)} %weights_ref.1), custom_call_target="tpu_custom_call" | custom-call | flops 2147483648 | bytes 25165824 | tf_op jit(solution)/shard_map/forward/pallas_call | solution.py:143
  21.8 0.0 copy-start
  21.8 6.2 %copy-done = f32[8,256,2048]{2,1,0:T(8,128)} copy-done((f32[8,256,2048]{2,1,0:T(8,128)}, f32[8,256,2048]{2,1,0:T(8,128)S(1)}, u32[]{:S(2)}) %copy-start) | copy-done | bytes 16777240
  28.0 3.3 %copy-done.2 = bf16[8,256,2048]{2,1,0:T(8,128)(2,1)} copy-done((bf16[8,256,2048]{2,1,0:T(8,128)(2,1)}, bf16[8,256,2048]{2,1,0:T(8,128)(2,1)S(1)}, u32[]{:S(2)}) %copy-start.2) | copy-done | bytes 8388632
  31.2 4.2 %all-to-all-start = ((f32[8,8,8,256]{3,2,1,0:T(8,128)}), f32[8,8,8,256]{3,2,1,0:T(8,128)}, u32[]{:S(2)}, u32[]{:S(2)}) async-start(f32[8,8,8,256]{3,2,1,0:T(8,128)} %get-tuple-element.14), calls=%async_computation | async-start | bytes 1048576 | tf_op jit(solution)/shard_map/all_to_all | solution.py:522
  36.1 0.7 copy-done.11
  36.8 0.7 copy-done.13
  37.6 1.4 copy-done.4
  39.0 1.0 copy-done.6
  40.0 1.1 copy-done.8
  41.2 1.0 copy-done.12
  42.2 1.0 copy-done.14
  43.2 1.0 copy-done.18
  44.2 1.0 copy-done.19
  45.2 7.2 %patches.1 = (f32[2,384,512]{2,1,0:T(8,128)S(1)}, f32[2,384,128]{2,1,0:T(8,128)S(1)}, f32[2,384,128]{2,1,0:T(8,128)S(1)}, f32[2,4,8,384]{3,2,1,0:T(8,128)}, f32[8,72,256]{2,1,0:T(8,128)S(1)}) custom-call(s32[6]{0:T(128)S(1)} %bitcast.16, s32[6]{0:T(128)S(1)} %bitcast.17, s32[1]{0:T(128)} %bitcast.10.count_ref, f32[2,384,512]{2,1,0:T(8,128)S(1)} %bitcast.12, ...), custom_call_target="tpu_custom_call" | custom-call | flops 3221225472 | bytes 6291456 | tf_op jit(solution)/shard_map/patches/pallas_call | solution.py:334
  52.4 0.8 copy-done.9
  53.2 0.7 copy-done.10
  53.9 14.5 %all_to_all.30 = f32[8,72,256]{2,1,0:T(8,128)} all-to-all(f32[8,72,256]{2,1,0:T(8,128)S(1)} %get-tuple-element.23), channel_id=1, replica_groups=mesh['tile'=4,'proj'=2,'cuts'=4] {'tile','proj'}, dimensions={0} | all-to-all | bytes 1179648 | tf_op jit(solution)/shard_map/all_to_all | solution.py:564
  68.5 9.3 %all-to-all-start.1 = ((f32[8,8,384]{2,1,0:T(8,128)}), f32[8,8,384]{2,1,0:T(8,128)S(1)}, u32[]{:S(2)}, u32[]{:S(2)}) async-start(f32[8,8,384]{2,1,0:T(8,128)} %bitcast.6), calls=%async_computation.1 | async-start | bytes 196608 | tf_op jit(solution)/shard_map/all_to_all | solution.py:542
  77.7 1.1 reduce_sum.37
  78.8 5.4 %all-to-all-done.1 = f32[8,8,384]{2,1,0:T(8,128)S(1)} async-done(((f32[8,8,384]{2,1,0:T(8,128)}), f32[8,8,384]{2,1,0:T(8,128)S(1)}, u32[]{:S(2)}, u32[]{:S(2)}) %all-to-all-start.1) | async-done | bytes 98336 | tf_op jit(solution)/shard_map/all_to_all | solution.py:542
  84.2 0.7 broadcast_in_dim.10
  84.9 3.5 %all-to-all-start.4 = ((f32[4,72,256]{2,1,0:T(8,128)}), f32[4,72,256]{2,1,0:T(8,128)S(1)}, u32[]{:S(2)}, u32[]{:S(2)}) async-start(f32[4,72,256]{2,1,0:T(8,128)} %broadcast_in_dim.10), calls=%async_computation.4 | async-start | bytes 589824 | tf_op jit(solution)/shard_map/all_to_all | solution.py:494
  88.4 0.7 collective-permute-start.2
  89.1 4.9 %collective-permute-start.3 = (f32[2,384,128]{2,1,0:T(8,128)}, f32[2,384,128]{2,1,0:T(8,128)S(1)}, u32[]{:S(2)}, u32[]{:S(2)}) collective-permute-start(f32[2,384,128]{2,1,0:T(8,128)} %copy-done.10), channel_id=1, source_target_pairs={{0,8},{8,16},{16,24},{1,9},{9,17},{17,25},{2,10},{10,18},{18,26},{... | collective-permute-start | bytes 1179656 | tf_op jit(solution)/shard_map/ppermute | solution.py:26
  94.0 1.3 collective-permute-start.4
  95.3 1.1 reduce_sum.36
  96.4 2.1 %all-to-all-done.4 = f32[4,72,256]{2,1,0:T(8,128)S(1)} async-done(((f32[4,72,256]{2,1,0:T(8,128)}), f32[4,72,256]{2,1,0:T(8,128)S(1)}, u32[]{:S(2)}, u32[]{:S(2)}) %all-to-all-start.4) | async-done | bytes 294944 | tf_op jit(solution)/shard_map/all_to_all | solution.py:494
  98.5 0.8 broadcast_in_dim.8
  99.3 0.0 copy-done.20
  99.3 3.4 %all-to-all-start.2 = ((bf16[8,8,8,256]{3,2,1,0:T(8,128)(2,1)}), bf16[8,8,8,256]{3,2,1,0:T(8,128)(2,1)S(1)}, u32[]{:S(2)}, u32[]{:S(2)}) async-start(bf16[8,8,8,256]{3,2,1,0:T(8,128)(2,1)} %broadcast_in_dim.8), calls=%async_computation.2 | async-start | bytes 524288 | tf_op jit(solution)/shard_map/all_to_all | solution.py:494
  102.7 1.0 reduce_sum.38
  103.7 0.6 slice_reduce_fusion
  105.0 0.9 fusion
  105.8 9.2 %all-to-all-done.2.residual_ref = bf16[8,8,8,256]{3,2,1,0:T(8,128)(2,1)S(1)} async-done(((bf16[8,8,8,256]{3,2,1,0:T(8,128)(2,1)}), bf16[8,8,8,256]{3,2,1,0:T(8,128)(2,1)S(1)}, u32[]{:S(2)}, u32[]{:S(2)}) %all-to-all-start.2) | async-done | bytes 262176 | tf_op jit(solution)/shard_map/all_to_all | solution.py:494
  115.0 0.8 broadcast_in_dim.11
  115.9 4.2 %all-to-all-start.5 = ((f32[8,64,256]{2,1,0:T(8,128)}), f32[8,64,256]{2,1,0:T(8,128)}, u32[]{:S(2)}, u32[]{:S(2)}) async-start(f32[8,64,256]{2,1,0:T(8,128)} %broadcast_in_dim.11), calls=%async_computation.5 | async-start | bytes 1048576 | tf_op jit(solution)/shard_map/all_to_all | solution.py:494
  120.0 3.4 %copy-done.3 = bf16[8,256,2048]{2,1,0:T(8,128)(2,1)S(1)} copy-done((bf16[8,256,2048]{2,1,0:T(8,128)(2,1)S(1)}, bf16[8,256,2048]{2,1,0:T(8,128)(2,1)}, u32[]{:S(2)}) %copy-start.3) | copy-done | bytes 8388632
  123.4 3.6 %backward.1.sums_ref = f32[256,64]{1,0:T(8,128)S(1)} custom-call(bf16[8,8,8,256]{3,2,1,0:T(8,128)(2,1)S(1)} %all-to-all-done.2.residual_ref, bf16[8,256,2048]{2,1,0:T(8,128)(2,1)S(1)} %copy-done.3), custom_call_target="tpu_custom_call" | custom-call | flops 536870912 | bytes 8388608 | tf_op jit(solution)/shard_map/backward/pallas_call | solution.py:398
  127.1 5.8 %copy-done.1 = f32[8,256,2048]{2,1,0:T(8,128)S(1)} copy-done((f32[8,256,2048]{2,1,0:T(8,128)S(1)}, f32[8,256,2048]{2,1,0:T(8,128)}, u32[]{:S(2)}) %copy-start.1) | copy-done | bytes 16777240
  132.8 7.9 %update.1 = (f32[8,256,2048]{2,1,0:T(8,128)}, f32[2,384,512]{2,1,0:T(8,128)}) custom-call(f32[256,64]{1,0:T(8,128)S(1)} %backward.1.sums_ref, bf16[256,2048]{1,0:T(8,128)(2,1)S(1)} %get-tuple-element.17.rays_ref, f32[8,256,2048]{2,1,0:T(8,128)S(1)} %copy-done.1, f32[2,384,512]{2,1,0:T(8,128)S(1)} %get-tuple-element.19.object_ref, ...), custom_call_target="tpu_custom_call" | custom-call | flops 2147483648 | bytes 16777216 | tf_op jit(solution)/shard_map/update/pallas_call | solution.py:467
  140.7 1.9 %copy.18 = f32[2,256,256]{2,1,0:T(8,128)} copy(f32[2,256,256]{2,1,0:T(8,128)} %bitcast.9) | data formatting | bytes 1048576
  (31 shorter events, 0.1 us)
Async XLA Ops:
  1.8 34.3 %collective-permute-start.1 = (f32[2,384,128]{2,1,0:T(8,128)S(1)}, f32[2,384,128]{2,1,0:T(8,128)S(1)}, u32[]{:S(2)}, u32[]{:S(2)}) collective-permute-start(f32[2,384,128]{2,1,0:T(8,128)S(1)} %get-tuple-element.25), channel_id=1, source_target_pairs={{8,0},{16,8},{24,16},{9,1},{17,9},{25,17},{10,2},{18,10},{26,18},{... | collective-permute-start | bytes 1179656 | tf_op jit(solution)/shard_map/ppermute | solution.py:26
  3.1 33.7 %collective-permute-start = (f32[2,384,128]{2,1,0:T(8,128)S(1)}, f32[2,384,128]{2,1,0:T(8,128)S(1)}, u32[]{:S(2)}, u32[]{:S(2)}) collective-permute-start(f32[2,384,128]{2,1,0:T(8,128)S(1)} %get-tuple-element.26), channel_id=1, source_target_pairs={{0,8},{8,16},{16,24},{1,9},{9,17},{17,25},{2,10},{10,18},{18,26},{... | collective-permute-start | bytes 1179656 | tf_op jit(solution)/shard_map/ppermute | solution.py:26
  8.6 0.9 copy-start.5
  9.5 0.7 copy-start.7
  10.2 27.4 %copy-start.15 = (f32[1,32,512]{2,1,0:T(8,128)S(1)}, f32[1,32,512]{2,1,0:T(8,128)}, u32[]{:S(2)}) copy-start(f32[1,32,512]{2,1,0:T(8,128)} %param.19) | copy-start | bytes 196612
  10.2 27.4 %copy-start.16 = (s32[1,1,6]{2,1,0:T(1,128)S(1)}, s32[1,1,6]{2,1,0:T(1,128)}, u32[]{:S(2)}) copy-start(s32[1,1,6]{2,1,0:T(1,128)} %param.16) | copy-start | bytes 76
  10.2 27.4 %copy-start.17 = (s32[1,1,6]{2,1,0:T(1,128)S(1)}, s32[1,1,6]{2,1,0:T(1,128)}, u32[]{:S(2)}) copy-start(s32[1,1,6]{2,1,0:T(1,128)} %param.17) | copy-start | bytes 76
  21.8 6.2 %copy-start = (f32[8,256,2048]{2,1,0:T(8,128)}, f32[8,256,2048]{2,1,0:T(8,128)S(1)}, u32[]{:S(2)}) copy-start(f32[8,256,2048]{2,1,0:T(8,128)S(1)} %get-tuple-element.18.volume_ref) | copy-start | bytes 50331652
  27.9 3.3 %copy-start.2 = (bf16[8,256,2048]{2,1,0:T(8,128)(2,1)}, bf16[8,256,2048]{2,1,0:T(8,128)(2,1)S(1)}, u32[]{:S(2)}) copy-start(bf16[8,256,2048]{2,1,0:T(8,128)(2,1)S(1)} %get-tuple-element.16.weights_ref) | copy-start | bytes 25165828
  31.2 22.7 %all-to-all-start = ((f32[8,8,8,256]{3,2,1,0:T(8,128)}), f32[8,8,8,256]{3,2,1,0:T(8,128)}, u32[]{:S(2)}, u32[]{:S(2)}) async-start(f32[8,8,8,256]{3,2,1,0:T(8,128)} %get-tuple-element.14), calls=%async_computation | async-start | bytes 1048576 | tf_op jit(solution)/shard_map/all_to_all | solution.py:522
  36.1 0.8 copy-start.11
  36.8 0.7 copy-start.13
  37.6 1.4 copy-start.4
  39.0 1.0 copy-start.6
  40.0 1.1 copy-start.8
  41.2 1.0 copy-start.12
  42.2 1.0 copy-start.14
  43.2 1.0 copy-start.18
  44.2 1.0 copy-start.19
  52.4 0.8 copy-start.9
  53.2 0.7 copy-start.10
  68.5 15.7 %all-to-all-start.1 = ((f32[8,8,384]{2,1,0:T(8,128)}), f32[8,8,384]{2,1,0:T(8,128)S(1)}, u32[]{:S(2)}, u32[]{:S(2)}) async-start(f32[8,8,384]{2,1,0:T(8,128)} %bitcast.6), calls=%async_computation.1 | async-start | bytes 196608 | tf_op jit(solution)/shard_map/all_to_all | solution.py:542
  84.9 13.6 %all-to-all-start.4 = ((f32[4,72,256]{2,1,0:T(8,128)}), f32[4,72,256]{2,1,0:T(8,128)S(1)}, u32[]{:S(2)}, u32[]{:S(2)}) async-start(f32[4,72,256]{2,1,0:T(8,128)} %broadcast_in_dim.10), calls=%async_computation.4 | async-start | bytes 589824 | tf_op jit(solution)/shard_map/all_to_all | solution.py:494
  88.4 8.0 %collective-permute-start.2 = (f32[8,8,128]{2,1,0:T(8,128)S(1)}, f32[8,8,128]{2,1,0:T(8,128)S(1)}, u32[]{:S(2)}, u32[]{:S(2)}) collective-permute-start(f32[8,8,128]{2,1,0:T(8,128)S(1)} %slice.27), channel_id=1, source_target_pairs={{4,8},{8,4},{12,16},{16,12},{20,24},{24,20},{5,9},{9,5},{13,17},{1... | collective-permute-start | bytes 98312 | tf_op jit(solution)/shard_map/ppermute | solution.py:549
  89.1 38.0 %collective-permute-start.3 = (f32[2,384,128]{2,1,0:T(8,128)}, f32[2,384,128]{2,1,0:T(8,128)S(1)}, u32[]{:S(2)}, u32[]{:S(2)}) collective-permute-start(f32[2,384,128]{2,1,0:T(8,128)} %copy-done.10), channel_id=1, source_target_pairs={{0,8},{8,16},{16,24},{1,9},{9,17},{17,25},{2,10},{10,18},{18,26},{... | collective-permute-start | bytes 1179656 | tf_op jit(solution)/shard_map/ppermute | solution.py:26
  94.0 33.0 %collective-permute-start.4 = (f32[2,384,128]{2,1,0:T(8,128)}, f32[2,384,128]{2,1,0:T(8,128)}, u32[]{:S(2)}, u32[]{:S(2)}) collective-permute-start(f32[2,384,128]{2,1,0:T(8,128)} %copy-done.9), channel_id=1, source_target_pairs={{8,0},{16,8},{24,16},{9,1},{17,9},{25,17},{10,2},{18,10},{26,18},{... | collective-permute-start | bytes 1179656 | tf_op jit(solution)/shard_map/ppermute | solution.py:26
  98.5 0.8 copy-start.20
  99.3 15.7 %all-to-all-start.2 = ((bf16[8,8,8,256]{3,2,1,0:T(8,128)(2,1)}), bf16[8,8,8,256]{3,2,1,0:T(8,128)(2,1)S(1)}, u32[]{:S(2)}, u32[]{:S(2)}) async-start(bf16[8,8,8,256]{3,2,1,0:T(8,128)(2,1)} %broadcast_in_dim.8), calls=%async_computation.2 | async-start | bytes 524288 | tf_op jit(solution)/shard_map/all_to_all | solution.py:494
  115.9 24.9 %all-to-all-start.5 = ((f32[8,64,256]{2,1,0:T(8,128)}), f32[8,64,256]{2,1,0:T(8,128)}, u32[]{:S(2)}, u32[]{:S(2)}) async-start(f32[8,64,256]{2,1,0:T(8,128)} %broadcast_in_dim.11), calls=%async_computation.5 | async-start | bytes 1048576 | tf_op jit(solution)/shard_map/all_to_all | solution.py:494
  120.0 3.4 %copy-start.3 = (bf16[8,256,2048]{2,1,0:T(8,128)(2,1)S(1)}, bf16[8,256,2048]{2,1,0:T(8,128)(2,1)}, u32[]{:S(2)}) copy-start(bf16[8,256,2048]{2,1,0:T(8,128)(2,1)} %copy-done.2) | copy-start | bytes 25165828
  127.1 5.8 %copy-start.1 = (f32[8,256,2048]{2,1,0:T(8,128)S(1)}, f32[8,256,2048]{2,1,0:T(8,128)}, u32[]{:S(2)}) copy-start(f32[8,256,2048]{2,1,0:T(8,128)} %copy-done) | copy-start | bytes 50331652

commit v2 on v1

v2 whole, which is shorter than its diff:
```python
import functools
import math

import jax
import jax.numpy as jnp
import numpy as np
from jax import lax
from jax.experimental import pallas as pl
from jax.experimental.pallas import tpu as pltpu
from jax.sharding import PartitionSpec as P

MIB = 1024 * 1024
VMEM = pltpu.VMEM
F32 = jnp.float32
BF16 = jnp.bfloat16
LANES = 128
SUBLANES = 8
ENERGY_ROWS = 8
AHEAD = 6
ANYWHERE = pl.BlockSpec(memory_space=pl.ANY)
IN_HBM = pl.BlockSpec(memory_space=pltpu.HBM)
WHOLE = pl.BlockSpec(memory_space=pltpu.VMEM)
SCALARS = pl.BlockSpec(memory_space=pltpu.SMEM)
DMA = pltpu.SemaphoreType.DMA

tomo_step = 1.0


def shifted(value, axis, steps):
    count = lax.axis_size(axis)
    leading, last = (max(0, -steps), min(count, count - steps))
    return lax.ppermute(value, axis, [(source, source + steps) for source in range(leading, last)])


def dft_blocks(side):
    indices = np.arange(side)
    products = (indices[:, None] * indices[None, :]) % side
    phase = products.astype(np.float32) * np.float32(2.0 * math.pi / side)
    norm = np.float32(1.0 / math.sqrt(side))
    real = np.cos(phase).astype(np.float32) * norm
    imag = -np.sin(phase).astype(np.float32) * norm
    left = np.block([[real, -imag], [imag, real]])
    right = np.block([[real, imag], [-imag, real]])
    return left.astype(jnp.bfloat16), right.astype(jnp.bfloat16)


def dot(left, right):
    return jnp.dot(left, right, preferred_element_type=F32)


def split_bf16(values):
    high = values.astype(BF16).astype(F32)
    low = (values - high).astype(BF16).astype(F32)
    return high, low


def forward_kernel(
    ids_ref,
    rays_hbm,
    volume_hbm,
    weights_hbm,
    out_hbm,
    rays_ref,
    volume_ref,
    weights_ref,
    out_ref,
    table_ref,
    sums_ref,
    rays_sem,
    volume_sem,
    weights_sem,
    out_sem,
):
    depth, projections, _ = sums_ref.shape
    width, lanes = table_ref.shape
    parts, _, _, share = out_ref.shape

    def volume_copy(z):
        return pltpu.make_async_copy(volume_hbm.at[z], volume_ref.at[z], volume_sem.at[z])

    def weights_copy(a):
        return pltpu.make_async_copy(
            weights_hbm.at[ids_ref[a]], weights_ref.at[a], weights_sem.at[a]
        )

    def out_copy(a):
        return pltpu.make_async_copy(out_ref.at[:, a], out_hbm.at[:, a], out_sem.at[a])

    rays_copy = pltpu.make_async_copy(rays_hbm, rays_ref, rays_sem)
    rays_copy.start()
    for z in range(min(AHEAD, depth)):
        volume_copy(z).start()
    for a in range(min(max(AHEAD - depth, 0), projections)):
        weights_copy(a).start()

    rays_copy.wait()
    rows = jnp.concatenate([rays_ref[pl.ds(ids_ref[a], 1), :] for a in range(projections)], axis=0)
    high, low = split_bf16(rows)
    stacked = [high, low]
    if lanes > 2 * projections:
        stacked.append(jnp.zeros((lanes - 2 * projections, width), F32))
    table_ref[...] = jnp.concatenate(stacked, axis=0).T.astype(BF16)

    @pl.loop(0, depth)
    def _(z):
        volume_copy(z).wait()

        @pl.when(z + AHEAD < depth)
        def _():
            volume_copy(z + AHEAD).start()

        @pl.when(jnp.logical_and(z + AHEAD >= depth, z + AHEAD - depth < projections))
        def _():
            weights_copy(z + AHEAD - depth).start()

        piece = min(512, width)
        first = second = None
        for k in range(0, width, piece):
            block = volume_ref[z, :, k : k + piece]
            high = block.astype(BF16)
            low = (block - high.astype(F32)).astype(BF16)
            of_high = dot(high, table_ref[k : k + piece, :])
            of_low = dot(low, table_ref[k : k + piece, :])
            first = of_high if first is None else first + of_high
            second = of_low if second is None else second + of_low
        first = first.T
        second = second.T
        sums_ref[z] = first[:projections] + (
            first[projections : 2 * projections] + second[:projections]
        )

    @pl.loop(0, projections)
    def _(a):
        weights_copy(a).wait()

        @pl.when(a + AHEAD < projections)
        def _():
            weights_copy(a + AHEAD).start()

        rows = sums_ref[:, pl.ds(a, 1), :].reshape(depth, sums_ref.shape[2])
        result = dot(rows.astype(BF16), weights_ref[a])
        for part in range(parts):
            out_ref[part, a] = result[:, part * share : (part + 1) * share]
        out_copy(a).start()

    @pl.loop(0, projections)
    def _(a):
        out_copy(a).wait()


def forward_parts(angle_ids, volume, proj_weights, ray_weights, parts):
    depth, rows, width = volume.shape
    projections = angle_ids.shape[0]
    lanes = -(-2 * projections // LANES) * LANES
    share = width // parts
    return pl.pallas_call(
        forward_kernel,
        in_specs=[SCALARS] + [IN_HBM] * 3,
        out_specs=IN_HBM,
        out_shape=jax.ShapeDtypeStruct((parts, projections, depth, share), F32),
        scratch_shapes=[
            VMEM(ray_weights.shape, F32),
            VMEM(volume.shape, F32),
            VMEM((projections, rows, width), BF16),
            VMEM((parts, projections, depth, share), F32),
            VMEM((width, lanes), BF16),
            VMEM((depth, projections, rows), F32),
            DMA,
            pltpu.SemaphoreType.DMA((depth,)),
            pltpu.SemaphoreType.DMA((projections,)),
            pltpu.SemaphoreType.DMA((projections,)),
        ],
        compiler_params=pltpu.CompilerParams(vmem_limit_bytes=44 * MIB),
        cost_estimate=pl.CostEstimate(
            flops=4 * depth * rows * width * lanes,
            bytes_accessed=depth * rows * width * 4 + projections * rows * width * 2,
            transcendentals=0,
        ),
        name="forward",
    )(angle_ids, ray_weights, volume, proj_weights)


def placed(values, down, across):
    rows, cols = values.shape
    tall = jnp.concatenate([values, jnp.zeros((SUBLANES, cols), F32)], axis=0)
    tall = pltpu.roll(tall, down, axis=0)
    wide = jnp.concatenate([tall, jnp.zeros((rows + SUBLANES, LANES), F32)], axis=1)
    return pltpu.roll(wide, across, axis=1)


def patch_kernel(
    rows_ref,
    cols_ref,
    count_ref,
    place_ref,
    own_hbm,
    left_hbm,
    right_hbm,
    probe_hbm,
    amp_hbm,
    dft_a_hbm,
    dft_b_hbm,
    dual_hbm,
    new_hbm,
    edge_left_hbm,
    edge_right_hbm,
    slab_hbm,
    *rest,
):
    shares = len(rest) - 26
    parts_hbm = rest[:shares]
    (
        probe_ref,
        amp_ref,
        dft_a_ref,
        dft_b_ref,
        dual_ref,
        new_ref,
        edge_left_ref,
        edge_right_ref,
        slab_ref,
        parts_ref,
        ext_ref,
        sum_ref,
        grad_ref,
        energy_ref,
        patch_a_ref,
        patch_b_ref,
        wave_a_ref,
        wave_b_ref,
        half_a_ref,
        half_b_ref,
        far_a_ref,
        far_b_ref,
        in_sem,
        slab_sem,
        parts_sem,
        out_sem,
    ) = rest[shares:]
    slots = amp_ref.shape[0]
    side = probe_ref.shape[1]
    _, height, margin = edge_left_ref.shape
    tile_cols = new_ref.shape[2]
    window = side + LANES
    chunk = 32
    tall = chunk + SUBLANES
    grad_rows = grad_ref.shape[1]
    extent = ext_ref.shape[2]
    inner = pl.ds(0, height)

    copies = [
        pltpu.make_async_copy(source, target, in_sem.at[k])
        for k, (source, target) in enumerate(
            (
                (left_hbm, ext_ref.at[:, inner, pl.ds(0, margin)]),
                (own_hbm, ext_ref.at[:, inner, pl.ds(margin, tile_cols)]),
                (right_hbm, ext_ref.at[:, inner, pl.ds(margin + tile_cols, margin)]),
                (probe_hbm, probe_ref),
                (dft_a_hbm, dft_a_ref),
                (dft_b_hbm, dft_b_ref),
                (amp_hbm, amp_ref),
                (dual_hbm, dual_ref),
            )
        )
    ]
    for copy in copies:
        copy.start()
    sum_ref[...] = jnp.zeros(sum_ref.shape, F32)
    grad_ref[...] = jnp.zeros(grad_ref.shape, F32)
    energy_ref[...] = jnp.zeros(energy_ref.shape, F32)
    for copy in copies:
        copy.wait()

    def pair_step(pair, carry):
        chains = []
        for k, refs in enumerate(
            (
                (patch_a_ref, wave_a_ref, half_a_ref, far_a_ref),
                (patch_b_ref, wave_b_ref, half_b_ref, far_b_ref),
            )
        ):
            slot = jnp.minimum(2 * pair + k, slots - 1)
            live = (2 * pair + k < count_ref[0]).astype(F32)
            row = rows_ref[slot]
            col = cols_ref[slot]
            lane = lax.rem(col, LANES)
            notch = lax.rem(row, SUBLANES)
            base = pl.multiple_of(col - lane, LANES)
            top = pl.multiple_of(row - notch, SUBLANES)
            chains.append((slot, live, lane, notch, base, top, *refs))
        for slot, live, lane, notch, base, top, patch_ref, wave_ref, half_ref, far_ref in chains:
            back_shift = lax.rem(window - lane, window)
            up_shift = lax.rem(tall - notch, tall)
            for r in range(0, side, chunk):
                cells = pl.ds(top + r, tall)
                here = slice(r, r + chunk)
                below = slice(side + r, side + r + chunk)
                x_re = pltpu.roll(ext_ref[0, cells, pl.ds(base, window)], back_shift, axis=1)
                x_im = pltpu.roll(ext_ref[1, cells, pl.ds(base, window)], back_shift, axis=1)
                x_re = pltpu.roll(x_re[:, :side], up_shift, axis=0)[:chunk]
                x_im = pltpu.roll(x_im[:, :side], up_shift, axis=0)[:chunk]
                p_re = probe_ref[0, here, :]
                p_im = probe_ref[1, here, :]
                patch_ref[here, :] = x_re
                patch_ref[below, :] = x_im
                wave_ref[here, :] = (p_re * x_re - p_im * x_im).astype(BF16)
                wave_ref[below, :] = (p_re * x_im + p_im * x_re).astype(BF16)
                power = x_re * x_re + x_im * x_im
                energy_ref[...] += live * jnp.sum(
                    power.reshape(chunk // SUBLANES, SUBLANES, side), axis=0
                )
        for *_, wave_ref, half_ref, far_ref in chains:
            half_ref[:, :side] = dot(dft_a_ref[:side, :], wave_ref[...]).astype(BF16)
            half_ref[:, side:] = dot(dft_a_ref[side:, :], wave_ref[...]).astype(BF16)
        for *_, half_ref, far_ref in chains:
            far_ref[...] = dot(half_ref[...], dft_b_ref[...])
        for slot, live, *_, wave_ref, half_ref, far_ref in chains:
            for r in range(0, side, chunk):
                here = slice(r, r + chunk)
                below = slice(side + r, side + r + chunk)
                f_re = far_ref[here, :side]
                f_im = far_ref[here, side:]
                inverse = lax.rsqrt(f_re * f_re + f_im * f_im + 0.25)
                factor = amp_ref[slot, here, :].astype(F32) * inverse - 1.0
                wave_ref[here, :] = (f_re * factor).astype(BF16)
                wave_ref[below, :] = (f_im * factor).astype(BF16)
        for *_, wave_ref, half_ref, far_ref in chains:
            half_ref[:, :side] = dot(dft_b_ref[:side, :], wave_ref[...]).astype(BF16)
            half_ref[:, side:] = dot(dft_b_ref[side:, :], wave_ref[...]).astype(BF16)
        for *_, half_ref, far_ref in chains:
            far_ref[...] = dot(half_ref[...], dft_a_ref[...])
        for slot, live, lane, notch, base, top, patch_ref, wave_ref, half_ref, far_ref in chains:
            for r in range(0, side, chunk):
                cells = pl.ds(top + r, tall)
                here = slice(r, r + chunk)
                below = slice(side + r, side + r + chunk)
                b_re = live * far_ref[here, :side]
                b_im = live * far_ref[here, side:]
                p_re = probe_ref[0, here, :]
                p_im = probe_ref[1, here, :]
                x_re = patch_ref[here, :]
                x_im = patch_ref[below, :]
                o_re = p_re * b_re + p_im * b_im
                o_im = p_re * b_im - p_im * b_re
                sum_ref[0, cells, pl.ds(base, window)] += placed(o_re, notch, lane)
                sum_ref[1, cells, pl.ds(base, window)] += placed(o_im, notch, lane)
                at = r % grad_rows
                part = r // grad_rows
                rows = slice(at, at + chunk)
                grad_ref[part, rows, :] += x_re * b_re + x_im * b_im
                part += side // grad_rows
                grad_ref[part, rows, :] += x_re * b_im - x_im * b_re
        return carry

    lax.fori_loop(0, lax.div(count_ref[0] + 1, 2), pair_step, 0)

    p_re = probe_ref[0]
    p_im = probe_ref[1]
    peak = jnp.max(p_re * p_re + p_im * p_im)
    scale = 1.0 / (jnp.full((1, LANES), peak, F32) + 1e-05)
    wide = jnp.tile(scale, (1, tile_cols // LANES))
    shares, layers, depth, share = slab_ref.shape
    edge = min(share - tile_cols // shares, margin)
    share -= edge
    holders = margin // edge
    first = (height - layers * depth) // 2
    band = pl.ds(first, layers * depth)
    mid = slice(margin, margin + tile_cols)
    far_side = slice(margin + tile_cols, 2 * margin + tile_cols)
    own_band = ext_ref[1, band, mid] + sum_ref[1, band, mid] * wide + dual_ref[...]
    left_band = sum_ref[1, band, :margin] * scale
    right_band = sum_ref[1, band, far_side] * scale
    for layer in range(layers):
        rows = slice(layer * depth, (layer + 1) * depth)
        for p in range(shares):
            slab_ref[p, layer, :, :share] = own_band[rows, p * share : (p + 1) * share]
            begin = (p - shares + holders) * edge
            if p < holders:
                outgoing = left_band[rows, p * edge : (p + 1) * edge]
            elif p >= shares - holders:
                outgoing = right_band[rows, begin : begin + edge]
            else:
                outgoing = jnp.zeros((depth, edge), F32)
            slab_ref[p, layer, :, share:] = outgoing
    slab_copy = pltpu.make_async_copy(slab_ref, slab_hbm, slab_sem)
    slab_copy.start()
    part_copies = []
    for step in range(shares):
        part = lax.rem(place_ref[0] + step, shares)
        parts_ref[step, :grad_rows, :] = grad_ref[part]
        parts_ref[step, grad_rows:, :] = energy_ref[...]
        part_copies.append(
            pltpu.make_async_copy(parts_ref.at[step], parts_hbm[step], parts_sem.at[step])
        )
        part_copies[-1].start()
    for c in range(2):
        new_ref[c] = ext_ref[c, inner, mid] + sum_ref[c, inner, mid] * wide
        edge_left_ref[c] = sum_ref[c, inner, :margin] * scale
        edge_right_ref[c] = sum_ref[c, inner, far_side] * scale
    last_copies = [
        pltpu.make_async_copy(source, target, out_sem.at[k])
        for k, (source, target) in enumerate(
            (
                (new_ref, new_hbm),
                (edge_left_ref, edge_left_hbm),
                (edge_right_ref, edge_right_hbm),
            )
        )
    ]
    for copy in last_copies:
        copy.start()
    slab_copy.wait()
    for copy in part_copies + last_copies:
        copy.wait()


def patch_updates(
    rows, cols, count, place, own, left, right, probe, amplitudes, dual, shares, layers
):
    side = probe.shape[1]
    _, height, tile_cols = own.shape
    margin = left.shape[2]
    slots = amplitudes.shape[0]
    slab_rows = dual.shape[0]
    share = tile_cols // shares
    edge = min(share, margin)
    dft_a, dft_b = dft_blocks(side)
    extent = tile_cols + 2 * margin + LANES
    shape = jax.ShapeDtypeStruct
    slab_shape = (shares, layers, slab_rows // layers, share + edge)
    part_rows = 2 * side // shares
    return pl.pallas_call(
        patch_kernel,
        in_specs=[SCALARS] * 4 + [IN_HBM, ANYWHERE, ANYWHERE] + [IN_HBM] * 5,
        out_specs=[IN_HBM] * (4 + shares),
        out_shape=[
            shape((2, height, tile_cols), F32),
            shape((2, height, margin), F32),
            shape((2, height, margin), F32),
            shape(slab_shape, F32),
        ]
        + [shape((part_rows + ENERGY_ROWS, side), F32)] * shares,
        scratch_shapes=[
            VMEM(probe.shape, F32),
            VMEM(amplitudes.shape, BF16),
            VMEM(dft_a.shape, BF16),
            VMEM(dft_b.shape, BF16),
            VMEM(dual.shape, F32),
            VMEM((2, height, tile_cols), F32),
            VMEM((2, height, margin), F32),
            VMEM((2, height, margin), F32),
            VMEM(slab_shape, F32),
            VMEM((shares, part_rows + ENERGY_ROWS, side), F32),
            VMEM((2, height + SUBLANES, extent), F32),
            VMEM((2, height + SUBLANES, extent), F32),
            VMEM((shares, part_rows, side), F32),
            VMEM((ENERGY_ROWS, side), F32),
            VMEM((2 * side, side), F32),
            VMEM((2 * side, side), F32),
            VMEM((2 * side, side), BF16),
            VMEM((2 * side, side), BF16),
            VMEM((side, 2 * side), BF16),
            VMEM((side, 2 * side), BF16),
            VMEM((side, 2 * side), F32),
            VMEM((side, 2 * side), F32),
            pltpu.SemaphoreType.DMA((8,)),
            DMA,
            pltpu.SemaphoreType.DMA((shares,)),
            pltpu.SemaphoreType.DMA((3,)),
        ],
        compiler_params=pltpu.CompilerParams(vmem_limit_bytes=32 * MIB),
        cost_estimate=pl.CostEstimate(
            flops=slots * 32 * side**3,
            bytes_accessed=8 * height * tile_cols * 4,
            transcendentals=slots * side * side,
        ),
        name="patches",
    )(
        rows,
        cols,
        count,
        place,
        own,
        left,
        right,
        probe,
        amplitudes,
        jnp.asarray(dft_a),
        jnp.asarray(dft_b),
        dual,
    )


def backward_kernel(
    ids_ref, residual_hbm, weights_hbm, out_ref, residual_ref, weights_ref, turned_ref, sem, weights_sem
):
    parts, projections, depth, share = residual_ref.shape
    both = projections * depth

    def weights_copy(a):
        return pltpu.make_async_copy(
            weights_hbm.at[ids_ref[a]], weights_ref.at[a], weights_sem.at[a]
        )

    residual_copy = pltpu.make_async_copy(residual_hbm, residual_ref, sem)
    residual_copy.start()
    for a in range(projections):
        weights_copy(a).start()
    residual_copy.wait()
    for part in range(parts):
        block = residual_ref[part].astype(F32).reshape(both, share)
        turned_ref[part * share : (part + 1) * share, :] = block.T
    out_ref[...] = jnp.zeros(out_ref.shape, F32)

    @pl.loop(0, projections)
    def _(a):
        weights_copy(a).wait()
        lane = lax.broadcasted_iota(jnp.int32, turned_ref.shape, 1)
        begin = a * depth
        kept = jnp.logical_and(lane >= begin, lane < begin + depth)
        chosen = jnp.where(kept, turned_ref[...], 0.0).astype(BF16)
        out_ref[...] += dot(weights_ref[a], chosen)


def backward_sums(angle_ids, residual, proj_weights):
    _, rows, width = proj_weights.shape
    _, projections, depth, _ = residual.shape
    return pl.pallas_call(
        backward_kernel,
        in_specs=[SCALARS, ANYWHERE, IN_HBM],
        out_specs=WHOLE,
        out_shape=jax.ShapeDtypeStruct((rows, projections * depth), F32),
        scratch_shapes=[
            VMEM(residual.shape, BF16),
            VMEM((projections, rows, width), BF16),
            VMEM((width, projections * depth), F32),
            DMA,
            pltpu.SemaphoreType.DMA((projections,)),
        ],
        compiler_params=pltpu.CompilerParams(vmem_limit_bytes=32 * MIB),
        cost_estimate=pl.CostEstimate(
            flops=2 * rows * width * projections * projections * depth,
            bytes_accessed=projections * rows * width * 2,
            transcendentals=0,
        ),
        name="backward",
    )(angle_ids, residual, proj_weights)


def update_kernel(
    ids_ref,
    sums_ref,
    rays_hbm,
    volume_hbm,
    object_hbm,
    from_left_hbm,
    from_right_hbm,
    out_hbm,
    new_object_hbm,
    rays_ref,
    stack_ref,
    spread_ref,
    volume_ref,
    done_ref,
    cells_ref,
    left_ref,
    right_ref,
    rays_sem,
    volume_sem,
    out_sem,
    object_sem,
):
    depth = volume_ref.shape[0]
    slots = done_ref.shape[0]
    margin = left_ref.shape[2]
    tile_cols = cells_ref.shape[2]
    width = rays_ref.shape[1]
    projections = sums_ref.shape[1] // depth
    both = sums_ref.shape[1]

    def volume_copy(z):
        return pltpu.make_async_copy(volume_hbm.at[z], volume_ref.at[z], volume_sem.at[z])

    def out_copy(z):
        slot = lax.rem(z, slots)
        return pltpu.make_async_copy(done_ref.at[slot], out_hbm.at[z], out_sem.at[slot])

    rays_copy = pltpu.make_async_copy(rays_hbm, rays_ref, rays_sem)
    rays_copy.start()
    for z in range(min(AHEAD, depth)):
        volume_copy(z).start()
    copies = [
        pltpu.make_async_copy(source, target, object_sem.at[k])
        for k, (source, target) in enumerate(
            ((object_hbm, cells_ref), (from_left_hbm, left_ref), (from_right_hbm, right_ref))
        )
    ]
    for copy in copies:
        copy.start()
    high, low = split_bf16(sums_ref[...])
    stack_ref[...] = jnp.concatenate([high, low, high, low], axis=1)
    rays_copy.wait()
    rows = [
        jnp.broadcast_to(rays_ref[pl.ds(ids_ref[a], 1), :], (depth, width))
        for a in range(projections)
    ]
    high, low = split_bf16(jnp.concatenate(rows, axis=0))
    for place, block in enumerate((high, high, low, low)):
        spread_ref[place * both : (place + 1) * both, :] = block.astype(BF16)

    @pl.loop(0, depth)
    def _(z):
        volume_copy(z).wait()

        @pl.when(z + AHEAD < depth)
        def _():
            volume_copy(z + AHEAD).start()

        @pl.when(z >= slots)
        def _():
            out_copy(z - slots).wait()

        lane = lax.broadcasted_iota(jnp.int32, stack_ref.shape, 1)
        kept = lax.rem(lane, depth) == z
        chosen = jnp.where(kept, stack_ref[...], 0.0).astype(BF16)
        done_ref[lax.rem(z, slots)] = volume_ref[z] - tomo_step * dot(chosen, spread_ref[...])
        out_copy(z).start()

    for copy in copies:
        copy.wait()
    cells_ref[:, :, :margin] += left_ref[...]
    cells_ref[:, :, tile_cols - margin :] += right_ref[...]
    object_copy = pltpu.make_async_copy(cells_ref, new_object_hbm, object_sem.at[0])
    object_copy.start()
    for z in range(max(depth - slots, 0), depth):
        out_copy(z).wait()
    object_copy.wait()


def volume_update(angle_ids, sums, rays, volume, partial_object, from_left, from_right):
    depth, rows, width = volume.shape
    slots = min(4, depth)
    return pl.pallas_call(
        update_kernel,
        in_specs=[SCALARS, WHOLE] + [IN_HBM] * 3 + [ANYWHERE] * 2,
        out_specs=[IN_HBM] * 2,
        out_shape=[
            jax.ShapeDtypeStruct(volume.shape, F32),
            jax.ShapeDtypeStruct(partial_object.shape, F32),
        ],
        scratch_shapes=[
            VMEM(rays.shape, F32),
            VMEM((rows, 4 * sums.shape[1]), F32),
            VMEM((4 * sums.shape[1], width), BF16),
            VMEM(volume.shape, F32),
            VMEM((slots, rows, width), F32),
            VMEM(partial_object.shape, F32),
            VMEM(from_left.shape, F32),
            VMEM(from_right.shape, F32),
            DMA,
            pltpu.SemaphoreType.DMA((depth,)),
            pltpu.SemaphoreType.DMA((slots,)),
            pltpu.SemaphoreType.DMA((3,)),
        ],
        compiler_params=pltpu.CompilerParams(vmem_limit_bytes=48 * MIB),
        cost_estimate=pl.CostEstimate(
            flops=8 * rows * width * sums.shape[1] * depth,
            bytes_accessed=2 * depth * rows * width * 4,
            transcendentals=0,
        ),
        name="update",
    )(angle_ids, sums, rays, volume, partial_object, from_left, from_right)


def gather_parts_kernel(group, *refs):
    *given, out_hbm, out_ref, sem = refs
    total = given[0][...]
    for ref in given[1:]:
        total = total + ref[...]
    _, rows, _ = out_ref.shape
    rows -= ENERGY_ROWS
    for k in range(group):
        out_ref[k, :rows, :] = total[k * rows : (k + 1) * rows]
        out_ref[k, rows:, :] = total[group * rows :]
    copy = pltpu.make_async_copy(out_ref, out_hbm, sem)
    copy.start()
    copy.wait()


def gather_parts(given, group):
    total_rows, side = given[0].shape
    rows = (total_rows - ENERGY_ROWS) // group + ENERGY_ROWS
    return pl.pallas_call(
        functools.partial(gather_parts_kernel, group),
        in_specs=[WHOLE] * len(given),
        out_specs=IN_HBM,
        out_shape=jax.ShapeDtypeStruct((group, rows, side), F32),
        scratch_shapes=[VMEM((group, rows, side), F32), DMA],
        name="probe_parts",
    )(*given)


def probe_rows_kernel(given_ref, probe_ref, out_hbm, out_ref, sem):
    group, rows, side = given_ref.shape
    rows -= ENERGY_ROWS
    total = given_ref[0]
    for k in range(1, group):
        total = total + given_ref[k]
    energy = jnp.sum(total[rows:], keepdims=True) / (side * side)
    new_rows = probe_ref[...] + total[:rows] / (energy + 1e-05)
    for k in range(group):
        out_ref[k] = new_rows
    copy = pltpu.make_async_copy(out_ref, out_hbm, sem)
    copy.start()
    copy.wait()


def probe_rows(given, own_rows):
    group, rows, side = given.shape
    shape = (group, rows - ENERGY_ROWS, side)
    return pl.pallas_call(
        probe_rows_kernel,
        in_specs=[WHOLE] * 2,
        out_specs=IN_HBM,
        out_shape=jax.ShapeDtypeStruct(shape, F32),
        scratch_shapes=[VMEM(shape, F32), DMA],
        name="probe_rows",
    )(given, own_rows)


def turned(value, axis, steps):
    count = lax.axis_size(axis)
    return lax.ppermute(value, axis, [(k, (k + steps) % count) for k in range(count)])


def on_device(
    object_field,
    probe_field,
    amplitudes,
    pos_rows,
    pos_cols,
    counts,
    admm_dual,
    volume,
    proj_weights,
    ray_weights,
    angle_ids,
):
    margin = probe_field.shape[1] // 2
    own = object_field[0]
    tile_cols = own.shape[2]
    flat_axes = ("tile", "proj")
    plane = lax.axis_size("tile") * lax.axis_size("proj")
    proj_count = lax.axis_size("proj")
    layers = lax.axis_size("cuts")
    from_left = shifted(own[:, :, tile_cols - margin :], "tile", 1)
    from_right = shifted(own[:, :, :margin], "tile", -1)
    forward = forward_parts(angle_ids, volume, proj_weights, ray_weights, plane)
    arrived = lax.all_to_all(forward, flat_axes, 0, 0, tiled=True)
    place = lax.axis_index("proj")
    partial_object, edge_left, edge_right, slab, *grad_parts = patch_updates(
        pos_rows[0, 0],
        pos_cols[0, 0],
        counts[0],
        place[None],
        own,
        from_left,
        from_right,
        probe_field,
        amplitudes[0, 0],
        admm_dual[0],
        proj_count,
        layers,
    )

    share = tile_cols // proj_count
    edge = slab.shape[3] - share
    holders = margin // edge
    pieces = slab.reshape(proj_count * layers, *slab.shape[2:])
    pieces = lax.all_to_all(pieces, ("proj", "cuts"), 0, 0, tiled=True)
    pairs = []
    for tile in range(lax.axis_size("tile") - 1):
        for k in range(holders):
            lower = tile * proj_count + proj_count - holders + k
            upper = (tile + 1) * proj_count + k
            pairs += [(lower, upper), (upper, lower)]
    grads_in = lax.ppermute(pieces[:, :, share:], flat_axes, pairs)
    at_start = jnp.pad(grads_in, ((0, 0), (0, 0), (0, share - edge)))
    at_end = jnp.pad(grads_in, ((0, 0), (0, 0), (share - edge, 0)))
    target = pieces[:, :, :share] + jnp.where(place < holders, at_start, at_end)
    residual = (jnp.sum(arrived, axis=0) - target).astype(BF16)
    copies = jnp.broadcast_to(residual[None], (plane, *residual.shape))

    group_axes = ("tile", "cuts")
    group = lax.axis_size("tile") * layers
    given = [grad_parts[0]]
    for step in range(1, proj_count):
        given.append(turned(grad_parts[step], "proj", step))
    by_receiver = gather_parts(given, group)
    copies, by_receiver = lax.optimization_barrier((copies, by_receiver))
    residual = lax.all_to_all(copies, flat_axes, 0, 0, tiled=True)
    received = lax.all_to_all(by_receiver, group_axes, 0, 0, tiled=True)

    residual, edge_left, edge_right = lax.optimization_barrier((residual, edge_left, edge_right))
    edge_from_right = shifted(edge_left, "tile", -1)
    edge_from_left = shifted(edge_right, "tile", 1)
    back_sums = backward_sums(angle_ids, residual, proj_weights)

    back_sums, received = lax.optimization_barrier((back_sums, received))
    side = probe_field.shape[1]
    rows = received.shape[1] - ENERGY_ROWS
    begin = (place * group + lax.axis_index(group_axes)) * rows
    own_rows = lax.dynamic_slice(
        probe_field.reshape(2 * side, side), (begin, jnp.zeros((), begin.dtype)), (rows, side)
    )
    new_rows = lax.all_to_all(probe_rows(received, own_rows), group_axes, 0, 0, tiled=True)

    new_volume, new_object = volume_update(
        angle_ids,
        back_sums,
        ray_weights,
        volume,
        partial_object,
        edge_from_left,
        edge_from_right,
    )
    new_volume, new_rows = lax.optimization_barrier((new_volume, new_rows))
    new_rows = new_rows.reshape(group * rows, side)
    if proj_count == 2:
        other = turned(new_rows, "proj", 1)
        first = place == 0
        new_probe = jnp.concatenate(
            [jnp.where(first, new_rows, other), jnp.where(first, other, new_rows)], axis=0
        )
    else:
        new_probe = lax.all_gather(new_rows, "proj", axis=0, tiled=True)
    return (new_object[None], new_probe.reshape(2, side, side), new_volume)


def solution(mesh):
    in_specs = (
        P(("proj", "cuts"), None, None, "tile"),
        P(),
        P(("proj", "cuts"), "tile", None, None, None),
        P(("proj", "cuts"), "tile", None),
        P(("proj", "cuts"), "tile", None),
        P(("proj", "cuts"), "tile"),
        P(("proj", "cuts"), None, "tile"),
        P("cuts", ("tile", "proj"), None),
        P(None, ("tile", "proj"), None),
        P(),
        P(),
    )
    out_specs = (P(("proj", "cuts"), None, None, "tile"), P(), P("cuts", ("tile", "proj"), None))
    return jax.shard_map(
        on_device, mesh=mesh, in_specs=in_specs, out_specs=out_specs, check_vma=False
    )
```

time: 144 us -> 133 us (0.924)
  local copies, waits for them, and re-layouts: 36.2 us -> 19.8 us
  Pallas kernels: 30.3 us -> 39.1 us
  starting transfers between devices: 38.1 us -> 44.1 us
  blocking collectives: 14.5 us -> 9.35 us
  other arithmetic: 4.65 us -> 0.92 us
    unnamed x43 -> x42, local copies, waits for them, and re-layouts: 32.7 us -> 17.2 us
    all_to_all x3 -> x2, waiting for transfers between devices: 11.3 us -> 0.01 us  [the longest x1 0.01 us: on_device(): lax.all_to_all(probe_rows(received, own_rows), group_axes, 0, 0, tiled=True)]
    pallas_call x4 -> x6, Pallas kernels: 30.3 us -> 39.1 us  [the longest x1 13.5 us: volume_update(): pl.pallas_call(update_kernel, in_specs=[SCALARS, WHOLE] + [IN_HBM] * 3 +...]
    all_to_all x1, waiting for transfers between devices: 0.01 us -> 8.56 us  [on_device(): arrived = lax.all_to_all(forward, flat_axes, 0, 0, tiled=True)]
    ppermute x4, waiting for transfers between devices: 0.01 us -> 7.33 us  [shifted(): lax.ppermute(value, axis, [(source, source + steps) for source in range(l...]
    all_to_all x1, starting transfers between devices: 4.17 us -> 9.84 us  [on_device(): arrived = lax.all_to_all(forward, flat_axes, 0, 0, tiled=True)]
    all_to_all x1, waiting for transfers between devices: 5.36 us -> 0.01 us  [on_device(): pieces = lax.all_to_all(pieces, ('proj', 'cuts'), 0, 0, tiled=True)]
    all_to_all x1, blocking collectives: 14.5 us -> 9.35 us  [on_device(): residual = lax.all_to_all(copies, flat_axes, 0, 0, tiled=True)]
  transfers between devices with their start and end apart: 10 -> 11, of which waited for: 3 -> 3; matrix products, arithmetic and copies ran while one was open for 4% -> 1% of each run, Pallas kernels for 21% -> 24%
where the time goes in v2:
time: 133 us; the launch traced here: 132 us
  starting transfers between devices  44.1 us (33%)
  Pallas kernels  39.1 us (29%)
  local copies, waits for them, and re-layouts  19.8 us (15%)
  waiting for transfers between devices  17.4 us (13%)
  blocking collectives  9.35 us (7%)
  between operations  1.59 us (1%)
    unnamed x42, local copies, waits for them, and re-layouts  17.2 us
    pallas_call x1, Pallas kernels, volume_update(): pl.pallas_call(update_kernel, in_specs=[SCALARS, WHOLE] + [IN_HBM] * 3 +...  13.5 us
    ppermute x4, starting transfers between devices, shifted(): lax.ppermute(value, axis, [(source, source + steps) for source in range(l...  11.9 us
    pallas_call x1, Pallas kernels, forward_parts(): pl.pallas_call(forward_kernel, in_specs=[SCALARS] + [IN_HBM] * 3, out_spe...  11.5 us
    all_to_all x1, starting transfers between devices, on_device(): arrived = lax.all_to_all(forward, flat_axes, 0, 0, tiled=True)  9.84 us
    all_to_all x1, blocking collectives, on_device(): residual = lax.all_to_all(copies, flat_axes, 0, 0, tiled=True)  9.35 us
    all_to_all x1, waiting for transfers between devices, on_device(): arrived = lax.all_to_all(forward, flat_axes, 0, 0, tiled=True)  8.56 us
    all_to_all x1, starting transfers between devices, on_device(): pieces = lax.all_to_all(pieces, ('proj', 'cuts'), 0, 0, tiled=True)  8.4 us
  transfers between devices with their start and end apart: 11, of which 3 were waited for; matrix products, arithmetic and copies ran while one was open for 1% of the time, Pallas kernels for 24%

profile of v2, /device:TPU:0, one launch (start us, length us, event | category | flops | bytes accessed | tf_op | source)
XLA Modules:
  0.0 132.3 jit_solution(11891683861976502579)
XLA Ops:
  0.6 0.0 copy-start.2
  0.7 1.3 fusion.2
  2.0 1.3 collective-permute-start.1
  3.3 5.5 %collective-permute-start = (f32[2,384,128]{2,1,0:T(8,128)S(1)}, f32[2,384,128]{2,1,0:T(8,128)S(1)}, u32[]{:S(2)}, u32[]{:S(2)}) collective-permute-start(f32[2,384,128]{2,1,0:T(8,128)S(1)} %get-tuple-element.38), channel_id=1, source_target_pairs={{0,8},{8,16},{16,24},{1,9},{9,17},{17,25},{2,10},{10,18},{18,26},{... | collective-permute-start | bytes 1179656 | tf_op jit(solution)/shard_map/ppermute | solution.py:32
  9.4 7.3 %collective-permute-done.1.right_hbm = f32[2,384,128]{2,1,0:T(8,128)S(1)} collective-permute-done((f32[2,384,128]{2,1,0:T(8,128)S(1)}, f32[2,384,128]{2,1,0:T(8,128)S(1)}, u32[]{:S(2)}, u32[]{:S(2)}) %collective-permute-start.1) | collective-permute-done | bytes 393248 | tf_op jit(solution)/shard_map/ppermute | solution.py:32
  16.7 0.7 copy-done.9
  17.5 0.0 collective-permute-done.left_hbm
  17.5 0.7 copy-done.11
  18.2 1.0 copy-done.5
  19.3 1.1 copy-done.6
  20.4 1.0 copy-done.10
  21.4 1.0 copy-done.12
  22.4 0.8 copy-done.15
  23.2 1.0 copy-done.18
  24.3 1.0 copy-done.19
  25.3 5.4 %patches.1 = (f32[2,384,512]{2,1,0:T(8,128)S(1)}, f32[2,384,128]{2,1,0:T(8,128)S(1)}, f32[2,384,128]{2,1,0:T(8,128)}, f32[2,4,8,384]{3,2,1,0:T(8,128)}, f32[264,256]{1,0:T(8,128)S(1)}, /*index=5*/f32[264,256]{1,0:T(8,128)S(1)}) custom-call(s32[6]{0:T(128)S(1)} %bitcast.20, s32[6]{0:T(128)S(1)} %bitcast.21, s32[1]{0:T(128)} %bitcast.14.count_ref, ...), custom_call_target="tpu_custom_call" | custom-call | flops 3221225472 | bytes 6291456 | tf_op jit(solution)/shard_map/patches/pallas_call | solution.py:432
  30.8 0.7 copy-done.3
  31.5 0.7 copy-done.7
  32.2 0.7 copy-done.13
  32.9 8.4 %all-to-all-start.1 = ((f32[8,8,384]{2,1,0:T(8,128)}), f32[8,8,384]{2,1,0:T(8,128)S(1)}, u32[]{:S(2)}, u32[]{:S(2)}) async-start(f32[8,8,384]{2,1,0:T(8,128)} %bitcast.7), calls=%async_computation.1 | async-start | bytes 196608 | tf_op jit(solution)/shard_map/all_to_all | solution.py:780
  41.4 11.5 %forward.1 = f32[8,8,8,256]{3,2,1,0:T(8,128)} custom-call(s32[8]{0:T(128)S(1)} %copy-done.4, f32[16,2048]{1,0:T(8,128)S(1)} %copy-done.1, f32[8,256,2048]{2,1,0:T(8,128)} %volume_hbm.3, bf16[16,256,2048]{2,1,0:T(8,128)(2,1)} %weights_hbm.3), custom_call_target="tpu_custom_call" | custom-call | flops 2147483648 | bytes 25165824 | tf_op jit(solution)/shard_map/forward/pallas_call | solution.py:156
  52.9 0.0 all-to-all-done.1
  52.9 9.8 %all-to-all-start = ((f32[8,8,8,256]{3,2,1,0:T(8,128)}), f32[8,8,8,256]{3,2,1,0:T(8,128)S(1)}, u32[]{:S(2)}, u32[]{:S(2)}) async-start(f32[8,8,8,256]{3,2,1,0:T(8,128)} %forward.1), calls=%async_computation | async-start | bytes 1048576 | tf_op jit(solution)/shard_map/all_to_all | solution.py:759
  62.7 0.5 collective-permute-start.3
  63.2 0.7 collective-permute-start.2
  63.9 0.0 copy-start.8
  63.9 8.6 %all-to-all-done = f32[8,8,8,256]{3,2,1,0:T(8,128)S(1)} async-done(((f32[8,8,8,256]{3,2,1,0:T(8,128)}), f32[8,8,8,256]{3,2,1,0:T(8,128)S(1)}, u32[]{:S(2)}, u32[]{:S(2)}) %all-to-all-start) | async-done | bytes 524320 | tf_op jit(solution)/shard_map/all_to_all | solution.py:759
  72.5 0.0 collective-permute-done.2
  72.5 0.0 collective-permute-done.3.refs_1_
  72.6 0.7 copy-done.20
  73.3 1.8 %probe_parts.1 = f32[16,24,256]{2,1,0:T(8,128)} custom-call(f32[264,256]{1,0:T(8,128)} %copy-done.3, f32[264,256]{1,0:T(8,128)} %copy-done.20), custom_call_target="tpu_custom_call" | custom-call | tf_op jit(solution)/shard_map/probe_parts/pallas_call | solution.py:693
  75.1 9.3 %all_to_all.25.residual_hbm = bf16[8,8,8,256]{3,2,1,0:T(8,128)(2,1)S(1)} all-to-all(bf16[8,8,8,256]{3,2,1,0:T(8,128)(2,1)S(1)} %broadcast_in_dim.13), channel_id=1, replica_groups=mesh['tile'=4,'proj'=2,'cuts'=4] {'tile','proj'}, dimensions={0} | all-to-all | bytes 524288 | tf_op jit(solution)/shard_map/all_to_all | solution.py:801
  84.5 5.1 %all-to-all-start.3 = ((f32[16,24,256]{2,1,0:T(8,128)}), f32[16,24,256]{2,1,0:T(8,128)}, u32[]{:S(2)}, u32[]{:S(2)}) async-start(f32[16,24,256]{2,1,0:T(8,128)} %probe_parts.1), calls=%async_computation.3 | async-start | bytes 786432 | tf_op jit(solution)/shard_map/all_to_all | solution.py:802
  89.6 3.8 %collective-permute-start.4 = (f32[2,384,128]{2,1,0:T(8,128)}, f32[2,384,128]{2,1,0:T(8,128)S(1)}, u32[]{:S(2)}, u32[]{:S(2)}) collective-permute-start(f32[2,384,128]{2,1,0:T(8,128)} %get-tuple-element.30), channel_id=1, source_target_pairs={{0,8},{8,16},{16,24},{1,9},{9,17},{17,25},{2,10},{10,18},{18,26},{... | collective-permute-start | bytes 1179656 | tf_op jit(solution)/shard_map/ppermute | solution.py:32
  93.4 1.3 collective-permute-start.5
  94.7 1.3 %constant_dynamic-slice_fusion.probe_ref = f32[16,256]{1,0:T(8,128)} fusion(f32[512,256]{1,0:T(8,128)} %bitcast.17, s32[]{:T(128)S(6)} %select_n.26), kind=kLoop, calls=%fused_computation.6 | loop fusion | bytes 32772 | tf_op jit(solution)/shard_map/dynamic_slice | solution.py:813
  96.0 5.8 %copy-done = bf16[16,256,2048]{2,1,0:T(8,128)(2,1)S(1)} copy-done((bf16[16,256,2048]{2,1,0:T(8,128)(2,1)S(1)}, bf16[16,256,2048]{2,1,0:T(8,128)(2,1)}, u32[]{:S(2)}) %copy-start) | copy-done | bytes 16777240
  101.8 4.9 %backward.1.sums_ref = f32[256,64]{1,0:T(8,128)S(1)} custom-call(s32[8]{0:T(128)S(1)} %copy-done.4, bf16[8,8,8,256]{3,2,1,0:T(8,128)(2,1)S(1)} %all_to_all.25.residual_hbm, bf16[16,256,2048]{2,1,0:T(8,128)(2,1)S(1)} %copy-done), custom_call_target="tpu_custom_call" | custom-call | flops 536870912 | bytes 8388608 | tf_op jit(solution)/shard_map/backward/pallas_call | solution.py:528
  106.8 0.0 all-to-all-done.3.given_ref
  106.8 1.9 %probe_rows.1 = f32[16,16,256]{2,1,0:T(8,128)} custom-call(f32[16,24,256]{2,1,0:T(8,128)} %all-to-all-done.3.given_ref, f32[16,256]{1,0:T(8,128)} %constant_dynamic-slice_fusion.probe_ref), custom_call_target="tpu_custom_call" | custom-call | tf_op jit(solution)/shard_map/probe_rows/pallas_call | solution.py:721
  108.6 7.6 %all-to-all-start.4 = ((f32[16,16,256]{2,1,0:T(8,128)}), f32[16,16,256]{2,1,0:T(8,128)S(1)}, u32[]{:S(2)}, u32[]{:S(2)}) async-start(f32[16,16,256]{2,1,0:T(8,128)} %probe_rows.1), calls=%async_computation.4 | async-start | bytes 524288 | tf_op jit(solution)/shard_map/all_to_all | solution.py:816
  116.3 0.0 collective-permute-done.4.from_left_hbm
  116.3 0.0 collective-permute-done.5.from_right_hbm
  116.3 13.5 %update.1 = (f32[8,256,2048]{2,1,0:T(8,128)}, f32[2,384,512]{2,1,0:T(8,128)}) custom-call(s32[8]{0:T(128)S(1)} %copy-done.4, f32[256,64]{1,0:T(8,128)S(1)} %backward.1.sums_ref, f32[16,2048]{1,0:T(8,128)S(1)} %copy-done.1, f32[8,256,2048]{2,1,0:T(8,128)} %volume_hbm.3, f32[2,384,512]{2,1,0:T(8,128)S(1)} %get-tuple-element.29.object_hbm, ...), custom_call_target="tpu_custom_call" | custom-call | flops 2147483648 | bytes 33554432 | tf_op jit(solution)/shard_map/update/pallas_call | solution.py:643
  129.9 0.0 all-to-all-done.4
  129.9 0.1 collective-permute-start.6
  130.0 1.5 %collective-permute-done.6 = f32[256,256]{1,0:T(8,128)S(1)} collective-permute-done((f32[256,256]{1,0:T(8,128)S(1)}, f32[256,256]{1,0:T(8,128)S(1)}, u32[]{:S(2)}, u32[]{:S(2)}) %collective-permute-start.6) | collective-permute-done | bytes 262176 | tf_op jit(solution)/shard_map/ppermute | solution.py:733
  131.5 0.8 pad_maximum_fusion
  (31 shorter events, 0.2 us)
Async XLA Ops:
  0.6 17.6 %copy-start.2 = (f32[1,2,384,512]{3,2,1,0:T(8,128)S(1)}, f32[1,2,384,512]{3,2,1,0:T(8,128)}, u32[]{:S(2)}) copy-start(f32[1,2,384,512]{3,2,1,0:T(8,128)} %param.13) | copy-start | bytes 4718596
  0.6 17.6 %copy-start.17 = (s32[1,1,6]{2,1,0:T(1,128)S(1)}, s32[1,1,6]{2,1,0:T(1,128)}, u32[]{:S(2)}) copy-start(s32[1,1,6]{2,1,0:T(1,128)} %param.17) | copy-start | bytes 76
  0.7 17.6 %copy-start.16 = (s32[1,1,6]{2,1,0:T(1,128)S(1)}, s32[1,1,6]{2,1,0:T(1,128)}, u32[]{:S(2)}) copy-start(s32[1,1,6]{2,1,0:T(1,128)} %param.16) | copy-start | bytes 76
  2.0 14.8 %collective-permute-start.1 = (f32[2,384,128]{2,1,0:T(8,128)S(1)}, f32[2,384,128]{2,1,0:T(8,128)S(1)}, u32[]{:S(2)}, u32[]{:S(2)}) collective-permute-start(f32[2,384,128]{2,1,0:T(8,128)S(1)} %get-tuple-element.37), channel_id=1, source_target_pairs={{8,0},{16,8},{24,16},{9,1},{17,9},{25,17},{10,2},{18,10},{26,18},{... | collective-permute-start | bytes 1179656 | tf_op jit(solution)/shard_map/ppermute | solution.py:32
  3.3 14.2 %collective-permute-start = (f32[2,384,128]{2,1,0:T(8,128)S(1)}, f32[2,384,128]{2,1,0:T(8,128)S(1)}, u32[]{:S(2)}, u32[]{:S(2)}) collective-permute-start(f32[2,384,128]{2,1,0:T(8,128)S(1)} %get-tuple-element.38), channel_id=1, source_target_pairs={{0,8},{8,16},{16,24},{1,9},{9,17},{17,25},{2,10},{10,18},{18,26},{... | collective-permute-start | bytes 1179656 | tf_op jit(solution)/shard_map/ppermute | solution.py:32
  16.7 0.7 copy-start.9
  17.5 0.7 copy-start.11
  18.2 1.0 copy-start.5
  19.3 1.1 copy-start.6
  20.4 1.0 copy-start.10
  21.4 1.0 copy-start.12
  22.4 0.8 copy-start.15
  23.2 1.0 copy-start.18
  24.3 1.0 copy-start.19
  25.3 16.0 %copy-start.1 = (f32[16,2048]{1,0:T(8,128)S(1)}, f32[16,2048]{1,0:T(8,128)}, u32[]{:S(2)}) copy-start(f32[16,2048]{1,0:T(8,128)} %rays_hbm.3) | copy-start | bytes 393220
  25.3 16.0 %copy-start.4 = (s32[8]{0:T(128)S(1)}, s32[8]{0:T(128)}, u32[]{:S(2)}) copy-start(s32[8]{0:T(128)} %ids_ref.5) | copy-start | bytes 100
  30.8 0.7 copy-start.3
  31.5 0.7 copy-start.7
  32.2 0.7 copy-start.13
  32.9 19.9 %all-to-all-start.1 = ((f32[8,8,384]{2,1,0:T(8,128)}), f32[8,8,384]{2,1,0:T(8,128)S(1)}, u32[]{:S(2)}, u32[]{:S(2)}) async-start(f32[8,8,384]{2,1,0:T(8,128)} %bitcast.7), calls=%async_computation.1 | async-start | bytes 196608 | tf_op jit(solution)/shard_map/all_to_all | solution.py:780
  41.4 21.4 %copy-start.14 = (f32[264,256]{1,0:T(8,128)S(1)}, f32[264,256]{1,0:T(8,128)}, u32[]{:S(2)}) copy-start(f32[264,256]{1,0:T(8,128)} %copy-done.13) | copy-start | bytes 811012
  52.9 19.6 %all-to-all-start = ((f32[8,8,8,256]{3,2,1,0:T(8,128)}), f32[8,8,8,256]{3,2,1,0:T(8,128)S(1)}, u32[]{:S(2)}, u32[]{:S(2)}) async-start(f32[8,8,8,256]{3,2,1,0:T(8,128)} %forward.1), calls=%async_computation | async-start | bytes 1048576 | tf_op jit(solution)/shard_map/all_to_all | solution.py:759
  62.7 9.8 %collective-permute-start.3 = (f32[264,256]{1,0:T(8,128)S(1)}, f32[264,256]{1,0:T(8,128)S(1)}, u32[]{:S(2)}, u32[]{:S(2)}) collective-permute-start(f32[264,256]{1,0:T(8,128)S(1)} %copy-done.14), channel_id=1, source_target_pairs={{0,4},{4,0},{1,5},{5,1},{2,6},{6,2},{3,7},{7,3},{8,12},{12,8},{9,1... | collective-permute-start | bytes 811016 | tf_op jit(solution)/shard_map/ppermute | solution.py:733
  63.2 9.3 %collective-permute-start.2 = (f32[8,8,128]{2,1,0:T(8,128)S(1)}, f32[8,8,128]{2,1,0:T(8,128)S(1)}, u32[]{:S(2)}, u32[]{:S(2)}) collective-permute-start(f32[8,8,128]{2,1,0:T(8,128)S(1)} %slice.19), channel_id=1, source_target_pairs={{4,8},{8,4},{12,16},{16,12},{20,24},{24,20},{5,9},{9,5},{13,17},{1... | collective-permute-start | bytes 98312 | tf_op jit(solution)/shard_map/ppermute | solution.py:787
  63.9 29.5 %copy-start.8 = (f32[2,384,128]{2,1,0:T(8,128)S(1)}, f32[2,384,128]{2,1,0:T(8,128)}, u32[]{:S(2)}) copy-start(f32[2,384,128]{2,1,0:T(8,128)} %copy-done.7) | copy-start | bytes 1179652
  72.6 0.7 copy-start.20
  84.5 22.3 %all-to-all-start.3 = ((f32[16,24,256]{2,1,0:T(8,128)}), f32[16,24,256]{2,1,0:T(8,128)}, u32[]{:S(2)}, u32[]{:S(2)}) async-start(f32[16,24,256]{2,1,0:T(8,128)} %probe_parts.1), calls=%async_computation.3 | async-start | bytes 786432 | tf_op jit(solution)/shard_map/all_to_all | solution.py:802
  89.6 26.7 %collective-permute-start.4 = (f32[2,384,128]{2,1,0:T(8,128)}, f32[2,384,128]{2,1,0:T(8,128)S(1)}, u32[]{:S(2)}, u32[]{:S(2)}) collective-permute-start(f32[2,384,128]{2,1,0:T(8,128)} %get-tuple-element.30), channel_id=1, source_target_pairs={{0,8},{8,16},{16,24},{1,9},{9,17},{17,25},{2,10},{10,18},{18,26},{... | collective-permute-start | bytes 1179656 | tf_op jit(solution)/shard_map/ppermute | solution.py:32
  93.4 22.9 %collective-permute-start.5 = (f32[2,384,128]{2,1,0:T(8,128)S(1)}, f32[2,384,128]{2,1,0:T(8,128)S(1)}, u32[]{:S(2)}, u32[]{:S(2)}) collective-permute-start(f32[2,384,128]{2,1,0:T(8,128)S(1)} %copy-done.8), channel_id=1, source_target_pairs={{8,0},{16,8},{24,16},{9,1},{17,9},{25,17},{10,2},{18,10},{26,18},{... | collective-permute-start | bytes 1179656 | tf_op jit(solution)/shard_map/ppermute | solution.py:32
  96.0 5.8 %copy-start = (bf16[16,256,2048]{2,1,0:T(8,128)(2,1)S(1)}, bf16[16,256,2048]{2,1,0:T(8,128)(2,1)}, u32[]{:S(2)}) copy-start(bf16[16,256,2048]{2,1,0:T(8,128)(2,1)} %weights_hbm.3) | copy-start | bytes 50331652
  108.6 21.2 %all-to-all-start.4 = ((f32[16,16,256]{2,1,0:T(8,128)}), f32[16,16,256]{2,1,0:T(8,128)S(1)}, u32[]{:S(2)}, u32[]{:S(2)}) async-start(f32[16,16,256]{2,1,0:T(8,128)} %probe_rows.1), calls=%async_computation.4 | async-start | bytes 524288 | tf_op jit(solution)/shard_map/all_to_all | solution.py:816
  129.9 1.6 %collective-permute-start.6 = (f32[256,256]{1,0:T(8,128)S(1)}, f32[256,256]{1,0:T(8,128)S(1)}, u32[]{:S(2)}, u32[]{:S(2)}) collective-permute-start(f32[256,256]{1,0:T(8,128)S(1)} %bitcast.22), channel_id=1, source_target_pairs={{0,4},{4,0},{1,5},{5,1},{2,6},{6,2},{3,7},{7,3},{8,12},{12,8},{9,1... | collective-permute-start | bytes 786440 | tf_op jit(solution)/shard_map/ppermute | solution.py:733

commit v3 on v2

--- a/solution.py
+++ b/solution.py
@@ -9,16 +9,14 @@
 from jax.experimental.pallas import tpu as pltpu
 from jax.sharding import PartitionSpec as P
 
-MIB = 1024 * 1024
+VMEM_LIMIT = 60 * 1024 * 1024
 VMEM = pltpu.VMEM
 F32 = jnp.float32
 BF16 = jnp.bfloat16
 LANES = 128
 SUBLANES = 8
-ENERGY_ROWS = 8
 AHEAD = 6
 ANYWHERE = pl.BlockSpec(memory_space=pl.ANY)
-IN_HBM = pl.BlockSpec(memory_space=pltpu.HBM)
 WHOLE = pl.BlockSpec(memory_space=pltpu.VMEM)
 SCALARS = pl.BlockSpec(memory_space=pltpu.SMEM)
 DMA = pltpu.SemaphoreType.DMA
@@ -155,8 +153,8 @@
     share = width // parts
     return pl.pallas_call(
         forward_kernel,
-        in_specs=[SCALARS] + [IN_HBM] * 3,
-        out_specs=IN_HBM,
+        in_specs=[SCALARS] + [ANYWHERE] * 3,
+        out_specs=ANYWHERE,
         out_shape=jax.ShapeDtypeStruct((parts, projections, depth, share), F32),
         scratch_shapes=[
             VMEM(ray_weights.shape, F32),
@@ -170,7 +168,7 @@
             pltpu.SemaphoreType.DMA((projections,)),
             pltpu.SemaphoreType.DMA((projections,)),
         ],
-        compiler_params=pltpu.CompilerParams(vmem_limit_bytes=44 * MIB),
+        compiler_params=pltpu.CompilerParams(vmem_limit_bytes=VMEM_LIMIT),
         cost_estimate=pl.CostEstimate(
             flops=4 * depth * rows * width * lanes,
             bytes_accessed=depth * rows * width * 4 + projections * rows * width * 2,
@@ -192,7 +190,6 @@
     rows_ref,
     cols_ref,
     count_ref,
-    place_ref,
     own_hbm,
     left_hbm,
     right_hbm,
@@ -205,38 +202,34 @@
     edge_left_hbm,
     edge_right_hbm,
     slab_hbm,
-    *rest,
+    parts_hbm,
+    probe_ref,
+    amp_ref,
+    dft_a_ref,
+    dft_b_ref,
+    dual_ref,
+    new_ref,
+    edge_left_ref,
+    edge_right_ref,
+    slab_ref,
+    parts_ref,
+    ext_ref,
+    sum_ref,
+    grad_ref,
+    energy_ref,
+    patch_a_ref,
+    patch_b_ref,
+    wave_a_ref,
+    wave_b_ref,
+    half_a_ref,
+    half_b_ref,
+    far_a_ref,
+    far_b_ref,
+    in_sem,
+    slab_sem,
+    parts_sem,
+    out_sem,
 ):
-    shares = len(rest) - 26
-    parts_hbm = rest[:shares]
-    (
-        probe_ref,
-        amp_ref,
-        dft_a_ref,
-        dft_b_ref,
-        dual_ref,
-        new_ref,
-        edge_left_ref,
-        edge_right_ref,
-        slab_ref,
-        parts_ref,
-        ext_ref,
-        sum_ref,
-        grad_ref,
-        energy_ref,
-        patch_a_ref,
-        patch_b_ref,
-        wave_a_ref,
-        wave_b_ref,
-        half_a_ref,
-        half_b_ref,
-        far_a_ref,
-        far_b_ref,
-        in_sem,
-        slab_sem,
-        parts_sem,
-        out_sem,
-    ) = rest[shares:]
     slots = amp_ref.shape[0]
     side = probe_ref.shape[1]
     _, height, margin = edge_left_ref.shape
@@ -244,8 +237,6 @@
     window = side + LANES
     chunk = 32
     tall = chunk + SUBLANES
-    grad_rows = grad_ref.shape[1]
-    extent = ext_ref.shape[2]
     inner = pl.ds(0, height)
 
     copies = [
@@ -344,12 +335,8 @@
                 o_im = p_re * b_im - p_im * b_re
                 sum_ref[0, cells, pl.ds(base, window)] += placed(o_re, notch, lane)
                 sum_ref[1, cells, pl.ds(base, window)] += placed(o_im, notch, lane)
-                at = r % grad_rows
-                part = r // grad_rows
-                rows = slice(at, at + chunk)
-                grad_ref[part, rows, :] += x_re * b_re + x_im * b_im
-                part += side // grad_rows
-                grad_ref[part, rows, :] += x_re * b_im - x_im * b_re
+                grad_ref[here, :] += x_re * b_re + x_im * b_im
+                grad_ref[below, :] += x_re * b_im - x_im * b_re
         return carry
 
     lax.fori_loop(0, lax.div(count_ref[0] + 1, 2), pair_step, 0)
@@ -384,15 +371,20 @@
             slab_ref[p, layer, :, share:] = outgoing
     slab_copy = pltpu.make_async_copy(slab_ref, slab_hbm, slab_sem)
     slab_copy.start()
-    part_copies = []
-    for step in range(shares):
-        part = lax.rem(place_ref[0] + step, shares)
-        parts_ref[step, :grad_rows, :] = grad_ref[part]
-        parts_ref[step, grad_rows:, :] = energy_ref[...]
-        part_copies.append(
-            pltpu.make_async_copy(parts_ref.at[step], parts_hbm[step], parts_sem.at[step])
-        )
-        part_copies[-1].start()
+    receivers, part_rows, _ = parts_ref.shape
+    blocks = side // LANES
+    taken = (part_rows - SUBLANES) // blocks
+    energy = energy_ref[:, :LANES]
+    for block in range(1, blocks):
+        energy = energy + energy_ref[:, block * LANES : (block + 1) * LANES]
+    for k in range(receivers):
+        for block in range(blocks):
+            parts_ref[k, block * taken : (block + 1) * taken, :] = grad_ref[
+                k * taken : (k + 1) * taken, block * LANES : (block + 1) * LANES
+            ]
+        parts_ref[k, blocks * taken :, :] = energy
+    parts_copy = pltpu.make_async_copy(parts_ref, parts_hbm, parts_sem)
+    parts_copy.start()
     for c in range(2):
         new_ref[c] = ext_ref[c, inner, mid] + sum_ref[c, inner, mid] * wide
         edge_left_ref[c] = sum_ref[c, inner, :margin] * scale
@@ -410,12 +402,13 @@
     for copy in last_copies:
         copy.start()
     slab_copy.wait()
-    for copy in part_copies + last_copies:
+    parts_copy.wait()
+    for copy in last_copies:
         copy.wait()
 
 
 def patch_updates(
-    rows, cols, count, place, own, left, right, probe, amplitudes, dual, shares, layers
+    rows, cols, count, own, left, right, probe, amplitudes, dual, shares, layers, receivers
 ):
     side = probe.shape[1]
     _, height, tile_cols = own.shape
@@ -428,18 +421,18 @@
     extent = tile_cols + 2 * margin + LANES
     shape = jax.ShapeDtypeStruct
     slab_shape = (shares, layers, slab_rows // layers, share + edge)
-    part_rows = 2 * side // shares
+    part_shape = (receivers, 2 * side // receivers * (side // LANES) + SUBLANES, LANES)
     return pl.pallas_call(
         patch_kernel,
-        in_specs=[SCALARS] * 4 + [IN_HBM, ANYWHERE, ANYWHERE] + [IN_HBM] * 5,
-        out_specs=[IN_HBM] * (4 + shares),
+        in_specs=[SCALARS] * 3 + [ANYWHERE] * 8,
+        out_specs=[ANYWHERE] * 5,
         out_shape=[
             shape((2, height, tile_cols), F32),
             shape((2, height, margin), F32),
             shape((2, height, margin), F32),
             shape(slab_shape, F32),
-        ]
-        + [shape((part_rows + ENERGY_ROWS, side), F32)] * shares,
+            shape(part_shape, F32),
+        ],
         scratch_shapes=[
             VMEM(probe.shape, F32),
             VMEM(amplitudes.shape, BF16),
@@ -450,11 +443,11 @@
             VMEM((2, height, margin), F32),
             VMEM((2, height, margin), F32),
             VMEM(slab_shape, F32),
-            VMEM((shares, part_rows + ENERGY_ROWS, side), F32),
+            VMEM(part_shape, F32),
             VMEM((2, height + SUBLANES, extent), F32),
             VMEM((2, height + SUBLANES, extent), F32),
-            VMEM((shares, part_rows, side), F32),
-            VMEM((ENERGY_ROWS, side), F32),
+            VMEM((2 * side, side), F32),
+            VMEM((SUBLANES, side), F32),
             VMEM((2 * side, side), F32),
             VMEM((2 * side, side), F32),
             VMEM((2 * side, side), BF16),
@@ -465,10 +458,10 @@
             VMEM((side, 2 * side), F32),
             pltpu.SemaphoreType.DMA((8,)),
             DMA,
-            pltpu.SemaphoreType.DMA((shares,)),
+            DMA,
             pltpu.SemaphoreType.DMA((3,)),
         ],
-        compiler_params=pltpu.CompilerParams(vmem_limit_bytes=32 * MIB),
+        compiler_params=pltpu.CompilerParams(vmem_limit_bytes=VMEM_LIMIT),
         cost_estimate=pl.CostEstimate(
             flops=slots * 32 * side**3,
             bytes_accessed=8 * height * tile_cols * 4,
@@ -479,7 +472,6 @@
         rows,
         cols,
         count,
-        place,
         own,
         left,
         right,
@@ -527,7 +519,7 @@
     _, projections, depth, _ = residual.shape
     return pl.pallas_call(
         backward_kernel,
-        in_specs=[SCALARS, ANYWHERE, IN_HBM],
+        in_specs=[SCALARS, ANYWHERE, ANYWHERE],
         out_specs=WHOLE,
         out_shape=jax.ShapeDtypeStruct((rows, projections * depth), F32),
         scratch_shapes=[
@@ -537,7 +529,7 @@
             DMA,
             pltpu.SemaphoreType.DMA((projections,)),
         ],
-        compiler_params=pltpu.CompilerParams(vmem_limit_bytes=32 * MIB),
+        compiler_params=pltpu.CompilerParams(vmem_limit_bytes=VMEM_LIMIT),
         cost_estimate=pl.CostEstimate(
             flops=2 * rows * width * projections * projections * depth,
             bytes_accessed=projections * rows * width * 2,
@@ -642,8 +634,8 @@
     slots = min(4, depth)
     return pl.pallas_call(
         update_kernel,
-        in_specs=[SCALARS, WHOLE] + [IN_HBM] * 3 + [ANYWHERE] * 2,
-        out_specs=[IN_HBM] * 2,
+        in_specs=[SCALARS, WHOLE] + [ANYWHERE] * 3 + [ANYWHERE] * 2,
+        out_specs=[ANYWHERE] * 2,
         out_shape=[
             jax.ShapeDtypeStruct(volume.shape, F32),
             jax.ShapeDtypeStruct(partial_object.shape, F32),
@@ -662,7 +654,7 @@
             pltpu.SemaphoreType.DMA((slots,)),
             pltpu.SemaphoreType.DMA((3,)),
         ],
-        compiler_params=pltpu.CompilerParams(vmem_limit_bytes=48 * MIB),
+        compiler_params=pltpu.CompilerParams(vmem_limit_bytes=VMEM_LIMIT),
         cost_estimate=pl.CostEstimate(
             flops=8 * rows * width * sums.shape[1] * depth,
             bytes_accessed=2 * depth * rows * width * 4,
@@ -672,65 +664,35 @@
     )(angle_ids, sums, rays, volume, partial_object, from_left, from_right)
 
 
-def gather_parts_kernel(group, *refs):
-    *given, out_hbm, out_ref, sem = refs
-    total = given[0][...]
-    for ref in given[1:]:
-        total = total + ref[...]
-    _, rows, _ = out_ref.shape
-    rows -= ENERGY_ROWS
+def probe_rows_kernel(given_ref, out_hbm, out_ref, sem):
+    group, rows, _ = given_ref.shape
+    taken, side = out_ref.shape[1:]
+    total = given_ref[0]
+    for k in range(1, group):
+        total = total + given_ref[k]
+    energy = jnp.sum(total[rows - SUBLANES :], keepdims=True) / (side * side)
+    steps = total[: rows - SUBLANES] / (energy + 1e-05)
+    steps = jnp.concatenate(
+        [steps[k * taken : (k + 1) * taken] for k in range(side // LANES)], axis=1
+    )
     for k in range(group):
-        out_ref[k, :rows, :] = total[k * rows : (k + 1) * rows]
-        out_ref[k, rows:, :] = total[group * rows :]
+        out_ref[k] = steps
     copy = pltpu.make_async_copy(out_ref, out_hbm, sem)
     copy.start()
     copy.wait()
 
 
-def gather_parts(given, group):
-    total_rows, side = given[0].shape
-    rows = (total_rows - ENERGY_ROWS) // group + ENERGY_ROWS
-    return pl.pallas_call(
-        functools.partial(gather_parts_kernel, group),
-        in_specs=[WHOLE] * len(given),
-        out_specs=IN_HBM,
-        out_shape=jax.ShapeDtypeStruct((group, rows, side), F32),
-        scratch_shapes=[VMEM((group, rows, side), F32), DMA],
-        name="probe_parts",
-    )(*given)
-
-
-def probe_rows_kernel(given_ref, probe_ref, out_hbm, out_ref, sem):
-    group, rows, side = given_ref.shape
-    rows -= ENERGY_ROWS
-    total = given_ref[0]
-    for k in range(1, group):
-        total = total + given_ref[k]
-    energy = jnp.sum(total[rows:], keepdims=True) / (side * side)
-    new_rows = probe_ref[...] + total[:rows] / (energy + 1e-05)
-    for k in range(group):
-        out_ref[k] = new_rows
-    copy = pltpu.make_async_copy(out_ref, out_hbm, sem)
-    copy.start()
-    copy.wait()
-
-
-def probe_rows(given, own_rows):
-    group, rows, side = given.shape
-    shape = (group, rows - ENERGY_ROWS, side)
+def probe_rows(given, side):
+    group, rows, _ = given.shape
+    shape = (group, (rows - SUBLANES) * LANES // side, side)
     return pl.pallas_call(
         probe_rows_kernel,
-        in_specs=[WHOLE] * 2,
-        out_specs=IN_HBM,
+        in_specs=[WHOLE],
+        out_specs=ANYWHERE,
         out_shape=jax.ShapeDtypeStruct(shape, F32),
         scratch_shapes=[VMEM(shape, F32), DMA],
         name="probe_rows",
-    )(given, own_rows)
-
-
-def turned(value, axis, steps):
-    count = lax.axis_size(axis)
-    return lax.ppermute(value, axis, [(k, (k + steps) % count) for k in range(count)])
+    )(given)
 
 
 def on_device(
@@ -756,13 +718,14 @@
     from_left = shifted(own[:, :, tile_cols - margin :], "tile", 1)
     from_right = shifted(own[:, :, :margin], "tile", -1)
     forward = forward_parts(angle_ids, volume, proj_weights, ray_weights, plane)
+    forward, from_left, from_right = lax.optimization_barrier((forward, from_left, from_right))
     arrived = lax.all_to_all(forward, flat_axes, 0, 0, tiled=True)
     place = lax.axis_index("proj")
-    partial_object, edge_left, edge_right, slab, *grad_parts = patch_updates(
+    everyone = ("proj", "tile", "cuts")
+    partial_object, edge_left, edge_right, slab, grad_parts = patch_updates(
         pos_rows[0, 0],
         pos_cols[0, 0],
         counts[0],
-        place[None],
         own,
         from_left,
         from_right,
@@ -771,11 +734,13 @@
         admm_dual[0],
         proj_count,
         layers,
+        plane * layers,
     )
 
     share = tile_cols // proj_count
     edge = slab.shape[3] - share
     holders = margin // edge
+    slab, arrived = lax.optimization_barrier((slab, arrived))
     pieces = slab.reshape(proj_count * layers, *slab.shape[2:])
     pieces = lax.all_to_all(pieces, ("proj", "cuts"), 0, 0, tiled=True)
     pairs = []
@@ -791,15 +756,9 @@
     residual = (jnp.sum(arrived, axis=0) - target).astype(BF16)
     copies = jnp.broadcast_to(residual[None], (plane, *residual.shape))
 
-    group_axes = ("tile", "cuts")
-    group = lax.axis_size("tile") * layers
-    given = [grad_parts[0]]
-    for step in range(1, proj_count):
-        given.append(turned(grad_parts[step], "proj", step))
-    by_receiver = gather_parts(given, group)
-    copies, by_receiver = lax.optimization_barrier((copies, by_receiver))
+    copies, grad_parts = lax.optimization_barrier((copies, grad_parts))
     residual = lax.all_to_all(copies, flat_axes, 0, 0, tiled=True)
-    received = lax.all_to_all(by_receiver, group_axes, 0, 0, tiled=True)
+    received = lax.all_to_all(grad_parts, everyone, 0, 0, tiled=True)
 
     residual, edge_left, edge_right = lax.optimization_barrier((residual, edge_left, edge_right))
     edge_from_right = shifted(edge_left, "tile", -1)
@@ -807,14 +766,8 @@
     back_sums = backward_sums(angle_ids, residual, proj_weights)
 
     back_sums, received = lax.optimization_barrier((back_sums, received))
-    side = probe_field.shape[1]
-    rows = received.shape[1] - ENERGY_ROWS
-    begin = (place * group + lax.axis_index(group_axes)) * rows
-    own_rows = lax.dynamic_slice(
-        probe_field.reshape(2 * side, side), (begin, jnp.zeros((), begin.dtype)), (rows, side)
-    )
-    new_rows = lax.all_to_all(probe_rows(received, own_rows), group_axes, 0, 0, tiled=True)
-
+    steps = probe_rows(received, probe_field.shape[1])
+    steps = lax.all_to_all(steps, everyone, 0, 0, tiled=True)
     new_volume, new_object = volume_update(
         angle_ids,
         back_sums,
@@ -824,17 +777,8 @@
         edge_from_left,
         edge_from_right,
     )
-    new_volume, new_rows = lax.optimization_barrier((new_volume, new_rows))
-    new_rows = new_rows.reshape(group * rows, side)
-    if proj_count == 2:
-        other = turned(new_rows, "proj", 1)
-        first = place == 0
-        new_probe = jnp.concatenate(
-            [jnp.where(first, new_rows, other), jnp.where(first, other, new_rows)], axis=0
-        )
-    else:
-        new_probe = lax.all_gather(new_rows, "proj", axis=0, tiled=True)
-    return (new_object[None], new_probe.reshape(2, side, side), new_volume)
+    new_probe = probe_field + steps.reshape(probe_field.shape)
+    return (new_object[None], new_probe, new_volume)
 
 
 def solution(mesh):

time: 133 us -> 136 us (1.023)
  blocking collectives: 9.35 us -> 30.2 us
  starting transfers between devices: 44.1 us -> 23.3 us
  local copies, waits for them, and re-layouts: 19.8 us -> 2.81 us
  waiting for transfers between devices: 17.4 us -> 33.4 us
  Pallas kernels: 39.1 us -> 44.3 us
    all_to_all x3 -> x2, starting transfers between devices: 21.2 us -> 5.24 us  [the longest x1 2.62 us: on_device(): steps = lax.all_to_all(steps, everyone, 0, 0, tiled=True)]
    unnamed x42 -> x16, local copies, waits for them, and re-layouts: 17.2 us -> 1.61 us
    ppermute x4, waiting for transfers between devices: 7.33 us -> 21.4 us  [shifted(): lax.ppermute(value, axis, [(source, source + steps) for source in range(l...]
    all_to_all x0 -> x1, blocking collectives: none -> 12.5 us  [on_device(): pieces = lax.all_to_all(pieces, ('proj', 'cuts'), 0, 0, tiled=True)]
    all_to_all x3 -> x2, waiting for transfers between devices: 0.01 us -> 10.6 us  [the longest x1 10.6 us: on_device(): received = lax.all_to_all(grad_parts, everyone, 0, 0, tiled=True)]
    all_to_all x1, blocking collectives: 9.35 us -> 17.8 us  [on_device(): residual = lax.all_to_all(copies, flat_axes, 0, 0, tiled=True)]
    all_to_all x1, waiting for transfers between devices: 8.56 us -> 1.38 us  [on_device(): arrived = lax.all_to_all(forward, flat_axes, 0, 0, tiled=True)]
    pallas_call x6 -> x5, Pallas kernels: 39.1 us -> 44.3 us  [the longest x1 13.7 us: forward_parts(): pl.pallas_call(forward_kernel, in_specs=[SCALARS] + [ANYWHERE] * 3, out_s...]
  transfers between devices with their start and end apart: 11 -> 8, of which waited for: 3 -> 4; matrix products, arithmetic and copies ran while one was open for 1% -> 0% of each run, Pallas kernels for 24% -> 31%
where the time goes in v3:
time: 136 us
  Pallas kernels  44.3 us (33%)
  waiting for transfers between devices  33.4 us (25%)
  blocking collectives  30.2 us (22%)
  starting transfers between devices  23.3 us (17%)
  local copies, waits for them, and re-layouts  2.81 us (2%)
  between operations  1.52 us (1%)
    ppermute x4, waiting for transfers between devices, shifted(): lax.ppermute(value, axis, [(source, source + steps) for source in range(l...  21.4 us
    all_to_all x1, blocking collectives, on_device(): residual = lax.all_to_all(copies, flat_axes, 0, 0, tiled=True)  17.8 us
    pallas_call x1, Pallas kernels, forward_parts(): pl.pallas_call(forward_kernel, in_specs=[SCALARS] + [ANYWHERE] * 3, out_s...  13.7 us
    pallas_call x1, Pallas kernels, volume_update(): pl.pallas_call(update_kernel, in_specs=[SCALARS, WHOLE] + [ANYWHERE] * 3...  12.7 us
    all_to_all x1, blocking collectives, on_device(): pieces = lax.all_to_all(pieces, ('proj', 'cuts'), 0, 0, tiled=True)  12.5 us
    ppermute x4, starting transfers between devices, shifted(): lax.ppermute(value, axis, [(source, source + steps) for source in range(l...  11.6 us
    all_to_all x1, waiting for transfers between devices, on_device(): received = lax.all_to_all(grad_parts, everyone, 0, 0, tiled=True)  10.6 us
    pallas_call x1, Pallas kernels, backward_sums(): pl.pallas_call(backward_kernel, in_specs=[SCALARS, ANYWHERE, ANYWHERE], o...  8.16 us
  transfers between devices with their start and end apart: 8, of which 4 were waited for; matrix products, arithmetic and copies ran while one was open for 0% of the time, Pallas kernels for 31%

profile of v3, /device:TPU:0, one launch (start us, length us, event | category | flops | bytes accessed | tf_op | source)
XLA Modules:
  0.0 136.5 jit_solution(2188232374688319322)
XLA Ops:
  0.6 1.2 fusion.2
  1.8 1.3 collective-permute-start.1
  3.1 5.5 %collective-permute-start = (f32[2,384,128]{2,1,0:T(8,128)S(1)}, f32[2,384,128]{2,1,0:T(8,128)S(1)}, u32[]{:S(2)}, u32[]{:S(2)}) collective-permute-start(f32[2,384,128]{2,1,0:T(8,128)S(1)} %get-tuple-element.42), channel_id=1, source_target_pairs={{0,8},{8,16},{16,24},{1,9},{9,17},{17,25},{2,10},{10,18},{18,26},{... | collective-permute-start | bytes 1179656 | tf_op jit(solution)/shard_map/ppermute | solution.py:30
  8.6 13.7 %forward.1 = f32[8,8,8,256]{3,2,1,0:T(8,128)} custom-call(s32[8]{0:T(128)} %ids_ref.5, f32[16,2048]{1,0:T(8,128)} %rays_hbm.3, f32[8,256,2048]{2,1,0:T(8,128)} %volume_hbm.3, bf16[16,256,2048]{2,1,0:T(8,128)(2,1)} %weights_hbm.3), custom_call_target="tpu_custom_call" | custom-call | flops 2147483648 | bytes 25165824 | tf_op jit(solution)/shard_map/forward/pallas_call | solution.py:154
  22.3 0.0 collective-permute-done.1.right_hbm
  22.3 0.0 copy-start.6
  22.3 0.0 collective-permute-done.left_hbm
  22.3 0.0 copy-start.7
  22.4 5.7 %all-to-all-start = ((f32[8,8,8,256]{3,2,1,0:T(8,128)}), f32[8,8,8,256]{3,2,1,0:T(8,128)S(1)}, u32[]{:S(2)}, u32[]{:S(2)}) async-start(f32[8,8,8,256]{3,2,1,0:T(8,128)} %forward.1), calls=%async_computation | async-start | bytes 1048576 | tf_op jit(solution)/shard_map/all_to_all | solution.py:722
  28.8 0.0 copy-done.6
  28.8 0.0 copy-done.7
  28.8 7.7 %patches.1 = (f32[2,384,512]{2,1,0:T(8,128)}, f32[2,384,128]{2,1,0:T(8,128)}, f32[2,384,128]{2,1,0:T(8,128)}, f32[2,4,8,384]{3,2,1,0:T(8,128)}, f32[32,40,128]{2,1,0:T(8,128)}) custom-call(s32[6]{0:T(128)} %bitcast.19, s32[6]{0:T(128)} %bitcast.20, s32[1]{0:T(128)} %bitcast.11.count_ref, f32[2,384,512]{2,1,0:T(8,128)} %bitcast.14, f32[2,384,128]{2,1,0:T(8,128)} %copy-done.7, ...), custom_call_target="tpu_custom_call" | custom-call | flops 3221225472 | bytes 6291456 | tf_op jit(solution)/shard_map/patches/pallas_call | solution.py:425
  36.5 1.4 %all-to-all-done = f32[8,8,8,256]{3,2,1,0:T(8,128)S(1)} async-done(((f32[8,8,8,256]{3,2,1,0:T(8,128)}), f32[8,8,8,256]{3,2,1,0:T(8,128)S(1)}, u32[]{:S(2)}, u32[]{:S(2)}) %all-to-all-start) | async-done | bytes 524320 | tf_op jit(solution)/shard_map/all_to_all | solution.py:722
  37.8 12.5 %all_to_all.25 = f32[8,8,384]{2,1,0:T(8,128)S(1)} all-to-all(f32[8,8,384]{2,1,0:T(8,128)} %bitcast.15), channel_id=1, replica_groups=mesh['tile'=4,'proj'=2,'cuts'=4] {'proj','cuts'}, dimensions={0} | all-to-all | bytes 196608 | tf_op jit(solution)/shard_map/all_to_all | solution.py:745
  50.3 0.7 collective-permute-start.2
  51.0 0.0 collective-permute-done.2
  51.1 17.8 %all_to_all.26.residual_hbm = bf16[8,8,8,256]{3,2,1,0:T(8,128)(2,1)} all-to-all(bf16[8,8,8,256]{3,2,1,0:T(8,128)(2,1)S(1)} %broadcast_in_dim.4), channel_id=1, replica_groups=mesh['tile'=4,'proj'=2,'cuts'=4] {'tile','proj'}, dimensions={0} | all-to-all | bytes 524288 | tf_op jit(solution)/shard_map/all_to_all | solution.py:760
  68.9 2.6 %all-to-all-start.3 = ((f32[32,40,128]{2,1,0:T(8,128)}), f32[32,40,128]{2,1,0:T(8,128)S(1)}, u32[]{:S(2)}, u32[]{:S(2)}) async-start(f32[32,40,128]{2,1,0:T(8,128)} %get-tuple-element.33), calls=%async_computation.3 | async-start | bytes 1310720 | tf_op jit(solution)/shard_map/all_to_all | solution.py:761
  71.5 8.2 %backward.1.sums_ref = f32[256,64]{1,0:T(8,128)} custom-call(s32[8]{0:T(128)} %ids_ref.5, bf16[8,8,8,256]{3,2,1,0:T(8,128)(2,1)} %all_to_all.26.residual_hbm, bf16[16,256,2048]{2,1,0:T(8,128)(2,1)} %weights_hbm.3), custom_call_target="tpu_custom_call" | custom-call | flops 536870912 | bytes 8388608 | tf_op jit(solution)/shard_map/backward/pallas_call | solution.py:520
  79.7 0.0 copy-start.5
  79.7 0.0 copy-start.4
  79.7 10.6 %all-to-all-done.3.given_ref = f32[32,40,128]{2,1,0:T(8,128)S(1)} async-done(((f32[32,40,128]{2,1,0:T(8,128)}), f32[32,40,128]{2,1,0:T(8,128)S(1)}, u32[]{:S(2)}, u32[]{:S(2)}) %all-to-all-start.3) | async-done | bytes 655392 | tf_op jit(solution)/shard_map/all_to_all | solution.py:761
  90.3 0.0 copy-start
  90.3 0.8 copy-done
  91.1 2.1 %probe_rows.1 = f32[32,16,256]{2,1,0:T(8,128)} custom-call(f32[32,40,128]{2,1,0:T(8,128)} %copy-done), custom_call_target="tpu_custom_call" | custom-call | tf_op jit(solution)/shard_map/probe_rows/pallas_call | solution.py:688
  93.2 2.6 %all-to-all-start.4 = ((f32[32,16,256]{2,1,0:T(8,128)}), f32[32,16,256]{2,1,0:T(8,128)S(1)}, u32[]{:S(2)}, u32[]{:S(2)}) async-start(f32[32,16,256]{2,1,0:T(8,128)} %probe_rows.1), calls=%async_computation.4 | async-start | bytes 1048576 | tf_op jit(solution)/shard_map/all_to_all | solution.py:770
  95.8 0.0 copy-done.5
  95.8 3.6 %collective-permute-start.3 = (f32[2,384,128]{2,1,0:T(8,128)S(1)}, f32[2,384,128]{2,1,0:T(8,128)S(1)}, u32[]{:S(2)}, u32[]{:S(2)}) collective-permute-start(f32[2,384,128]{2,1,0:T(8,128)S(1)} %copy-done.5), channel_id=1, source_target_pairs={{0,8},{8,16},{16,24},{1,9},{9,17},{17,25},{2,10},{10,18},{18,26},{... | collective-permute-start | bytes 1179656 | tf_op jit(solution)/shard_map/ppermute | solution.py:30
  99.4 0.0 copy-done.4
  99.4 1.3 collective-permute-start.4
  100.7 10.5 %collective-permute-done.3.from_left_hbm = f32[2,384,128]{2,1,0:T(8,128)S(1)} collective-permute-done((f32[2,384,128]{2,1,0:T(8,128)S(1)}, f32[2,384,128]{2,1,0:T(8,128)S(1)}, u32[]{:S(2)}, u32[]{:S(2)}) %collective-permute-start.3) | collective-permute-done | bytes 393248 | tf_op jit(solution)/shard_map/ppermute | solution.py:30
  111.2 0.0 copy-start.2
  111.2 10.9 %collective-permute-done.4.from_right_hbm = f32[2,384,128]{2,1,0:T(8,128)S(1)} collective-permute-done((f32[2,384,128]{2,1,0:T(8,128)S(1)}, f32[2,384,128]{2,1,0:T(8,128)S(1)}, u32[]{:S(2)}, u32[]{:S(2)}) %collective-permute-start.4) | collective-permute-done | bytes 393248 | tf_op jit(solution)/shard_map/ppermute | solution.py:30
  122.2 0.0 copy-start.3
  122.2 0.0 copy-done.2
  122.2 0.7 copy-done.3
  122.9 0.0 copy-start.1
  122.9 12.7 %update.1 = (f32[8,256,2048]{2,1,0:T(8,128)}, f32[2,384,512]{2,1,0:T(8,128)}) custom-call(s32[8]{0:T(128)} %ids_ref.5, f32[256,64]{1,0:T(8,128)} %backward.1.sums_ref, f32[16,2048]{1,0:T(8,128)} %rays_hbm.3, f32[8,256,2048]{2,1,0:T(8,128)} %volume_hbm.3, f32[2,384,512]{2,1,0:T(8,128)} %get-tuple-element.35.object_hbm, f32[2,384,128]{2,1,0:T(8,128)} %copy-done.2, ...), custom_call_target="tpu_custom_call" | custom-call | flops 2147483648 | bytes 33554432 | tf_op jit(solution)/shard_map/update/pallas_call | solution.py:635
  135.6 0.0 all-to-all-done.4
  135.6 0.0 copy-done.1
  135.6 0.9 bitcast_add_fusion
  (4 shorter events, 0.1 us)
Async XLA Ops:
  1.8 20.5 %collective-permute-start.1 = (f32[2,384,128]{2,1,0:T(8,128)S(1)}, f32[2,384,128]{2,1,0:T(8,128)S(1)}, u32[]{:S(2)}, u32[]{:S(2)}) collective-permute-start(f32[2,384,128]{2,1,0:T(8,128)S(1)} %get-tuple-element.41), channel_id=1, source_target_pairs={{8,0},{16,8},{24,16},{9,1},{17,9},{25,17},{10,2},{18,10},{26,18},{... | collective-permute-start | bytes 1179656 | tf_op jit(solution)/shard_map/ppermute | solution.py:30
  3.1 19.2 %collective-permute-start = (f32[2,384,128]{2,1,0:T(8,128)S(1)}, f32[2,384,128]{2,1,0:T(8,128)S(1)}, u32[]{:S(2)}, u32[]{:S(2)}) collective-permute-start(f32[2,384,128]{2,1,0:T(8,128)S(1)} %get-tuple-element.42), channel_id=1, source_target_pairs={{0,8},{8,16},{16,24},{1,9},{9,17},{17,25},{2,10},{10,18},{18,26},{... | collective-permute-start | bytes 1179656 | tf_op jit(solution)/shard_map/ppermute | solution.py:30
  22.3 6.4 %copy-start.6 = (f32[2,384,128]{2,1,0:T(8,128)}, f32[2,384,128]{2,1,0:T(8,128)S(1)}, u32[]{:S(2)}) copy-start(f32[2,384,128]{2,1,0:T(8,128)S(1)} %collective-permute-done.1.right_hbm) | copy-start | bytes 1179652
  22.3 6.4 %copy-start.7 = (f32[2,384,128]{2,1,0:T(8,128)}, f32[2,384,128]{2,1,0:T(8,128)S(1)}, u32[]{:S(2)}) copy-start(f32[2,384,128]{2,1,0:T(8,128)S(1)} %collective-permute-done.left_hbm) | copy-start | bytes 1179652
  22.4 15.5 %all-to-all-start = ((f32[8,8,8,256]{3,2,1,0:T(8,128)}), f32[8,8,8,256]{3,2,1,0:T(8,128)S(1)}, u32[]{:S(2)}, u32[]{:S(2)}) async-start(f32[8,8,8,256]{3,2,1,0:T(8,128)} %forward.1), calls=%async_computation | async-start | bytes 1048576 | tf_op jit(solution)/shard_map/all_to_all | solution.py:722
  50.3 0.7 collective-permute-start.2
  68.9 21.4 %all-to-all-start.3 = ((f32[32,40,128]{2,1,0:T(8,128)}), f32[32,40,128]{2,1,0:T(8,128)S(1)}, u32[]{:S(2)}, u32[]{:S(2)}) async-start(f32[32,40,128]{2,1,0:T(8,128)} %get-tuple-element.33), calls=%async_computation.3 | async-start | bytes 1310720 | tf_op jit(solution)/shard_map/all_to_all | solution.py:761
  79.7 16.2 %copy-start.5 = (f32[2,384,128]{2,1,0:T(8,128)S(1)}, f32[2,384,128]{2,1,0:T(8,128)}, u32[]{:S(2)}) copy-start(f32[2,384,128]{2,1,0:T(8,128)} %get-tuple-element.36) | copy-start | bytes 1179652
  79.7 19.7 %copy-start.4 = (f32[2,384,128]{2,1,0:T(8,128)S(1)}, f32[2,384,128]{2,1,0:T(8,128)}, u32[]{:S(2)}) copy-start(f32[2,384,128]{2,1,0:T(8,128)} %get-tuple-element.37) | copy-start | bytes 1179652
  90.3 0.8 copy-start
  93.2 42.4 %all-to-all-start.4 = ((f32[32,16,256]{2,1,0:T(8,128)}), f32[32,16,256]{2,1,0:T(8,128)S(1)}, u32[]{:S(2)}, u32[]{:S(2)}) async-start(f32[32,16,256]{2,1,0:T(8,128)} %probe_rows.1), calls=%async_computation.4 | async-start | bytes 1048576 | tf_op jit(solution)/shard_map/all_to_all | solution.py:770
  95.8 15.4 %collective-permute-start.3 = (f32[2,384,128]{2,1,0:T(8,128)S(1)}, f32[2,384,128]{2,1,0:T(8,128)S(1)}, u32[]{:S(2)}, u32[]{:S(2)}) collective-permute-start(f32[2,384,128]{2,1,0:T(8,128)S(1)} %copy-done.5), channel_id=1, source_target_pairs={{0,8},{8,16},{16,24},{1,9},{9,17},{17,25},{2,10},{10,18},{18,26},{... | collective-permute-start | bytes 1179656 | tf_op jit(solution)/shard_map/ppermute | solution.py:30
  99.4 22.7 %collective-permute-start.4 = (f32[2,384,128]{2,1,0:T(8,128)S(1)}, f32[2,384,128]{2,1,0:T(8,128)S(1)}, u32[]{:S(2)}, u32[]{:S(2)}) collective-permute-start(f32[2,384,128]{2,1,0:T(8,128)S(1)} %copy-done.4), channel_id=1, source_target_pairs={{8,0},{16,8},{24,16},{9,1},{17,9},{25,17},{10,2},{18,10},{26,18},{... | collective-permute-start | bytes 1179656 | tf_op jit(solution)/shard_map/ppermute | solution.py:30
  111.2 10.9 %copy-start.2 = (f32[2,384,128]{2,1,0:T(8,128)}, f32[2,384,128]{2,1,0:T(8,128)S(1)}, u32[]{:S(2)}) copy-start(f32[2,384,128]{2,1,0:T(8,128)S(1)} %collective-permute-done.3.from_left_hbm) | copy-start | bytes 1179652
  122.2 0.8 copy-start.3
  122.9 12.7 %copy-start.1 = (f32[2,256,256]{2,1,0:T(8,128)S(1)}, f32[2,256,256]{2,1,0:T(8,128)}, u32[]{:S(2)}) copy-start(f32[2,256,256]{2,1,0:T(8,128)} %probe_hbm.1) | copy-start | bytes 1572868

commit v4 on v2

--- a/solution.py
+++ b/solution.py
@@ -9,16 +9,15 @@
 from jax.experimental.pallas import tpu as pltpu
 from jax.sharding import PartitionSpec as P
 
-MIB = 1024 * 1024
+VMEM_LIMIT = 60 * 1024 * 1024
 VMEM = pltpu.VMEM
 F32 = jnp.float32
 BF16 = jnp.bfloat16
 LANES = 128
 SUBLANES = 8
-ENERGY_ROWS = 8
 AHEAD = 6
+WEIGHTS_AHEAD = 6
 ANYWHERE = pl.BlockSpec(memory_space=pl.ANY)
-IN_HBM = pl.BlockSpec(memory_space=pltpu.HBM)
 WHOLE = pl.BlockSpec(memory_space=pltpu.VMEM)
 SCALARS = pl.BlockSpec(memory_space=pltpu.SMEM)
 DMA = pltpu.SemaphoreType.DMA
@@ -32,16 +31,14 @@
     return lax.ppermute(value, axis, [(source, source + steps) for source in range(leading, last)])
 
 
-def dft_blocks(side):
+def dft_table(side):
     indices = np.arange(side)
     products = (indices[:, None] * indices[None, :]) % side
     phase = products.astype(np.float32) * np.float32(2.0 * math.pi / side)
     norm = np.float32(1.0 / math.sqrt(side))
     real = np.cos(phase).astype(np.float32) * norm
     imag = -np.sin(phase).astype(np.float32) * norm
-    left = np.block([[real, -imag], [imag, real]])
-    right = np.block([[real, imag], [-imag, real]])
-    return left.astype(jnp.bfloat16), right.astype(jnp.bfloat16)
+    return np.stack([real, imag]).astype(jnp.bfloat16)
 
 
 def dot(left, right):
@@ -155,8 +152,8 @@
     share = width // parts
     return pl.pallas_call(
         forward_kernel,
-        in_specs=[SCALARS] + [IN_HBM] * 3,
-        out_specs=IN_HBM,
+        in_specs=[SCALARS] + [ANYWHERE] * 3,
+        out_specs=ANYWHERE,
         out_shape=jax.ShapeDtypeStruct((parts, projections, depth, share), F32),
         scratch_shapes=[
             VMEM(ray_weights.shape, F32),
@@ -170,7 +167,7 @@
             pltpu.SemaphoreType.DMA((projections,)),
             pltpu.SemaphoreType.DMA((projections,)),
         ],
-        compiler_params=pltpu.CompilerParams(vmem_limit_bytes=44 * MIB),
+        compiler_params=pltpu.CompilerParams(vmem_limit_bytes=VMEM_LIMIT),
         cost_estimate=pl.CostEstimate(
             flops=4 * depth * rows * width * lanes,
             bytes_accessed=depth * rows * width * 4 + projections * rows * width * 2,
@@ -198,8 +195,7 @@
     right_hbm,
     probe_hbm,
     amp_hbm,
-    dft_a_hbm,
-    dft_b_hbm,
+    table_hbm,
     dual_hbm,
     new_hbm,
     edge_left_hbm,
@@ -207,11 +203,12 @@
     slab_hbm,
     *rest,
 ):
-    shares = len(rest) - 26
+    shares = len(rest) - 27
     parts_hbm = rest[:shares]
     (
         probe_ref,
         amp_ref,
+        table_ref,
         dft_a_ref,
         dft_b_ref,
         dual_ref,
@@ -224,28 +221,19 @@
         sum_ref,
         grad_ref,
         energy_ref,
-        patch_a_ref,
-        patch_b_ref,
-        wave_a_ref,
-        wave_b_ref,
-        half_a_ref,
-        half_b_ref,
-        far_a_ref,
-        far_b_ref,
+        *chain_refs,
         in_sem,
-        slab_sem,
+        amp_sem,
         parts_sem,
         out_sem,
     ) = rest[shares:]
-    slots = amp_ref.shape[0]
+    chain_refs = [chain_refs[k : k + 4] for k in range(0, len(chain_refs), 4)]
     side = probe_ref.shape[1]
     _, height, margin = edge_left_ref.shape
     tile_cols = new_ref.shape[2]
     window = side + LANES
     chunk = 32
     tall = chunk + SUBLANES
-    grad_rows = grad_ref.shape[1]
-    extent = ext_ref.shape[2]
     inner = pl.ds(0, height)
 
     copies = [
@@ -256,31 +244,44 @@
                 (own_hbm, ext_ref.at[:, inner, pl.ds(margin, tile_cols)]),
                 (right_hbm, ext_ref.at[:, inner, pl.ds(margin + tile_cols, margin)]),
                 (probe_hbm, probe_ref),
-                (dft_a_hbm, dft_a_ref),
-                (dft_b_hbm, dft_b_ref),
-                (amp_hbm, amp_ref),
+                (table_hbm, table_ref),
                 (dual_hbm, dual_ref),
             )
         )
     ]
     for copy in copies:
         copy.start()
+    live_count = count_ref[0]
+
+    def amp_copy(k):
+        return pltpu.make_async_copy(amp_hbm.at[k], amp_ref.at[k], amp_sem.at[k])
+
+    @pl.loop(0, live_count)
+    def _(k):
+        amp_copy(k).start()
+
     sum_ref[...] = jnp.zeros(sum_ref.shape, F32)
     grad_ref[...] = jnp.zeros(grad_ref.shape, F32)
     energy_ref[...] = jnp.zeros(energy_ref.shape, F32)
     for copy in copies:
         copy.wait()
+    real = table_ref[0]
+    imag = table_ref[1]
+    for ref, sign in ((dft_a_ref, -1), (dft_b_ref, 1)):
+        ref[:side, :side] = real
+        ref[side:, side:] = real
+        ref[:side, side:] = sign * imag
+        ref[side:, :side] = -sign * imag
+
+    @pl.loop(0, live_count)
+    def _(k):
+        amp_copy(k).wait()
 
     def pair_step(pair, carry):
         chains = []
-        for k, refs in enumerate(
-            (
-                (patch_a_ref, wave_a_ref, half_a_ref, far_a_ref),
-                (patch_b_ref, wave_b_ref, half_b_ref, far_b_ref),
-            )
-        ):
-            slot = jnp.minimum(2 * pair + k, slots - 1)
-            live = (2 * pair + k < count_ref[0]).astype(F32)
+        for k, refs in enumerate(chain_refs):
+            slot = jnp.minimum(2 * pair + k, live_count - 1)
+            live = (2 * pair + k < live_count).astype(F32)
             row = rows_ref[slot]
             col = cols_ref[slot]
             lane = lax.rem(col, LANES)
@@ -344,15 +345,11 @@
                 o_im = p_re * b_im - p_im * b_re
                 sum_ref[0, cells, pl.ds(base, window)] += placed(o_re, notch, lane)
                 sum_ref[1, cells, pl.ds(base, window)] += placed(o_im, notch, lane)
-                at = r % grad_rows
-                part = r // grad_rows
-                rows = slice(at, at + chunk)
-                grad_ref[part, rows, :] += x_re * b_re + x_im * b_im
-                part += side // grad_rows
-                grad_ref[part, rows, :] += x_re * b_im - x_im * b_re
+                grad_ref[here, :] += x_re * b_re + x_im * b_im
+                grad_ref[below, :] += x_re * b_im - x_im * b_re
         return carry
 
-    lax.fori_loop(0, lax.div(count_ref[0] + 1, 2), pair_step, 0)
+    lax.fori_loop(0, lax.div(live_count + 1, 2), pair_step, 0)
 
     p_re = probe_ref[0]
     p_im = probe_ref[1]
@@ -382,35 +379,28 @@
             else:
                 outgoing = jnp.zeros((depth, edge), F32)
             slab_ref[p, layer, :, share:] = outgoing
-    slab_copy = pltpu.make_async_copy(slab_ref, slab_hbm, slab_sem)
+    slab_copy = pltpu.make_async_copy(slab_ref, slab_hbm, out_sem.at[3])
     slab_copy.start()
-    part_copies = []
+    part_rows = parts_ref.shape[1] - SUBLANES
+    last_copies = [slab_copy]
     for step in range(shares):
-        part = lax.rem(place_ref[0] + step, shares)
-        parts_ref[step, :grad_rows, :] = grad_ref[part]
-        parts_ref[step, grad_rows:, :] = energy_ref[...]
-        part_copies.append(
-            pltpu.make_async_copy(parts_ref.at[step], parts_hbm[step], parts_sem.at[step])
-        )
-        part_copies[-1].start()
+        begin = pl.multiple_of(lax.rem(place_ref[0] + step, shares) * part_rows, SUBLANES)
+        parts_ref[step, :part_rows, :] = grad_ref[pl.ds(begin, part_rows), :]
+        parts_ref[step, part_rows:, :] = energy_ref[...]
+        copy = pltpu.make_async_copy(parts_ref.at[step], parts_hbm[step], parts_sem.at[step])
+        copy.start()
+        last_copies.append(copy)
     for c in range(2):
         new_ref[c] = ext_ref[c, inner, mid] + sum_ref[c, inner, mid] * wide
         edge_left_ref[c] = sum_ref[c, inner, :margin] * scale
         edge_right_ref[c] = sum_ref[c, inner, far_side] * scale
-    last_copies = [
-        pltpu.make_async_copy(source, target, out_sem.at[k])
-        for k, (source, target) in enumerate(
-            (
-                (new_ref, new_hbm),
-                (edge_left_ref, edge_left_hbm),
-                (edge_right_ref, edge_right_hbm),
-            )
-        )
-    ]
+    for k, (source, target) in enumerate(
+        ((new_ref, new_hbm), (edge_left_ref, edge_left_hbm), (edge_right_ref, edge_right_hbm))
+    ):
+        copy = pltpu.make_async_copy(source, target, out_sem.at[k])
+        copy.start()
+        last_copies.append(copy)
     for copy in last_copies:
-        copy.start()
-    slab_copy.wait()
-    for copy in part_copies + last_copies:
         copy.wait()
 
 
@@ -424,51 +414,52 @@
     slab_rows = dual.shape[0]
     share = tile_cols // shares
     edge = min(share, margin)
-    dft_a, dft_b = dft_blocks(side)
+    table = dft_table(side)
     extent = tile_cols + 2 * margin + LANES
     shape = jax.ShapeDtypeStruct
     slab_shape = (shares, layers, slab_rows // layers, share + edge)
-    part_rows = 2 * side // shares
+    part_rows = 2 * side // shares + SUBLANES
+    chain = [
+        VMEM((2 * side, side), F32),
+        VMEM((2 * side, side), BF16),
+        VMEM((side, 2 * side), BF16),
+        VMEM((side, 2 * side), F32),
+    ]
     return pl.pallas_call(
         patch_kernel,
-        in_specs=[SCALARS] * 4 + [IN_HBM, ANYWHERE, ANYWHERE] + [IN_HBM] * 5,
-        out_specs=[IN_HBM] * (4 + shares),
+        in_specs=[SCALARS] * 4 + [ANYWHERE] * 7,
+        out_specs=[ANYWHERE] * (4 + shares),
         out_shape=[
             shape((2, height, tile_cols), F32),
             shape((2, height, margin), F32),
             shape((2, height, margin), F32),
             shape(slab_shape, F32),
         ]
-        + [shape((part_rows + ENERGY_ROWS, side), F32)] * shares,
+        + [shape((part_rows, side), F32)] * shares,
         scratch_shapes=[
             VMEM(probe.shape, F32),
             VMEM(amplitudes.shape, BF16),
-            VMEM(dft_a.shape, BF16),
-            VMEM(dft_b.shape, BF16),
+            VMEM(table.shape, BF16),
+            VMEM((2 * side, 2 * side), BF16),
+            VMEM((2 * side, 2 * side), BF16),
             VMEM(dual.shape, F32),
             VMEM((2, height, tile_cols), F32),
             VMEM((2, height, margin), F32),
             VMEM((2, height, margin), F32),
             VMEM(slab_shape, F32),
-            VMEM((shares, part_rows + ENERGY_ROWS, side), F32),
+            VMEM((shares, part_rows, side), F32),
             VMEM((2, height + SUBLANES, extent), F32),
             VMEM((2, height + SUBLANES, extent), F32),
-            VMEM((shares, part_rows, side), F32),
-            VMEM((ENERGY_ROWS, side), F32),
             VMEM((2 * side, side), F32),
-            VMEM((2 * side, side), F32),
-            VMEM((2 * side, side), BF16),
-            VMEM((2 * side, side), BF16),
-            VMEM((side, 2 * side), BF16),
-            VMEM((side, 2 * side), BF16),
-            VMEM((side, 2 * side), F32),
-            VMEM((side, 2 * side), F32),
-            pltpu.SemaphoreType.DMA((8,)),
-            DMA,
+            VMEM((SUBLANES, side), F32),
+            *chain,
+            *chain,
+            pltpu.SemaphoreType.DMA((6,)),
+            pltpu.SemaphoreType.DMA((slots,)),
             pltpu.SemaphoreType.DMA((shares,)),
-            pltpu.SemaphoreType.DMA((3,)),
+            pltpu.SemaphoreType.DMA((4,)),
         ],
-        compiler_params=pltpu.CompilerParams(vmem_limit_bytes=32 * MIB),
+        compiler_params=pltpu.CompilerParams(vmem_limit_bytes=VMEM_LIMIT),
         cost_estimate=pl.CostEstimate(
             flops=slots * 32 * side**3,
             bytes_accessed=8 * height * tile_cols * 4,
@@ -485,71 +476,15 @@
         right,
         probe,
         amplitudes,
-        jnp.asarray(dft_a),
-        jnp.asarray(dft_b),
+        jnp.asarray(table),
         dual,
     )
 
 
-def backward_kernel(
-    ids_ref, residual_hbm, weights_hbm, out_ref, residual_ref, weights_ref, turned_ref, sem, weights_sem
-):
-    parts, projections, depth, share = residual_ref.shape
-    both = projections * depth
-
-    def weights_copy(a):
-        return pltpu.make_async_copy(
-            weights_hbm.at[ids_ref[a]], weights_ref.at[a], weights_sem.at[a]
-        )
-
-    residual_copy = pltpu.make_async_copy(residual_hbm, residual_ref, sem)
-    residual_copy.start()
-    for a in range(projections):
-        weights_copy(a).start()
-    residual_copy.wait()
-    for part in range(parts):
-        block = residual_ref[part].astype(F32).reshape(both, share)
-        turned_ref[part * share : (part + 1) * share, :] = block.T
-    out_ref[...] = jnp.zeros(out_ref.shape, F32)
-
-    @pl.loop(0, projections)
-    def _(a):
-        weights_copy(a).wait()
-        lane = lax.broadcasted_iota(jnp.int32, turned_ref.shape, 1)
-        begin = a * depth
-        kept = jnp.logical_and(lane >= begin, lane < begin + depth)
-        chosen = jnp.where(kept, turned_ref[...], 0.0).astype(BF16)
-        out_ref[...] += dot(weights_ref[a], chosen)
-
-
-def backward_sums(angle_ids, residual, proj_weights):
-    _, rows, width = proj_weights.shape
-    _, projections, depth, _ = residual.shape
-    return pl.pallas_call(
-        backward_kernel,
-        in_specs=[SCALARS, ANYWHERE, IN_HBM],
-        out_specs=WHOLE,
-        out_shape=jax.ShapeDtypeStruct((rows, projections * depth), F32),
-        scratch_shapes=[
-            VMEM(residual.shape, BF16),
-            VMEM((projections, rows, width), BF16),
-            VMEM((width, projections * depth), F32),
-            DMA,
-            pltpu.SemaphoreType.DMA((projections,)),
-        ],
-        compiler_params=pltpu.CompilerParams(vmem_limit_bytes=32 * MIB),
-        cost_estimate=pl.CostEstimate(
-            flops=2 * rows * width * projections * projections * depth,
-            bytes_accessed=projections * rows * width * 2,
-            transcendentals=0,
-        ),
-        name="backward",
-    )(angle_ids, residual, proj_weights)
-
-
 def update_kernel(
     ids_ref,
-    sums_ref,
+    residual_hbm,
+    weights_hbm,
     rays_hbm,
     volume_hbm,
     object_hbm,
@@ -557,15 +492,20 @@
     from_right_hbm,
     out_hbm,
     new_object_hbm,
+    residual_ref,
+    weights_ref,
     rays_ref,
+    volume_ref,
+    turned_ref,
+    total_ref,
     stack_ref,
     spread_ref,
-    volume_ref,
     done_ref,
     cells_ref,
     left_ref,
     right_ref,
-    rays_sem,
+    small_sem,
+    weights_sem,
     volume_sem,
     out_sem,
     object_sem,
@@ -575,8 +515,13 @@
     margin = left_ref.shape[2]
     tile_cols = cells_ref.shape[2]
     width = rays_ref.shape[1]
-    projections = sums_ref.shape[1] // depth
-    both = sums_ref.shape[1]
+    parts, projections, _, share = residual_ref.shape
+    both = projections * depth
+
+    def weights_copy(a):
+        return pltpu.make_async_copy(
+            weights_hbm.at[ids_ref[a]], weights_ref.at[a], weights_sem.at[a]
+        )
 
     def volume_copy(z):
         return pltpu.make_async_copy(volume_hbm.at[z], volume_ref.at[z], volume_sem.at[z])
@@ -585,20 +530,24 @@
         slot = lax.rem(z, slots)
         return pltpu.make_async_copy(done_ref.at[slot], out_hbm.at[z], out_sem.at[slot])
 
-    rays_copy = pltpu.make_async_copy(rays_hbm, rays_ref, rays_sem)
+    residual_copy = pltpu.make_async_copy(residual_hbm, residual_ref, small_sem.at[0])
+    residual_copy.start()
+    rays_copy = pltpu.make_async_copy(rays_hbm, rays_ref, small_sem.at[1])
     rays_copy.start()
-    for z in range(min(AHEAD, depth)):
-        volume_copy(z).start()
+    for a in range(min(WEIGHTS_AHEAD, projections)):
+        weights_copy(a).start()
     copies = [
         pltpu.make_async_copy(source, target, object_sem.at[k])
         for k, (source, target) in enumerate(
             ((object_hbm, cells_ref), (from_left_hbm, left_ref), (from_right_hbm, right_ref))
         )
     ]
-    for copy in copies:
-        copy.start()
-    high, low = split_bf16(sums_ref[...])
-    stack_ref[...] = jnp.concatenate([high, low, high, low], axis=1)
+
+    residual_copy.wait()
+    for part in range(parts):
+        block = residual_ref[part].astype(F32).reshape(both, share)
+        turned_ref[part * share : (part + 1) * share, :] = block.T
+    total_ref[...] = jnp.zeros(total_ref.shape, F32)
     rays_copy.wait()
     rows = [
         jnp.broadcast_to(rays_ref[pl.ds(ids_ref[a], 1), :], (depth, width))
@@ -608,13 +557,35 @@
     for place, block in enumerate((high, high, low, low)):
         spread_ref[place * both : (place + 1) * both, :] = block.astype(BF16)
 
+    @pl.loop(0, projections)
+    def _(a):
+        @pl.when(a + WEIGHTS_AHEAD < projections)
+        def _():
+            weights_copy(a + WEIGHTS_AHEAD).start()
+
+        z = a + WEIGHTS_AHEAD - projections
+
+        @pl.when(jnp.logical_and(z >= 0, z < depth))
+        def _():
+            volume_copy(z).start()
+
+        weights_copy(a).wait()
+        lane = lax.broadcasted_iota(jnp.int32, turned_ref.shape, 1)
+        begin = a * depth
+        kept = jnp.logical_and(lane >= begin, lane < begin + depth)
+        chosen = jnp.where(kept, turned_ref[...], 0.0).astype(BF16)
+        total_ref[...] += dot(weights_ref[a], chosen)
+
+    for z in range(min(WEIGHTS_AHEAD, depth), depth):
+        volume_copy(z).start()
+    for copy in copies:
+        copy.start()
+    high, low = split_bf16(total_ref[...])
+    stack_ref[...] = jnp.concatenate([high, low, high, low], axis=1)
+
     @pl.loop(0, depth)
     def _(z):
         volume_copy(z).wait()
-
-        @pl.when(z + AHEAD < depth)
-        def _():
-            volume_copy(z + AHEAD).start()
 
         @pl.when(z >= slots)
         def _():
@@ -637,39 +608,48 @@
     object_copy.wait()
 
 
-def volume_update(angle_ids, sums, rays, volume, partial_object, from_left, from_right):
+def volume_update(
+    angle_ids, residual, proj_weights, rays, volume, partial_object, from_left, from_right
+):
     depth, rows, width = volume.shape
+    projections = angle_ids.shape[0]
+    both = projections * depth
     slots = min(4, depth)
     return pl.pallas_call(
         update_kernel,
-        in_specs=[SCALARS, WHOLE] + [IN_HBM] * 3 + [ANYWHERE] * 2,
-        out_specs=[IN_HBM] * 2,
+        in_specs=[SCALARS] + [ANYWHERE] * 7,
+        out_specs=[ANYWHERE] * 2,
         out_shape=[
             jax.ShapeDtypeStruct(volume.shape, F32),
             jax.ShapeDtypeStruct(partial_object.shape, F32),
         ],
         scratch_shapes=[
+            VMEM(residual.shape, BF16),
+            VMEM((projections, rows, width), BF16),
             VMEM(rays.shape, F32),
-            VMEM((rows, 4 * sums.shape[1]), F32),
-            VMEM((4 * sums.shape[1], width), BF16),
             VMEM(volume.shape, F32),
+            VMEM((width, both), F32),
+            VMEM((rows, both), F32),
+            VMEM((rows, 4 * both), F32),
+            VMEM((4 * both, width), BF16),
             VMEM((slots, rows, width), F32),
             VMEM(partial_object.shape, F32),
             VMEM(from_left.shape, F32),
             VMEM(from_right.shape, F32),
-            DMA,
+            pltpu.SemaphoreType.DMA((2,)),
+            pltpu.SemaphoreType.DMA((projections,)),
             pltpu.SemaphoreType.DMA((depth,)),
             pltpu.SemaphoreType.DMA((slots,)),
             pltpu.SemaphoreType.DMA((3,)),
         ],
-        compiler_params=pltpu.CompilerParams(vmem_limit_bytes=48 * MIB),
+        compiler_params=pltpu.CompilerParams(vmem_limit_bytes=VMEM_LIMIT),
         cost_estimate=pl.CostEstimate(
-            flops=8 * rows * width * sums.shape[1] * depth,
-            bytes_accessed=2 * depth * rows * width * 4,
+            flops=2 * rows * width * both * (projections + 4 * depth),
+            bytes_accessed=2 * depth * rows * width * 4 + projections * rows * width * 2,
             transcendentals=0,
         ),
         name="update",
-    )(angle_ids, sums, rays, volume, partial_object, from_left, from_right)
+    )(angle_ids, residual, proj_weights, rays, volume, partial_object, from_left, from_right)
 
 
 def gather_parts_kernel(group, *refs):
@@ -678,7 +658,7 @@
     for ref in given[1:]:
         total = total + ref[...]
     _, rows, _ = out_ref.shape
-    rows -= ENERGY_ROWS
+    rows -= SUBLANES
     for k in range(group):
         out_ref[k, :rows, :] = total[k * rows : (k + 1) * rows]
         out_ref[k, rows:, :] = total[group * rows :]
@@ -689,43 +669,45 @@
 
 def gather_parts(given, group):
     total_rows, side = given[0].shape
-    rows = (total_rows - ENERGY_ROWS) // group + ENERGY_ROWS
+    rows = (total_rows - SUBLANES) // group + SUBLANES
     return pl.pallas_call(
         functools.partial(gather_parts_kernel, group),
         in_specs=[WHOLE] * len(given),
-        out_specs=IN_HBM,
+        out_specs=ANYWHERE,
         out_shape=jax.ShapeDtypeStruct((group, rows, side), F32),
         scratch_shapes=[VMEM((group, rows, side), F32), DMA],
+        compiler_params=pltpu.CompilerParams(vmem_limit_bytes=VMEM_LIMIT),
         name="probe_parts",
     )(*given)
 
 
-def probe_rows_kernel(given_ref, probe_ref, out_hbm, out_ref, sem):
+def probe_rows_kernel(given_ref, out_hbm, out_ref, sem):
     group, rows, side = given_ref.shape
-    rows -= ENERGY_ROWS
+    rows -= SUBLANES
     total = given_ref[0]
     for k in range(1, group):
         total = total + given_ref[k]
     energy = jnp.sum(total[rows:], keepdims=True) / (side * side)
-    new_rows = probe_ref[...] + total[:rows] / (energy + 1e-05)
+    steps = total[:rows] / (energy + 1e-05)
     for k in range(group):
-        out_ref[k] = new_rows
+        out_ref[k] = steps
     copy = pltpu.make_async_copy(out_ref, out_hbm, sem)
     copy.start()
     copy.wait()
 
 
-def probe_rows(given, own_rows):
+def probe_rows(given):
     group, rows, side = given.shape
-    shape = (group, rows - ENERGY_ROWS, side)
+    shape = (group, rows - SUBLANES, side)
     return pl.pallas_call(
         probe_rows_kernel,
-        in_specs=[WHOLE] * 2,
-        out_specs=IN_HBM,
+        in_specs=[WHOLE],
+        out_specs=ANYWHERE,
         out_shape=jax.ShapeDtypeStruct(shape, F32),
         scratch_shapes=[VMEM(shape, F32), DMA],
+        compiler_params=pltpu.CompilerParams(vmem_limit_bytes=VMEM_LIMIT),
         name="probe_rows",
-    )(given, own_rows)
+    )(given)
 
 
 def turned(value, axis, steps):
@@ -756,6 +738,7 @@
     from_left = shifted(own[:, :, tile_cols - margin :], "tile", 1)
     from_right = shifted(own[:, :, :margin], "tile", -1)
     forward = forward_parts(angle_ids, volume, proj_weights, ray_weights, plane)
+    forward, from_left, from_right = lax.optimization_barrier((forward, from_left, from_right))
     arrived = lax.all_to_all(forward, flat_axes, 0, 0, tiled=True)
     place = lax.axis_index("proj")
     partial_object, edge_left, edge_right, slab, *grad_parts = patch_updates(
@@ -776,6 +759,7 @@
     share = tile_cols // proj_count
     edge = slab.shape[3] - share
     holders = margin // edge
+    slab, arrived = lax.optimization_barrier((slab, arrived))
     pieces = slab.reshape(proj_count * layers, *slab.shape[2:])
     pieces = lax.all_to_all(pieces, ("proj", "cuts"), 0, 0, tiled=True)
     pairs = []
@@ -796,45 +780,35 @@
     given = [grad_parts[0]]
     for step in range(1, proj_count):
         given.append(turned(grad_parts[step], "proj", step))
-    by_receiver = gather_parts(given, group)
-    copies, by_receiver = lax.optimization_barrier((copies, by_receiver))
+    copies, given, edge_left, edge_right = lax.optimization_barrier(
+        (copies, given, edge_left, edge_right)
+    )
     residual = lax.all_to_all(copies, flat_axes, 0, 0, tiled=True)
-    received = lax.all_to_all(by_receiver, group_axes, 0, 0, tiled=True)
-
-    residual, edge_left, edge_right = lax.optimization_barrier((residual, edge_left, edge_right))
+    received = lax.all_to_all(gather_parts(given, group), group_axes, 0, 0, tiled=True)
     edge_from_right = shifted(edge_left, "tile", -1)
     edge_from_left = shifted(edge_right, "tile", 1)
-    back_sums = backward_sums(angle_ids, residual, proj_weights)
-
-    back_sums, received = lax.optimization_barrier((back_sums, received))
-    side = probe_field.shape[1]
-    rows = received.shape[1] - ENERGY_ROWS
-    begin = (place * group + lax.axis_index(group_axes)) * rows
-    own_rows = lax.dynamic_slice(
-        probe_field.reshape(2 * side, side), (begin, jnp.zeros((), begin.dtype)), (rows, side)
-    )
-    new_rows = lax.all_to_all(probe_rows(received, own_rows), group_axes, 0, 0, tiled=True)
-
+    steps = probe_rows(received)
+    steps, residual = lax.optimization_barrier((steps, residual))
+    steps = lax.all_to_all(steps, group_axes, 0, 0, tiled=True)
     new_volume, new_object = volume_update(
         angle_ids,
-        back_sums,
+        residual,
+        proj_weights,
         ray_weights,
         volume,
         partial_object,
         edge_from_left,
         edge_from_right,
     )
-    new_volume, new_rows = lax.optimization_barrier((new_volume, new_rows))
-    new_rows = new_rows.reshape(group * rows, side)
+    steps = steps.reshape(-1, probe_field.shape[1])
     if proj_count == 2:
-        other = turned(new_rows, "proj", 1)
+        other = turned(steps, "proj", 1)
         first = place == 0
-        new_probe = jnp.concatenate(
-            [jnp.where(first, new_rows, other), jnp.where(first, other, new_rows)], axis=0
-        )
+        steps = jnp.stack([jnp.where(first, steps, other), jnp.where(first, other, steps)])
     else:
-        new_probe = lax.all_gather(new_rows, "proj", axis=0, tiled=True)
-    return (new_object[None], new_probe.reshape(2, side, side), new_volume)
+        steps = lax.all_gather(steps, "proj", axis=0, tiled=True)
+    new_probe = probe_field + steps.reshape(probe_field.shape)
+    return (new_object[None], new_probe, new_volume)
 
 
 def solution(mesh):

time: 133 us -> 134 us (level)
  starting transfers between devices: 44.1 us -> 26.1 us
  local copies, waits for them, and re-layouts: 19.8 us -> 2.77 us
  waiting for transfers between devices: 17.4 us -> 32.5 us
  blocking collectives: 9.35 us -> 22.9 us
  Pallas kernels: 39.1 us -> 47.3 us
    unnamed x42 -> x18, local copies, waits for them, and re-layouts: 17.2 us -> 0.81 us
    all_to_all x1, blocking collectives: 9.35 us -> 22.9 us  [on_device(): lax.all_to_all(gather_parts(given, group), group_axes, 0, 0, tiled=True)]
    all_to_all x2, waiting for transfers between devices: 0.01 us -> 10.2 us  [the longest x1 5.19 us: on_device(): steps = lax.all_to_all(steps, group_axes, 0, 0, tiled=True)]
    ppermute x4, waiting for transfers between devices: 7.33 us -> 16.3 us  [shifted(): lax.ppermute(value, axis, [(source, source + steps) for source in range(l...]
    all_to_all x1, waiting for transfers between devices: 8.56 us -> 0.01 us  [on_device(): arrived = lax.all_to_all(forward, flat_axes, 0, 0, tiled=True)]
    pallas_call x5 -> x4, Pallas kernels: 37.3 us -> 45.4 us  [the longest x1 17.6 us: volume_update(): pl.pallas_call(update_kernel, in_specs=[SCALARS] + [ANYWHERE] * 7, out_sp...]
    all_to_all x1, starting transfers between devices: 9.84 us -> 3.49 us  [on_device(): arrived = lax.all_to_all(forward, flat_axes, 0, 0, tiled=True)]
    all_to_all x1, waiting for transfers between devices: 0.01 us -> 5.97 us  [on_device(): pieces = lax.all_to_all(pieces, ('proj', 'cuts'), 0, 0, tiled=True)]
  transfers between devices with their start and end apart: 11 -> 11, of which waited for: 3 -> 6; matrix products, arithmetic and copies ran while one was open for 1% -> 0% of each run, Pallas kernels for 24% -> 34%
where the time goes in v4:
time: 134 us
  Pallas kernels  47.3 us (35%)
  waiting for transfers between devices  32.5 us (24%)
  starting transfers between devices  26.1 us (19%)
  blocking collectives  22.9 us (17%)
  local copies, waits for them, and re-layouts  2.77 us (2%)
  between operations  1.53 us (1%)
    all_to_all x1, blocking collectives, on_device(): lax.all_to_all(gather_parts(given, group), group_axes, 0, 0, tiled=True)  22.9 us
    pallas_call x1, Pallas kernels, volume_update(): pl.pallas_call(update_kernel, in_specs=[SCALARS] + [ANYWHERE] * 7, out_sp...  17.6 us
    ppermute x4, waiting for transfers between devices, shifted(): lax.ppermute(value, axis, [(source, source + steps) for source in range(l...  16.3 us
    pallas_call x1, Pallas kernels, forward_parts(): pl.pallas_call(forward_kernel, in_specs=[SCALARS] + [ANYWHERE] * 3, out_s...  13.7 us
    pallas_call x1, Pallas kernels, patch_updates(): pl.pallas_call(patch_kernel, in_specs=[SCALARS] * 4 + [ANYWHERE] * 7, out...  12.3 us
    ppermute x4, starting transfers between devices, shifted(): lax.ppermute(value, axis, [(source, source + steps) for source in range(l...  11.2 us
    all_to_all x1, waiting for transfers between devices, on_device(): pieces = lax.all_to_all(pieces, ('proj', 'cuts'), 0, 0, tiled=True)  5.97 us
    all_to_all x1, waiting for transfers between devices, on_device(): steps = lax.all_to_all(steps, group_axes, 0, 0, tiled=True)  5.19 us
  transfers between devices with their start and end apart: 11, of which 6 were waited for; matrix products, arithmetic and copies ran while one was open for 0% of the time, Pallas kernels for 34%

profile of v4, /device:TPU:0, one launch (start us, length us, event | category | flops | bytes accessed | tf_op | source)
XLA Modules:
  0.0 134.1 jit_solution(7656929429622524603)
XLA Ops:
  0.6 1.2 fusion.2
  1.8 4.9 %collective-permute-start = (f32[2,384,128]{2,1,0:T(8,128)S(1)}, f32[2,384,128]{2,1,0:T(8,128)S(1)}, u32[]{:S(2)}, u32[]{:S(2)}) collective-permute-start(f32[2,384,128]{2,1,0:T(8,128)S(1)} %get-tuple-element.44), channel_id=1, source_target_pairs={{0,8},{8,16},{16,24},{1,9},{9,17},{17,25},{2,10},{10,18},{18,26},{... | collective-permute-start | bytes 1179656 | tf_op jit(solution)/shard_map/ppermute | solution.py:31
  6.7 1.3 collective-permute-start.1
  8.0 13.7 %forward.1 = f32[8,8,8,256]{3,2,1,0:T(8,128)} custom-call(s32[8]{0:T(128)} %ids_ref.3, f32[16,2048]{1,0:T(8,128)} %rays_hbm.3, f32[8,256,2048]{2,1,0:T(8,128)} %volume_hbm.3, bf16[16,256,2048]{2,1,0:T(8,128)(2,1)} %weights_hbm.3), custom_call_target="tpu_custom_call" | custom-call | flops 2147483648 | bytes 25165824 | tf_op jit(solution)/shard_map/forward/pallas_call | solution.py:153
  21.7 0.0 collective-permute-done.left_hbm
  21.7 0.0 copy-start.7
  21.7 3.7 %collective-permute-done.1.right_hbm = f32[2,384,128]{2,1,0:T(8,128)S(1)} collective-permute-done((f32[2,384,128]{2,1,0:T(8,128)S(1)}, f32[2,384,128]{2,1,0:T(8,128)S(1)}, u32[]{:S(2)}, u32[]{:S(2)}) %collective-permute-start.1) | collective-permute-done | bytes 393248 | tf_op jit(solution)/shard_map/ppermute | solution.py:31
  25.4 0.0 copy-start.8
  25.4 3.5 %all-to-all-start = ((f32[8,8,8,256]{3,2,1,0:T(8,128)}), f32[8,8,8,256]{3,2,1,0:T(8,128)S(1)}, u32[]{:S(2)}, u32[]{:S(2)}) async-start(f32[8,8,8,256]{3,2,1,0:T(8,128)} %forward.1), calls=%async_computation | async-start | bytes 1048576 | tf_op jit(solution)/shard_map/all_to_all | solution.py:742
  29.5 0.0 copy-done.7
  29.6 0.0 copy-done.8
  29.6 12.3 %patches.1 = (f32[2,384,512]{2,1,0:T(8,128)}, f32[2,384,128]{2,1,0:T(8,128)}, f32[2,384,128]{2,1,0:T(8,128)}, f32[2,4,8,384]{3,2,1,0:T(8,128)}, f32[264,256]{1,0:T(8,128)}, /*index=5*/f32[264,256]{1,0:T(8,128)}) custom-call(s32[6]{0:T(128)} %bitcast.24, s32[6]{0:T(128)} %bitcast.25, s32[1]{0:T(128)} %bitcast.16.count_ref, s32[1]{0:T(128)} %bitcast.3.place_ref, ...), custom_call_target="tpu_custom_call" | custom-call | flops 3221225472 | bytes 6291456 | tf_op jit(solution)/shard_map/patches/pallas_call | solution.py:428
  41.9 0.0 all-to-all-done
  41.9 3.4 %all-to-all-start.1 = ((f32[8,8,384]{2,1,0:T(8,128)}), f32[8,8,384]{2,1,0:T(8,128)S(1)}, u32[]{:S(2)}, u32[]{:S(2)}) async-start(f32[8,8,384]{2,1,0:T(8,128)} %bitcast.20), calls=%async_computation.1 | async-start | bytes 196608 | tf_op jit(solution)/shard_map/all_to_all | solution.py:764
  45.2 0.4 collective-permute-start.3
  45.7 6.0 %all-to-all-done.1 = f32[8,8,384]{2,1,0:T(8,128)S(1)} async-done(((f32[8,8,384]{2,1,0:T(8,128)}), f32[8,8,384]{2,1,0:T(8,128)S(1)}, u32[]{:S(2)}, u32[]{:S(2)}) %all-to-all-start.1) | async-done | bytes 98336 | tf_op jit(solution)/shard_map/all_to_all | solution.py:764
  51.6 0.7 collective-permute-start.2
  52.4 0.0 collective-permute-done.2
  52.4 0.0 collective-permute-done.3.refs_1_
  52.4 0.0 copy-start.4
  52.4 0.8 broadcast_in_dim.13
  53.2 0.0 copy-done.4
  53.2 0.0 copy-start.6
  53.2 0.0 copy-start.5
  53.2 1.9 %probe_parts.1 = f32[16,24,256]{2,1,0:T(8,128)} custom-call(f32[264,256]{1,0:T(8,128)} %get-tuple-element.33.refs_0_, f32[264,256]{1,0:T(8,128)} %copy-done.4), custom_call_target="tpu_custom_call" | custom-call | tf_op jit(solution)/shard_map/probe_parts/pallas_call | solution.py:673
  55.1 22.9 %all_to_all.25.given_ref = f32[16,24,256]{2,1,0:T(8,128)} all-to-all(f32[16,24,256]{2,1,0:T(8,128)} %probe_parts.1), channel_id=1, replica_groups=mesh['tile'=4,'proj'=2,'cuts'=4] {'tile','cuts'}, dimensions={0} | all-to-all | bytes 786432 | tf_op jit(solution)/shard_map/all_to_all | solution.py:787
  78.0 3.4 %all-to-all-start.3 = ((bf16[8,8,8,256]{3,2,1,0:T(8,128)(2,1)}), bf16[8,8,8,256]{3,2,1,0:T(8,128)(2,1)S(1)}, u32[]{:S(2)}, u32[]{:S(2)}) async-start(bf16[8,8,8,256]{3,2,1,0:T(8,128)(2,1)} %broadcast_in_dim.13), calls=%async_computation.3 | async-start | bytes 524288 | tf_op jit(solution)/shard_map/all_to_all | solution.py:786
  81.4 1.9 %probe_rows.1 = f32[16,16,256]{2,1,0:T(8,128)} custom-call(f32[16,24,256]{2,1,0:T(8,128)} %all_to_all.25.given_ref), custom_call_target="tpu_custom_call" | custom-call | tf_op jit(solution)/shard_map/probe_rows/pallas_call | solution.py:702
  83.3 5.0 %all-to-all-done.3.residual_hbm = bf16[8,8,8,256]{3,2,1,0:T(8,128)(2,1)S(1)} async-done(((bf16[8,8,8,256]{3,2,1,0:T(8,128)(2,1)}), bf16[8,8,8,256]{3,2,1,0:T(8,128)(2,1)S(1)}, u32[]{:S(2)}, u32[]{:S(2)}) %all-to-all-start.3) | async-done | bytes 262176 | tf_op jit(solution)/shard_map/all_to_all | solution.py:786
  88.3 0.0 copy-start
  88.3 3.5 %all-to-all-start.4 = ((f32[16,16,256]{2,1,0:T(8,128)}), f32[16,16,256]{2,1,0:T(8,128)S(1)}, u32[]{:S(2)}, u32[]{:S(2)}) async-start(f32[16,16,256]{2,1,0:T(8,128)} %probe_rows.1), calls=%async_computation.4 | async-start | bytes 524288 | tf_op jit(solution)/shard_map/all_to_all | solution.py:792
  91.8 0.0 copy-done.6
  91.8 3.8 %collective-permute-start.4 = (f32[2,384,128]{2,1,0:T(8,128)S(1)}, f32[2,384,128]{2,1,0:T(8,128)S(1)}, u32[]{:S(2)}, u32[]{:S(2)}) collective-permute-start(f32[2,384,128]{2,1,0:T(8,128)S(1)} %copy-done.6), channel_id=1, source_target_pairs={{0,8},{8,16},{16,24},{1,9},{9,17},{17,25},{2,10},{10,18},{18,26},{... | collective-permute-start | bytes 1179656 | tf_op jit(solution)/shard_map/ppermute | solution.py:31
  95.6 0.0 copy-done.5
  95.6 1.3 collective-permute-start.5
  96.9 5.2 %all-to-all-done.4 = f32[16,16,256]{2,1,0:T(8,128)S(1)} async-done(((f32[16,16,256]{2,1,0:T(8,128)}), f32[16,16,256]{2,1,0:T(8,128)S(1)}, u32[]{:S(2)}, u32[]{:S(2)}) %all-to-all-start.4) | async-done | bytes 262176 | tf_op jit(solution)/shard_map/all_to_all | solution.py:792
  102.1 0.0 collective-permute-start.6
  102.1 2.3 %collective-permute-done.4.from_left_hbm = f32[2,384,128]{2,1,0:T(8,128)S(1)} collective-permute-done((f32[2,384,128]{2,1,0:T(8,128)S(1)}, f32[2,384,128]{2,1,0:T(8,128)S(1)}, u32[]{:S(2)}, u32[]{:S(2)}) %collective-permute-start.4) | collective-permute-done | bytes 393248 | tf_op jit(solution)/shard_map/ppermute | solution.py:31
  104.4 0.0 copy-start.2
  104.4 10.4 %collective-permute-done.5.from_right_hbm = f32[2,384,128]{2,1,0:T(8,128)S(1)} collective-permute-done((f32[2,384,128]{2,1,0:T(8,128)S(1)}, f32[2,384,128]{2,1,0:T(8,128)S(1)}, u32[]{:S(2)}, u32[]{:S(2)}) %collective-permute-start.5) | collective-permute-done | bytes 393248 | tf_op jit(solution)/shard_map/ppermute | solution.py:31
  114.8 0.0 copy-start.3
  114.8 0.0 copy-done
  114.8 0.0 copy-done.2
  114.8 0.8 copy-done.3
  115.5 17.6 %update.1 = (f32[8,256,2048]{2,1,0:T(8,128)}, f32[2,384,512]{2,1,0:T(8,128)}) custom-call(s32[8]{0:T(128)} %ids_ref.3, bf16[8,8,8,256]{3,2,1,0:T(8,128)(2,1)} %copy-done, bf16[16,256,2048]{2,1,0:T(8,128)(2,1)} %weights_hbm.3, f32[16,2048]{1,0:T(8,128)} %rays_hbm.3, f32[8,256,2048]{2,1,0:T(8,128)} %volume_hbm.3, f32[2,384,512]{2,1,0:T(8,128)} %get-tuple-element.37.object_hbm, ...), custom_call_target="tpu_custom_call" | custom-call | flops 2684354560 | bytes 41943040 | tf_op jit(solution)/shard_map/update/pallas_call | solution.py:618
  133.1 0.0 collective-permute-done.6
  133.2 0.0 copy-done.1
  133.2 0.9 maximum_add_fusion
  (5 shorter events, 0.1 us)
Async XLA Ops:
  1.8 19.9 %collective-permute-start = (f32[2,384,128]{2,1,0:T(8,128)S(1)}, f32[2,384,128]{2,1,0:T(8,128)S(1)}, u32[]{:S(2)}, u32[]{:S(2)}) collective-permute-start(f32[2,384,128]{2,1,0:T(8,128)S(1)} %get-tuple-element.44), channel_id=1, source_target_pairs={{0,8},{8,16},{16,24},{1,9},{9,17},{17,25},{2,10},{10,18},{18,26},{... | collective-permute-start | bytes 1179656 | tf_op jit(solution)/shard_map/ppermute | solution.py:31
  6.7 18.7 %collective-permute-start.1 = (f32[2,384,128]{2,1,0:T(8,128)S(1)}, f32[2,384,128]{2,1,0:T(8,128)S(1)}, u32[]{:S(2)}, u32[]{:S(2)}) collective-permute-start(f32[2,384,128]{2,1,0:T(8,128)S(1)} %get-tuple-element.43), channel_id=1, source_target_pairs={{8,0},{16,8},{24,16},{9,1},{17,9},{25,17},{10,2},{18,10},{26,18},{... | collective-permute-start | bytes 1179656 | tf_op jit(solution)/shard_map/ppermute | solution.py:31
  21.7 7.8 %copy-start.7 = (f32[2,384,128]{2,1,0:T(8,128)}, f32[2,384,128]{2,1,0:T(8,128)S(1)}, u32[]{:S(2)}) copy-start(f32[2,384,128]{2,1,0:T(8,128)S(1)} %collective-permute-done.left_hbm) | copy-start | bytes 1179652
  25.4 4.2 %copy-start.8 = (f32[2,384,128]{2,1,0:T(8,128)}, f32[2,384,128]{2,1,0:T(8,128)S(1)}, u32[]{:S(2)}) copy-start(f32[2,384,128]{2,1,0:T(8,128)S(1)} %collective-permute-done.1.right_hbm) | copy-start | bytes 1179652
  25.4 16.5 %all-to-all-start = ((f32[8,8,8,256]{3,2,1,0:T(8,128)}), f32[8,8,8,256]{3,2,1,0:T(8,128)S(1)}, u32[]{:S(2)}, u32[]{:S(2)}) async-start(f32[8,8,8,256]{3,2,1,0:T(8,128)} %forward.1), calls=%async_computation | async-start | bytes 1048576 | tf_op jit(solution)/shard_map/all_to_all | solution.py:742
  41.9 9.8 %all-to-all-start.1 = ((f32[8,8,384]{2,1,0:T(8,128)}), f32[8,8,384]{2,1,0:T(8,128)S(1)}, u32[]{:S(2)}, u32[]{:S(2)}) async-start(f32[8,8,384]{2,1,0:T(8,128)} %bitcast.20), calls=%async_computation.1 | async-start | bytes 196608 | tf_op jit(solution)/shard_map/all_to_all | solution.py:764
  45.2 7.1 %collective-permute-start.3 = (f32[264,256]{1,0:T(8,128)}, f32[264,256]{1,0:T(8,128)S(1)}, u32[]{:S(2)}, u32[]{:S(2)}) collective-permute-start(f32[264,256]{1,0:T(8,128)} %get-tuple-element.30), channel_id=1, source_target_pairs={{0,4},{4,0},{1,5},{5,1},{2,6},{6,2},{3,7},{7,3},{8,12},{12,8},{9,1... | collective-permute-start | bytes 811016 | tf_op jit(solution)/shard_map/ppermute | solution.py:715
  51.6 0.7 collective-permute-start.2
  52.4 0.8 copy-start.4
  53.2 38.6 %copy-start.6 = (f32[2,384,128]{2,1,0:T(8,128)S(1)}, f32[2,384,128]{2,1,0:T(8,128)}, u32[]{:S(2)}) copy-start(f32[2,384,128]{2,1,0:T(8,128)} %get-tuple-element.38) | copy-start | bytes 1179652
  53.2 42.4 %copy-start.5 = (f32[2,384,128]{2,1,0:T(8,128)S(1)}, f32[2,384,128]{2,1,0:T(8,128)}, u32[]{:S(2)}) copy-start(f32[2,384,128]{2,1,0:T(8,128)} %get-tuple-element.39) | copy-start | bytes 1179652
  78.0 10.3 %all-to-all-start.3 = ((bf16[8,8,8,256]{3,2,1,0:T(8,128)(2,1)}), bf16[8,8,8,256]{3,2,1,0:T(8,128)(2,1)S(1)}, u32[]{:S(2)}, u32[]{:S(2)}) async-start(bf16[8,8,8,256]{3,2,1,0:T(8,128)(2,1)} %broadcast_in_dim.13), calls=%async_computation.3 | async-start | bytes 524288 | tf_op jit(solution)/shard_map/all_to_all | solution.py:786
  88.3 26.5 %copy-start = (bf16[8,8,8,256]{3,2,1,0:T(8,128)(2,1)}, bf16[8,8,8,256]{3,2,1,0:T(8,128)(2,1)S(1)}, u32[]{:S(2)}) copy-start(bf16[8,8,8,256]{3,2,1,0:T(8,128)(2,1)S(1)} %all-to-all-done.3.residual_hbm) | copy-start | bytes 786436
  88.3 13.8 %all-to-all-start.4 = ((f32[16,16,256]{2,1,0:T(8,128)}), f32[16,16,256]{2,1,0:T(8,128)S(1)}, u32[]{:S(2)}, u32[]{:S(2)}) async-start(f32[16,16,256]{2,1,0:T(8,128)} %probe_rows.1), calls=%async_computation.4 | async-start | bytes 524288 | tf_op jit(solution)/shard_map/all_to_all | solution.py:792
  91.8 12.6 %collective-permute-start.4 = (f32[2,384,128]{2,1,0:T(8,128)S(1)}, f32[2,384,128]{2,1,0:T(8,128)S(1)}, u32[]{:S(2)}, u32[]{:S(2)}) collective-permute-start(f32[2,384,128]{2,1,0:T(8,128)S(1)} %copy-done.6), channel_id=1, source_target_pairs={{0,8},{8,16},{16,24},{1,9},{9,17},{17,25},{2,10},{10,18},{18,26},{... | collective-permute-start | bytes 1179656 | tf_op jit(solution)/shard_map/ppermute | solution.py:31
  95.6 19.2 %collective-permute-start.5 = (f32[2,384,128]{2,1,0:T(8,128)S(1)}, f32[2,384,128]{2,1,0:T(8,128)S(1)}, u32[]{:S(2)}, u32[]{:S(2)}) collective-permute-start(f32[2,384,128]{2,1,0:T(8,128)S(1)} %copy-done.5), channel_id=1, source_target_pairs={{8,0},{16,8},{24,16},{9,1},{17,9},{25,17},{10,2},{18,10},{26,18},{... | collective-permute-start | bytes 1179656 | tf_op jit(solution)/shard_map/ppermute | solution.py:31
  102.1 31.1 %collective-permute-start.6 = (f32[256,256]{1,0:T(8,128)S(1)}, f32[256,256]{1,0:T(8,128)S(1)}, u32[]{:S(2)}, u32[]{:S(2)}) collective-permute-start(f32[256,256]{1,0:T(8,128)S(1)} %bitcast.17), channel_id=1, source_target_pairs={{0,4},{4,0},{1,5},{5,1},{2,6},{6,2},{3,7},{7,3},{8,12},{12,8},{9,1... | collective-permute-start | bytes 786440 | tf_op jit(solution)/shard_map/ppermute | solution.py:715
  104.4 10.4 %copy-start.2 = (f32[2,384,128]{2,1,0:T(8,128)}, f32[2,384,128]{2,1,0:T(8,128)S(1)}, u32[]{:S(2)}) copy-start(f32[2,384,128]{2,1,0:T(8,128)S(1)} %collective-permute-done.4.from_left_hbm) | copy-start | bytes 1179652
  114.8 0.8 copy-start.3
  115.5 17.7 %copy-start.1 = (f32[2,256,256]{2,1,0:T(8,128)S(1)}, f32[2,256,256]{2,1,0:T(8,128)}, u32[]{:S(2)}) copy-start(f32[2,256,256]{2,1,0:T(8,128)} %probe_hbm.1) | copy-start | bytes 1572868

commit v5 on v4

--- a/solution.py
+++ b/solution.py
@@ -15,8 +15,7 @@
 BF16 = jnp.bfloat16
 LANES = 128
 SUBLANES = 8
-AHEAD = 6
-WEIGHTS_AHEAD = 6
+AHEAD = 3
 ANYWHERE = pl.BlockSpec(memory_space=pl.ANY)
 WHOLE = pl.BlockSpec(memory_space=pltpu.VMEM)
 SCALARS = pl.BlockSpec(memory_space=pltpu.SMEM)
@@ -481,41 +480,10 @@
     )
 
 
-def update_kernel(
-    ids_ref,
-    residual_hbm,
-    weights_hbm,
-    rays_hbm,
-    volume_hbm,
-    object_hbm,
-    from_left_hbm,
-    from_right_hbm,
-    out_hbm,
-    new_object_hbm,
-    residual_ref,
-    weights_ref,
-    rays_ref,
-    volume_ref,
-    turned_ref,
-    total_ref,
-    stack_ref,
-    spread_ref,
-    done_ref,
-    cells_ref,
-    left_ref,
-    right_ref,
-    small_sem,
-    weights_sem,
-    volume_sem,
-    out_sem,
-    object_sem,
+def backward_kernel(
+    ids_ref, residual_hbm, weights_hbm, out_ref, residual_ref, weights_ref, turned_ref, sem, weights_sem
 ):
-    depth = volume_ref.shape[0]
-    slots = done_ref.shape[0]
-    margin = left_ref.shape[2]
-    tile_cols = cells_ref.shape[2]
-    width = rays_ref.shape[1]
-    parts, projections, _, share = residual_ref.shape
+    parts, projections, depth, share = residual_ref.shape
     both = projections * depth
 
     def weights_copy(a):
@@ -523,31 +491,90 @@
             weights_hbm.at[ids_ref[a]], weights_ref.at[a], weights_sem.at[a]
         )
 
-    def volume_copy(z):
-        return pltpu.make_async_copy(volume_hbm.at[z], volume_ref.at[z], volume_sem.at[z])
-
-    def out_copy(z):
-        slot = lax.rem(z, slots)
-        return pltpu.make_async_copy(done_ref.at[slot], out_hbm.at[z], out_sem.at[slot])
-
-    residual_copy = pltpu.make_async_copy(residual_hbm, residual_ref, small_sem.at[0])
+    residual_copy = pltpu.make_async_copy(residual_hbm, residual_ref, sem)
     residual_copy.start()
-    rays_copy = pltpu.make_async_copy(rays_hbm, rays_ref, small_sem.at[1])
-    rays_copy.start()
-    for a in range(min(WEIGHTS_AHEAD, projections)):
+    for a in range(min(AHEAD, projections)):
         weights_copy(a).start()
-    copies = [
-        pltpu.make_async_copy(source, target, object_sem.at[k])
-        for k, (source, target) in enumerate(
-            ((object_hbm, cells_ref), (from_left_hbm, left_ref), (from_right_hbm, right_ref))
-        )
-    ]
-
     residual_copy.wait()
     for part in range(parts):
         block = residual_ref[part].astype(F32).reshape(both, share)
         turned_ref[part * share : (part + 1) * share, :] = block.T
-    total_ref[...] = jnp.zeros(total_ref.shape, F32)
+    out_ref[...] = jnp.zeros(out_ref.shape, F32)
+
+    @pl.loop(0, projections)
+    def _(a):
+        weights_copy(a).wait()
+
+        @pl.when(a + AHEAD < projections)
+        def _():
+            weights_copy(a + AHEAD).start()
+
+        lane = lax.broadcasted_iota(jnp.int32, turned_ref.shape, 1)
+        begin = a * depth
+        kept = jnp.logical_and(lane >= begin, lane < begin + depth)
+        chosen = jnp.where(kept, turned_ref[...], 0.0).astype(BF16)
+        out_ref[...] += dot(weights_ref[a], chosen)
+
+
+def backward_sums(angle_ids, residual, proj_weights):
+    _, rows, width = proj_weights.shape
+    _, projections, depth, _ = residual.shape
+    return pl.pallas_call(
+        backward_kernel,
+        in_specs=[SCALARS, ANYWHERE, ANYWHERE],
+        out_specs=WHOLE,
+        out_shape=jax.ShapeDtypeStruct((rows, projections * depth), F32),
+        scratch_shapes=[
+            VMEM(residual.shape, BF16),
+            VMEM((projections, rows, width), BF16),
+            VMEM((width, projections * depth), F32),
+            DMA,
+            pltpu.SemaphoreType.DMA((projections,)),
+        ],
+        compiler_params=pltpu.CompilerParams(vmem_limit_bytes=VMEM_LIMIT),
+        cost_estimate=pl.CostEstimate(
+            flops=2 * rows * width * projections * projections * depth,
+            bytes_accessed=projections * rows * width * 2,
+            transcendentals=0,
+        ),
+        name="backward",
+    )(angle_ids, residual, proj_weights)
+
+
+def update_kernel(
+    ids_ref,
+    sums_ref,
+    rays_hbm,
+    volume_hbm,
+    out_hbm,
+    rays_ref,
+    stack_ref,
+    spread_ref,
+    volume_ref,
+    done_ref,
+    rays_sem,
+    volume_sem,
+    out_sem,
+):
+    depth = volume_ref.shape[0]
+    slots = done_ref.shape[0]
+    width = rays_ref.shape[1]
+    projections = sums_ref.shape[1] // depth
+    both = sums_ref.shape[1]
+
+    def volume_copy(z):
+        return pltpu.make_async_copy(volume_hbm.at[z], volume_ref.at[z], volume_sem.at[z])
+
+    def out_copy(z):
+        slot = lax.rem(z, slots)
+        return pltpu.make_async_copy(done_ref.at[slot], out_hbm.at[z], out_sem.at[slot])
+
+    rays_copy = pltpu.make_async_copy(rays_hbm, rays_ref, rays_sem)
+    rays_copy.start()
+    for z in range(min(AHEAD, depth)):
+        volume_copy(z).start()
+    high, low = split_bf16(sums_ref[...])
+    stack_ref[...] = jnp.concatenate([high, low, high, low], axis=1)
     rays_copy.wait()
     rows = [
         jnp.broadcast_to(rays_ref[pl.ds(ids_ref[a], 1), :], (depth, width))
@@ -557,35 +584,13 @@
     for place, block in enumerate((high, high, low, low)):
         spread_ref[place * both : (place + 1) * both, :] = block.astype(BF16)
 
-    @pl.loop(0, projections)
-    def _(a):
-        @pl.when(a + WEIGHTS_AHEAD < projections)
-        def _():
-            weights_copy(a + WEIGHTS_AHEAD).start()
-
-        z = a + WEIGHTS_AHEAD - projections
-
-        @pl.when(jnp.logical_and(z >= 0, z < depth))
-        def _():
-            volume_copy(z).start()
-
-        weights_copy(a).wait()
-        lane = lax.broadcasted_iota(jnp.int32, turned_ref.shape, 1)
-        begin = a * depth
-        kept = jnp.logical_and(lane >= begin, lane < begin + depth)
-        chosen = jnp.where(kept, turned_ref[...], 0.0).astype(BF16)
-        total_ref[...] += dot(weights_ref[a], chosen)
-
-    for z in range(min(WEIGHTS_AHEAD, depth), depth):
-        volume_copy(z).start()
-    for copy in copies:
-        copy.start()
-    high, low = split_bf16(total_ref[...])
-    stack_ref[...] = jnp.concatenate([high, low, high, low], axis=1)
-
     @pl.loop(0, depth)
     def _(z):
         volume_copy(z).wait()
+
+        @pl.when(z + AHEAD < depth)
+        def _():
+            volume_copy(z + AHEAD).start()
 
         @pl.when(z >= slots)
         def _():
@@ -597,59 +602,36 @@
         done_ref[lax.rem(z, slots)] = volume_ref[z] - tomo_step * dot(chosen, spread_ref[...])
         out_copy(z).start()
 
-    for copy in copies:
-        copy.wait()
-    cells_ref[:, :, :margin] += left_ref[...]
-    cells_ref[:, :, tile_cols - margin :] += right_ref[...]
-    object_copy = pltpu.make_async_copy(cells_ref, new_object_hbm, object_sem.at[0])
-    object_copy.start()
     for z in range(max(depth - slots, 0), depth):
         out_copy(z).wait()
-    object_copy.wait()
-
-
-def volume_update(
-    angle_ids, residual, proj_weights, rays, volume, partial_object, from_left, from_right
-):
+
+
+def volume_update(angle_ids, sums, rays, volume):
     depth, rows, width = volume.shape
-    projections = angle_ids.shape[0]
-    both = projections * depth
     slots = min(4, depth)
     return pl.pallas_call(
         update_kernel,
-        in_specs=[SCALARS] + [ANYWHERE] * 7,
-        out_specs=[ANYWHERE] * 2,
-        out_shape=[
-            jax.ShapeDtypeStruct(volume.shape, F32),
-            jax.ShapeDtypeStruct(partial_object.shape, F32),
-        ],
+        in_specs=[SCALARS, WHOLE] + [ANYWHERE] * 2,
+        out_specs=ANYWHERE,
+        out_shape=jax.ShapeDtypeStruct(volume.shape, F32),
         scratch_shapes=[
-            VMEM(residual.shape, BF16),
-            VMEM((projections, rows, width), BF16),
             VMEM(rays.shape, F32),
+            VMEM((rows, 4 * sums.shape[1]), F32),
+            VMEM((4 * sums.shape[1], width), BF16),
             VMEM(volume.shape, F32),
-            VMEM((width, both), F32),
-            VMEM((rows, both), F32),
-            VMEM((rows, 4 * both), F32),
-            VMEM((4 * both, width), BF16),
             VMEM((slots, rows, width), F32),
-            VMEM(partial_object.shape, F32),
-            VMEM(from_left.shape, F32),
-            VMEM(from_right.shape, F32),
-            pltpu.SemaphoreType.DMA((2,)),
-            pltpu.SemaphoreType.DMA((projections,)),
+            DMA,
             pltpu.SemaphoreType.DMA((depth,)),
             pltpu.SemaphoreType.DMA((slots,)),
-            pltpu.SemaphoreType.DMA((3,)),
         ],
         compiler_params=pltpu.CompilerParams(vmem_limit_bytes=VMEM_LIMIT),
         cost_estimate=pl.CostEstimate(
-            flops=2 * rows * width * both * (projections + 4 * depth),
-            bytes_accessed=2 * depth * rows * width * 4 + projections * rows * width * 2,
+            flops=8 * rows * width * sums.shape[1] * depth,
+            bytes_accessed=2 * depth * rows * width * 4,
             transcendentals=0,
         ),
         name="update",
-    )(angle_ids, residual, proj_weights, rays, volume, partial_object, from_left, from_right)
+    )(angle_ids, sums, rays, volume)
 
 
 def gather_parts_kernel(group, *refs):
@@ -657,11 +639,16 @@
     total = given[0][...]
     for ref in given[1:]:
         total = total + ref[...]
-    _, rows, _ = out_ref.shape
-    rows -= SUBLANES
+    blocks = total.shape[1] // LANES
+    rows = (out_ref.shape[1] - SUBLANES) // blocks
+    columns = [total[:, k * LANES : (k + 1) * LANES] for k in range(blocks)]
+    energy = columns[0][group * rows :]
+    for block in columns[1:]:
+        energy = energy + block[group * rows :]
     for k in range(group):
-        out_ref[k, :rows, :] = total[k * rows : (k + 1) * rows]
-        out_ref[k, rows:, :] = total[group * rows :]
+        for place, block in enumerate(columns):
+            out_ref[k, place * rows : (place + 1) * rows, :] = block[k * rows : (k + 1) * rows]
+        out_ref[k, blocks * rows :, :] = energy
     copy = pltpu.make_async_copy(out_ref, out_hbm, sem)
     copy.start()
     copy.wait()
@@ -669,36 +656,40 @@
 
 def gather_parts(given, group):
     total_rows, side = given[0].shape
-    rows = (total_rows - SUBLANES) // group + SUBLANES
+    rows = (total_rows - SUBLANES) // group * (side // LANES) + SUBLANES
+    shape = (group, rows, LANES)
     return pl.pallas_call(
         functools.partial(gather_parts_kernel, group),
         in_specs=[WHOLE] * len(given),
         out_specs=ANYWHERE,
-        out_shape=jax.ShapeDtypeStruct((group, rows, side), F32),
-        scratch_shapes=[VMEM((group, rows, side), F32), DMA],
+        out_shape=jax.ShapeDtypeStruct(shape, F32),
+        scratch_shapes=[VMEM(shape, F32), DMA],
         compiler_params=pltpu.CompilerParams(vmem_limit_bytes=VMEM_LIMIT),
         name="probe_parts",
     )(*given)
 
 
 def probe_rows_kernel(given_ref, out_hbm, out_ref, sem):
-    group, rows, side = given_ref.shape
-    rows -= SUBLANES
+    group, rows, _ = given_ref.shape
+    receivers, taken, side = out_ref.shape
     total = given_ref[0]
     for k in range(1, group):
         total = total + given_ref[k]
-    energy = jnp.sum(total[rows:], keepdims=True) / (side * side)
-    steps = total[:rows] / (energy + 1e-05)
-    for k in range(group):
+    energy = jnp.sum(total[rows - SUBLANES :], keepdims=True) / (side * side)
+    steps = total[: rows - SUBLANES] / (energy + 1e-05)
+    steps = jnp.concatenate(
+        [steps[k * taken : (k + 1) * taken] for k in range(side // LANES)], axis=1
+    )
+    for k in range(receivers):
         out_ref[k] = steps
     copy = pltpu.make_async_copy(out_ref, out_hbm, sem)
     copy.start()
     copy.wait()
 
 
-def probe_rows(given):
-    group, rows, side = given.shape
-    shape = (group, rows - SUBLANES, side)
+def probe_rows(given, side, receivers):
+    _, rows, _ = given.shape
+    shape = (receivers, (rows - SUBLANES) * LANES // side, side)
     return pl.pallas_call(
         probe_rows_kernel,
         in_specs=[WHOLE],
@@ -738,7 +729,7 @@
     from_left = shifted(own[:, :, tile_cols - margin :], "tile", 1)
     from_right = shifted(own[:, :, :margin], "tile", -1)
     forward = forward_parts(angle_ids, volume, proj_weights, ray_weights, plane)
-    forward, from_left, from_right = lax.optimization_barrier((forward, from_left, from_right))
+    _, from_left, from_right = lax.optimization_barrier((forward, from_left, from_right))
     arrived = lax.all_to_all(forward, flat_axes, 0, 0, tiled=True)
     place = lax.axis_index("proj")
     partial_object, edge_left, edge_right, slab, *grad_parts = patch_updates(
@@ -762,6 +753,7 @@
     slab, arrived = lax.optimization_barrier((slab, arrived))
     pieces = slab.reshape(proj_count * layers, *slab.shape[2:])
     pieces = lax.all_to_all(pieces, ("proj", "cuts"), 0, 0, tiled=True)
+    pieces, grad_parts = lax.optimization_barrier((pieces, grad_parts))
     pairs = []
     for tile in range(lax.axis_size("tile") - 1):
         for k in range(holders):
@@ -780,34 +772,31 @@
     given = [grad_parts[0]]
     for step in range(1, proj_count):
         given.append(turned(grad_parts[step], "proj", step))
-    copies, given, edge_left, edge_right = lax.optimization_barrier(
-        (copies, given, edge_left, edge_right)
+    copies, given = lax.optimization_barrier((copies, given))
+    residual = lax.all_to_all(copies, flat_axes, 0, 0, tiled=True)
+    by_receiver = gather_parts(given, group)
+    residual, by_receiver, edge_left, edge_right = lax.optimization_barrier(
+        (residual, by_receiver, edge_left, edge_right)
     )
-    residual = lax.all_to_all(copies, flat_axes, 0, 0, tiled=True)
-    received = lax.all_to_all(gather_parts(given, group), group_axes, 0, 0, tiled=True)
+    received = lax.all_to_all(by_receiver, group_axes, 0, 0, tiled=True)
+    edge_from_left = shifted(edge_right, "tile", 1)
+    back_sums = backward_sums(angle_ids, residual, proj_weights)
+    back_sums, received, edge_from_left, edge_left = lax.optimization_barrier(
+        (back_sums, received, edge_from_left, edge_left)
+    )
     edge_from_right = shifted(edge_left, "tile", -1)
-    edge_from_left = shifted(edge_right, "tile", 1)
-    steps = probe_rows(received)
-    steps, residual = lax.optimization_barrier((steps, residual))
-    steps = lax.all_to_all(steps, group_axes, 0, 0, tiled=True)
-    new_volume, new_object = volume_update(
-        angle_ids,
-        residual,
-        proj_weights,
-        ray_weights,
-        volume,
-        partial_object,
-        edge_from_left,
-        edge_from_right,
+    steps = probe_rows(received, probe_field.shape[1], plane * layers)
+    back_sums, steps = lax.optimization_barrier((back_sums, steps))
+    steps = lax.all_to_all(steps, ("proj", "tile", "cuts"), 0, 0, tiled=True)
+    new_volume = volume_update(angle_ids, back_sums, ray_weights, volume)
+    new_volume, steps = lax.optimization_barrier((new_volume, steps))
+    new_probe = probe_field + steps.reshape(probe_field.shape)
+    rest = tile_cols - margin
+    new_object = (
+        partial_object
+        + jnp.pad(edge_from_left, ((0, 0), (0, 0), (0, rest)))
+        + jnp.pad(edge_from_right, ((0, 0), (0, 0), (rest, 0)))
     )
-    steps = steps.reshape(-1, probe_field.shape[1])
-    if proj_count == 2:
-        other = turned(steps, "proj", 1)
-        first = place == 0
-        steps = jnp.stack([jnp.where(first, steps, other), jnp.where(first, other, steps)])
-    else:
-        steps = lax.all_gather(steps, "proj", axis=0, tiled=True)
-    new_probe = probe_field + steps.reshape(probe_field.shape)
     return (new_object[None], new_probe, new_volume)
 
 

time: 134 us -> 113 us (0.84)
  waiting for transfers between devices: 32.5 us -> 11.7 us
  starting transfers between devices: 26.1 us -> 37.8 us
  blocking collectives: 22.9 us -> 11.8 us
  Pallas kernels: 47.3 us -> 43.9 us
    ppermute x4, waiting for transfers between devices: 16.3 us -> 4.71 us  [shifted(): lax.ppermute(value, axis, [(source, source + steps) for source in range(l...]
    all_to_all x2, waiting for transfers between devices: 11.2 us -> 0.01 us  [the longest x1 0.01 us: on_device(): received = lax.all_to_all(by_receiver, group_axes, 0, 0, tiled=True)]
    all_to_all x1, blocking collectives: 22.9 us -> 11.8 us  [on_device(): pieces = lax.all_to_all(pieces, ('proj', 'cuts'), 0, 0, tiled=True)]
    all_to_all x1, starting transfers between devices: 3.41 us -> 11.4 us  [on_device(): residual = lax.all_to_all(copies, flat_axes, 0, 0, tiled=True)]
    pallas_call x1, Pallas kernels: 12.3 us -> 7.12 us  [patch_updates(): pl.pallas_call(patch_kernel, in_specs=[SCALARS] * 4 + [ANYWHERE] * 7, out...]
    all_to_all x2, starting transfers between devices: 6.91 us -> 9.41 us  [the longest x1 5.87 us: on_device(): steps = lax.all_to_all(steps, ('proj', 'tile', 'cuts'), 0, 0, tiled=True)]
    pallas_call x1 -> x2, Pallas kernels: 17.6 us -> 19.9 us  [the longest x1 13.1 us: volume_update(): pl.pallas_call(update_kernel, in_specs=[SCALARS, WHOLE] + [ANYWHERE] * 2,...]
  transfers between devices with their start and end apart: 11 -> 10, of which waited for: 6 -> 5; matrix products, arithmetic and copies ran while one was open for 0% -> 1% of each run, Pallas kernels for 34% -> 37%
where the time goes in v5:
time: 113 us
  Pallas kernels  43.9 us (39%)
  starting transfers between devices  37.8 us (33%)
  blocking collectives  11.8 us (10%)
  waiting for transfers between devices  11.7 us (10%)
  local copies, waits for them, and re-layouts  3.54 us (3%)
  other arithmetic  2.24 us (2%)
  between operations  1.51 us (1%)
    pallas_call x1, Pallas kernels, forward_parts(): pl.pallas_call(forward_kernel, in_specs=[SCALARS] + [ANYWHERE] * 3, out_s...  13.2 us
    pallas_call x1, Pallas kernels, volume_update(): pl.pallas_call(update_kernel, in_specs=[SCALARS, WHOLE] + [ANYWHERE] * 2,...  13.1 us
    ppermute x4, starting transfers between devices, shifted(): lax.ppermute(value, axis, [(source, source + steps) for source in range(l...  12 us
    all_to_all x1, blocking collectives, on_device(): pieces = lax.all_to_all(pieces, ('proj', 'cuts'), 0, 0, tiled=True)  11.8 us
    all_to_all x1, starting transfers between devices, on_device(): residual = lax.all_to_all(copies, flat_axes, 0, 0, tiled=True)  11.4 us
    pallas_call x1, Pallas kernels, patch_updates(): pl.pallas_call(patch_kernel, in_specs=[SCALARS] * 4 + [ANYWHERE] * 7, out...  7.12 us
    pallas_call x1, Pallas kernels, backward_sums(): pl.pallas_call(backward_kernel, in_specs=[SCALARS, ANYWHERE, ANYWHERE], o...  6.73 us
    all_to_all x1, starting transfers between devices, on_device(): steps = lax.all_to_all(steps, ('proj', 'tile', 'cuts'), 0, 0, tiled=True)  5.87 us
  transfers between devices with their start and end apart: 10, of which 5 were waited for; matrix products, arithmetic and copies ran while one was open for 1% of the time, Pallas kernels for 37%

profile of v5, /device:TPU:0, one launch (start us, length us, event | category | flops | bytes accessed | tf_op | source)
XLA Modules:
  0.0 112.5 jit_solution(7531133789046276190)
XLA Ops:
  0.6 1.2 %fusion = (f32[2,384,128]{2,1,0:T(8,128)S(1)}, f32[2,384,128]{2,1,0:T(8,128)S(1)}) fusion(f32[2,384,512]{2,1,0:T(8,128)} %bitcast.15), kind=kLoop, calls=%fused_computation.3 | loop fusion | bytes 1572864 | tf_op jit(solution)/shard_map/slice | solution.py:730
  1.8 1.3 %collective-permute-start.1 = (f32[2,384,128]{2,1,0:T(8,128)S(1)}, f32[2,384,128]{2,1,0:T(8,128)S(1)}, u32[]{:S(2)}, u32[]{:S(2)}) collective-permute-start(f32[2,384,128]{2,1,0:T(8,128)S(1)} %get-tuple-element.59), channel_id=1, source_target_pairs={{8,0},{16,8},{24,16},{9,1},{17,9},{25,17},{10,2},{18,10},{26,18},{... | collective-permute-start | bytes 1179656 | tf_op jit(solution)/shard_map/ppermute | solution.py:30
  3.1 5.5 %collective-permute-start = (f32[2,384,128]{2,1,0:T(8,128)S(1)}, f32[2,384,128]{2,1,0:T(8,128)S(1)}, u32[]{:S(2)}, u32[]{:S(2)}) collective-permute-start(f32[2,384,128]{2,1,0:T(8,128)S(1)} %get-tuple-element.60), channel_id=1, source_target_pairs={{0,8},{8,16},{16,24},{1,9},{9,17},{17,25},{2,10},{10,18},{18,26},{... | collective-permute-start | bytes 1179656 | tf_op jit(solution)/shard_map/ppermute | solution.py:30
  8.6 13.2 %forward.1 = f32[8,8,8,256]{3,2,1,0:T(8,128)} custom-call(s32[8]{0:T(128)} %ids_ref.5, f32[16,2048]{1,0:T(8,128)} %rays_hbm.3, f32[8,256,2048]{2,1,0:T(8,128)} %volume_hbm.3, bf16[16,256,2048]{2,1,0:T(8,128)(2,1)} %weights_hbm.3), custom_call_target="tpu_custom_call" | custom-call | flops 2147483648 | bytes 25165824 | tf_op jit(solution)/shard_map/forward/pallas_call | solution.py:152
  21.8 4.2 %all-to-all-start = ((f32[8,8,8,256]{3,2,1,0:T(8,128)}), f32[8,8,8,256]{3,2,1,0:T(8,128)S(1)}, u32[]{:S(2)}, u32[]{:S(2)}) async-start(f32[8,8,8,256]{3,2,1,0:T(8,128)} %forward.1), calls=%async_computation | async-start | bytes 1048576 | tf_op jit(solution)/shard_map/all_to_all | solution.py:733
  26.6 0.0 collective-permute-done.1.right_hbm
  26.6 0.0 copy-start.7
  26.7 0.0 collective-permute-done.left_hbm
  26.7 0.0 copy-start.8
  26.7 0.7 copy-done.7
  27.4 0.1 copy-done.8
  27.5 7.1 %patches.1 = (f32[2,384,512]{2,1,0:T(8,128)}, f32[2,384,128]{2,1,0:T(8,128)}, f32[2,384,128]{2,1,0:T(8,128)}, f32[2,4,8,384]{3,2,1,0:T(8,128)}, f32[264,256]{1,0:T(8,128)}, /*index=5*/f32[264,256]{1,0:T(8,128)}) custom-call(s32[6]{0:T(128)} %bitcast.20, s32[6]{0:T(128)} %bitcast.21, s32[1]{0:T(128)} %bitcast.13.count_ref, s32[1]{0:T(128)} %bitcast.3.place_ref, ...), custom_call_target="tpu_custom_call" | custom-call | flops 3221225472 | bytes 6291456 | tf_op jit(solution)/shard_map/patches/pallas_call | solution.py:427
  34.7 1.1 all-to-all-done
  35.7 11.8 %all_to_all.25 = f32[8,8,384]{2,1,0:T(8,128)S(1)} all-to-all(f32[8,8,384]{2,1,0:T(8,128)} %bitcast.17), channel_id=1, replica_groups=mesh['tile'=4,'proj'=2,'cuts'=4] {'proj','cuts'}, dimensions={0} | all-to-all | bytes 196608 | tf_op jit(solution)/shard_map/all_to_all | solution.py:755
  47.6 0.1 collective-permute-start.3
  47.7 0.0 copy-start.6
  47.7 0.8 collective-permute-start.2
  48.5 0.0 collective-permute-done.2
  48.6 0.8 collective-permute-done.3.refs_1_
  49.3 0.8 broadcast_in_dim.13
  50.1 11.4 %all-to-all-start.2 = ((bf16[8,8,8,256]{3,2,1,0:T(8,128)(2,1)}), bf16[8,8,8,256]{3,2,1,0:T(8,128)(2,1)S(1)}, u32[]{:S(2)}, u32[]{:S(2)}) async-start(bf16[8,8,8,256]{3,2,1,0:T(8,128)(2,1)} %broadcast_in_dim.13), calls=%async_computation.2 | async-start | bytes 524288 | tf_op jit(solution)/shard_map/all_to_all | solution.py:776
  61.5 0.0 copy-done.4
  61.5 1.8 %probe_parts.1 = f32[16,40,128]{2,1,0:T(8,128)} custom-call(f32[264,256]{1,0:T(8,128)} %get-tuple-element.43.refs_0_, f32[264,256]{1,0:T(8,128)} %copy-done.4), custom_call_target="tpu_custom_call" | custom-call | tf_op jit(solution)/shard_map/probe_parts/pallas_call | solution.py:661
  63.3 5.1 %all-to-all-done.2.residual_hbm = bf16[8,8,8,256]{3,2,1,0:T(8,128)(2,1)S(1)} async-done(((bf16[8,8,8,256]{3,2,1,0:T(8,128)(2,1)}), bf16[8,8,8,256]{3,2,1,0:T(8,128)(2,1)S(1)}, u32[]{:S(2)}, u32[]{:S(2)}) %all-to-all-start.2) | async-done | bytes 262176 | tf_op jit(solution)/shard_map/all_to_all | solution.py:776
  68.4 0.0 copy-start.2
  68.4 3.5 %all-to-all-start.3 = ((f32[16,40,128]{2,1,0:T(8,128)}), f32[16,40,128]{2,1,0:T(8,128)S(1)}, u32[]{:S(2)}, u32[]{:S(2)}) async-start(f32[16,40,128]{2,1,0:T(8,128)} %probe_parts.1), calls=%async_computation.3 | async-start | bytes 655360 | tf_op jit(solution)/shard_map/all_to_all | solution.py:781
  71.9 0.0 copy-done.6
  72.0 3.8 %collective-permute-start.4 = (f32[2,384,128]{2,1,0:T(8,128)S(1)}, f32[2,384,128]{2,1,0:T(8,128)S(1)}, u32[]{:S(2)}, u32[]{:S(2)}) collective-permute-start(f32[2,384,128]{2,1,0:T(8,128)S(1)} %copy-done.6), channel_id=1, source_target_pairs={{0,8},{8,16},{16,24},{1,9},{9,17},{17,25},{2,10},{10,18},{18,26},{... | collective-permute-start | bytes 1179656 | tf_op jit(solution)/shard_map/ppermute | solution.py:30
  75.7 0.0 copy-done.2
  75.7 6.7 %backward.1.sums_ref = f32[256,64]{1,0:T(8,128)} custom-call(s32[8]{0:T(128)} %ids_ref.5, bf16[8,8,8,256]{3,2,1,0:T(8,128)(2,1)} %copy-done.2, bf16[16,256,2048]{2,1,0:T(8,128)(2,1)} %weights_hbm.3), custom_call_target="tpu_custom_call" | custom-call | flops 536870912 | bytes 8388608 | tf_op jit(solution)/shard_map/backward/pallas_call | solution.py:522
  82.5 0.0 copy-start.5
  82.5 2.4 %collective-permute-done.4 = f32[2,384,128]{2,1,0:T(8,128)S(1)} collective-permute-done((f32[2,384,128]{2,1,0:T(8,128)S(1)}, f32[2,384,128]{2,1,0:T(8,128)S(1)}, u32[]{:S(2)}, u32[]{:S(2)}) %collective-permute-start.4) | collective-permute-done | bytes 393248 | tf_op jit(solution)/shard_map/ppermute | solution.py:30
  84.9 0.0 all-to-all-done.3.given_ref
  84.9 0.0 copy-start.1
  84.9 0.7 copy-done.1
  85.6 1.9 %probe_rows.1 = f32[32,16,256]{2,1,0:T(8,128)} custom-call(f32[16,40,128]{2,1,0:T(8,128)} %copy-done.1), custom_call_target="tpu_custom_call" | custom-call | tf_op jit(solution)/shard_map/probe_rows/pallas_call | solution.py:693
  87.6 5.9 %all-to-all-start.4 = ((f32[32,16,256]{2,1,0:T(8,128)}), f32[32,16,256]{2,1,0:T(8,128)S(1)}, u32[]{:S(2)}, u32[]{:S(2)}) async-start(f32[32,16,256]{2,1,0:T(8,128)} %probe_rows.1), calls=%async_computation.4 | async-start | bytes 1048576 | tf_op jit(solution)/shard_map/all_to_all | solution.py:790
  93.4 0.0 copy-done.5
  93.4 0.0 copy-start
  93.5 1.4 %collective-permute-start.5 = (f32[2,384,128]{2,1,0:T(8,128)S(1)}, f32[2,384,128]{2,1,0:T(8,128)S(1)}, u32[]{:S(2)}, u32[]{:S(2)}) collective-permute-start(f32[2,384,128]{2,1,0:T(8,128)S(1)} %copy-done.5), channel_id=1, source_target_pairs={{8,0},{16,8},{24,16},{9,1},{17,9},{25,17},{10,2},{18,10},{26,18},{... | collective-permute-start | bytes 1179656 | tf_op jit(solution)/shard_map/ppermute | solution.py:30
  94.9 13.1 %update.1 = f32[8,256,2048]{2,1,0:T(8,128)} custom-call(s32[8]{0:T(128)} %ids_ref.5, f32[256,64]{1,0:T(8,128)} %backward.1.sums_ref, f32[16,2048]{1,0:T(8,128)} %rays_hbm.3, f32[8,256,2048]{2,1,0:T(8,128)} %volume_hbm.3), custom_call_target="tpu_custom_call" | custom-call | flops 2147483648 | bytes 33554432 | tf_op jit(solution)/shard_map/update/pallas_call | solution.py:612
  108.0 2.3 %collective-permute-done.5 = f32[2,384,128]{2,1,0:T(8,128)S(1)} collective-permute-done((f32[2,384,128]{2,1,0:T(8,128)S(1)}, f32[2,384,128]{2,1,0:T(8,128)S(1)}, u32[]{:S(2)}, u32[]{:S(2)}) %collective-permute-start.5) | collective-permute-done | bytes 393248 | tf_op jit(solution)/shard_map/ppermute | solution.py:30
  110.3 0.0 copy-done
  110.3 0.0 copy-start.3
  110.3 1.3 %add_bitcast_fusion = f32[1,2,384,512]{3,2,1,0:T(8,128)} fusion(f32[2,384,128]{2,1,0:T(8,128)S(1)} %collective-permute-done.5, f32[2,384,512]{2,1,0:T(8,128)S(1)} %copy-done, f32[2,384,128]{2,1,0:T(8,128)S(1)} %collective-permute-done.4), kind=kLoop, calls=%fused_computation | loop fusion | flops 786432 | bytes 3932160 | tf_op jit(solution)/shard_map/broadcast_in_dim | solution.py:800
  111.7 0.0 all-to-all-done.4
  111.7 0.0 copy-done.3
  111.7 0.9 bitcast_add_fusion
  (4 shorter events, 0.1 us)
Async XLA Ops:
  1.8 24.8 %collective-permute-start.1 = (f32[2,384,128]{2,1,0:T(8,128)S(1)}, f32[2,384,128]{2,1,0:T(8,128)S(1)}, u32[]{:S(2)}, u32[]{:S(2)}) collective-permute-start(f32[2,384,128]{2,1,0:T(8,128)S(1)} %get-tuple-element.59), channel_id=1, source_target_pairs={{8,0},{16,8},{24,16},{9,1},{17,9},{25,17},{10,2},{18,10},{26,18},{... | collective-permute-start | bytes 1179656 | tf_op jit(solution)/shard_map/ppermute | solution.py:30
  3.1 23.5 %collective-permute-start = (f32[2,384,128]{2,1,0:T(8,128)S(1)}, f32[2,384,128]{2,1,0:T(8,128)S(1)}, u32[]{:S(2)}, u32[]{:S(2)}) collective-permute-start(f32[2,384,128]{2,1,0:T(8,128)S(1)} %get-tuple-element.60), channel_id=1, source_target_pairs={{0,8},{8,16},{16,24},{1,9},{9,17},{17,25},{2,10},{10,18},{18,26},{... | collective-permute-start | bytes 1179656 | tf_op jit(solution)/shard_map/ppermute | solution.py:30
  21.8 13.9 %all-to-all-start = ((f32[8,8,8,256]{3,2,1,0:T(8,128)}), f32[8,8,8,256]{3,2,1,0:T(8,128)S(1)}, u32[]{:S(2)}, u32[]{:S(2)}) async-start(f32[8,8,8,256]{3,2,1,0:T(8,128)} %forward.1), calls=%async_computation | async-start | bytes 1048576 | tf_op jit(solution)/shard_map/all_to_all | solution.py:733
  26.6 0.8 copy-start.7
  26.7 0.9 copy-start.8
  47.6 1.8 %collective-permute-start.3 = (f32[264,256]{1,0:T(8,128)}, f32[264,256]{1,0:T(8,128)S(1)}, u32[]{:S(2)}, u32[]{:S(2)}) collective-permute-start(f32[264,256]{1,0:T(8,128)} %get-tuple-element.41), channel_id=1, source_target_pairs={{0,4},{4,0},{1,5},{5,1},{2,6},{6,2},{3,7},{7,3},{8,12},{12,8},{9,1... | collective-permute-start | bytes 811016 | tf_op jit(solution)/shard_map/ppermute | solution.py:706
  47.7 24.3 %copy-start.6 = (f32[2,384,128]{2,1,0:T(8,128)S(1)}, f32[2,384,128]{2,1,0:T(8,128)}, u32[]{:S(2)}) copy-start(f32[2,384,128]{2,1,0:T(8,128)} %get-tuple-element.49) | copy-start | bytes 1179652
  47.7 0.8 collective-permute-start.2
  49.3 12.1 %copy-start.4 = (f32[264,256]{1,0:T(8,128)}, f32[264,256]{1,0:T(8,128)S(1)}, u32[]{:S(2)}) copy-start(f32[264,256]{1,0:T(8,128)S(1)} %collective-permute-done.3.refs_1_) | copy-start | bytes 811012
  50.1 18.3 %all-to-all-start.2 = ((bf16[8,8,8,256]{3,2,1,0:T(8,128)(2,1)}), bf16[8,8,8,256]{3,2,1,0:T(8,128)(2,1)S(1)}, u32[]{:S(2)}, u32[]{:S(2)}) async-start(bf16[8,8,8,256]{3,2,1,0:T(8,128)(2,1)} %broadcast_in_dim.13), calls=%async_computation.2 | async-start | bytes 524288 | tf_op jit(solution)/shard_map/all_to_all | solution.py:776
  68.4 7.3 %copy-start.2 = (bf16[8,8,8,256]{3,2,1,0:T(8,128)(2,1)}, bf16[8,8,8,256]{3,2,1,0:T(8,128)(2,1)S(1)}, u32[]{:S(2)}) copy-start(bf16[8,8,8,256]{3,2,1,0:T(8,128)(2,1)S(1)} %all-to-all-done.2.residual_hbm) | copy-start | bytes 786436
  68.4 16.5 %all-to-all-start.3 = ((f32[16,40,128]{2,1,0:T(8,128)}), f32[16,40,128]{2,1,0:T(8,128)S(1)}, u32[]{:S(2)}, u32[]{:S(2)}) async-start(f32[16,40,128]{2,1,0:T(8,128)} %probe_parts.1), calls=%async_computation.3 | async-start | bytes 655360 | tf_op jit(solution)/shard_map/all_to_all | solution.py:781
  72.0 12.9 %collective-permute-start.4 = (f32[2,384,128]{2,1,0:T(8,128)S(1)}, f32[2,384,128]{2,1,0:T(8,128)S(1)}, u32[]{:S(2)}, u32[]{:S(2)}) collective-permute-start(f32[2,384,128]{2,1,0:T(8,128)S(1)} %copy-done.6), channel_id=1, source_target_pairs={{0,8},{8,16},{16,24},{1,9},{9,17},{17,25},{2,10},{10,18},{18,26},{... | collective-permute-start | bytes 1179656 | tf_op jit(solution)/shard_map/ppermute | solution.py:30
  82.5 11.0 %copy-start.5 = (f32[2,384,128]{2,1,0:T(8,128)S(1)}, f32[2,384,128]{2,1,0:T(8,128)}, u32[]{:S(2)}) copy-start(f32[2,384,128]{2,1,0:T(8,128)} %get-tuple-element.52) | copy-start | bytes 1179652
  84.9 0.7 copy-start.1
  87.6 24.1 %all-to-all-start.4 = ((f32[32,16,256]{2,1,0:T(8,128)}), f32[32,16,256]{2,1,0:T(8,128)S(1)}, u32[]{:S(2)}, u32[]{:S(2)}) async-start(f32[32,16,256]{2,1,0:T(8,128)} %probe_rows.1), calls=%async_computation.4 | async-start | bytes 1048576 | tf_op jit(solution)/shard_map/all_to_all | solution.py:790
  93.4 16.9 %copy-start = (f32[2,384,512]{2,1,0:T(8,128)S(1)}, f32[2,384,512]{2,1,0:T(8,128)}, u32[]{:S(2)}) copy-start(f32[2,384,512]{2,1,0:T(8,128)} %get-tuple-element.33) | copy-start | bytes 4718596
  93.5 16.9 %collective-permute-start.5 = (f32[2,384,128]{2,1,0:T(8,128)S(1)}, f32[2,384,128]{2,1,0:T(8,128)S(1)}, u32[]{:S(2)}, u32[]{:S(2)}) collective-permute-start(f32[2,384,128]{2,1,0:T(8,128)S(1)} %copy-done.5), channel_id=1, source_target_pairs={{8,0},{16,8},{24,16},{9,1},{17,9},{25,17},{10,2},{18,10},{26,18},{... | collective-permute-start | bytes 1179656 | tf_op jit(solution)/shard_map/ppermute | solution.py:30
  110.3 1.3 %copy-start.3 = (f32[2,256,256]{2,1,0:T(8,128)S(1)}, f32[2,256,256]{2,1,0:T(8,128)}, u32[]{:S(2)}) copy-start(f32[2,256,256]{2,1,0:T(8,128)} %probe_hbm.1) | copy-start | bytes 1572868

commit v6 on v5

--- a/solution.py
+++ b/solution.py
@@ -16,6 +16,8 @@
 LANES = 128
 SUBLANES = 8
 AHEAD = 3
+UPDATE_AHEAD = 6
+SMALL_LIMIT = 16 * 1024 * 1024
 ANYWHERE = pl.BlockSpec(memory_space=pl.ANY)
 WHOLE = pl.BlockSpec(memory_space=pltpu.VMEM)
 SCALARS = pl.BlockSpec(memory_space=pltpu.SMEM)
@@ -110,20 +112,17 @@
             weights_copy(z + AHEAD - depth).start()
 
         piece = min(512, width)
-        first = second = None
+        total = None
         for k in range(0, width, piece):
             block = volume_ref[z, :, k : k + piece]
             high = block.astype(BF16)
             low = (block - high.astype(F32)).astype(BF16)
-            of_high = dot(high, table_ref[k : k + piece, :])
-            of_low = dot(low, table_ref[k : k + piece, :])
-            first = of_high if first is None else first + of_high
-            second = of_low if second is None else second + of_low
-        first = first.T
-        second = second.T
-        sums_ref[z] = first[:projections] + (
-            first[projections : 2 * projections] + second[:projections]
-        )
+            stacked = jnp.concatenate([high, low], axis=0)
+            part = dot(stacked, table_ref[k : k + piece, :])
+            total = part if total is None else total + part
+        rows = volume_ref.shape[1]
+        total = (total[:rows] + total[rows:]).T
+        sums_ref[z] = total[:projections] + total[projections : 2 * projections]
 
     @pl.loop(0, projections)
     def _(a):
@@ -571,7 +570,7 @@
 
     rays_copy = pltpu.make_async_copy(rays_hbm, rays_ref, rays_sem)
     rays_copy.start()
-    for z in range(min(AHEAD, depth)):
+    for z in range(min(UPDATE_AHEAD, depth)):
         volume_copy(z).start()
     high, low = split_bf16(sums_ref[...])
     stack_ref[...] = jnp.concatenate([high, low, high, low], axis=1)
@@ -588,9 +587,9 @@
     def _(z):
         volume_copy(z).wait()
 
-        @pl.when(z + AHEAD < depth)
+        @pl.when(z + UPDATE_AHEAD < depth)
         def _():
-            volume_copy(z + AHEAD).start()
+            volume_copy(z + UPDATE_AHEAD).start()
 
         @pl.when(z >= slots)
         def _():
@@ -664,7 +663,7 @@
         out_specs=ANYWHERE,
         out_shape=jax.ShapeDtypeStruct(shape, F32),
         scratch_shapes=[VMEM(shape, F32), DMA],
-        compiler_params=pltpu.CompilerParams(vmem_limit_bytes=VMEM_LIMIT),
+        compiler_params=pltpu.CompilerParams(vmem_limit_bytes=SMALL_LIMIT),
         name="probe_parts",
     )(*given)
 
@@ -696,7 +695,7 @@
         out_specs=ANYWHERE,
         out_shape=jax.ShapeDtypeStruct(shape, F32),
         scratch_shapes=[VMEM(shape, F32), DMA],
-        compiler_params=pltpu.CompilerParams(vmem_limit_bytes=VMEM_LIMIT),
+        compiler_params=pltpu.CompilerParams(vmem_limit_bytes=SMALL_LIMIT),
         name="probe_rows",
     )(given)
 
@@ -781,12 +780,12 @@
     received = lax.all_to_all(by_receiver, group_axes, 0, 0, tiled=True)
     edge_from_left = shifted(edge_right, "tile", 1)
     back_sums = backward_sums(angle_ids, residual, proj_weights)
-    back_sums, received, edge_from_left, edge_left = lax.optimization_barrier(
-        (back_sums, received, edge_from_left, edge_left)
-    )
+    back_sums, received, edge_left = lax.optimization_barrier((back_sums, received, edge_left))
     edge_from_right = shifted(edge_left, "tile", -1)
     steps = probe_rows(received, probe_field.shape[1], plane * layers)
-    back_sums, steps = lax.optimization_barrier((back_sums, steps))
+    back_sums, steps, edge_from_left = lax.optimization_barrier(
+        (back_sums, steps, edge_from_left)
+    )
     steps = lax.all_to_all(steps, ("proj", "tile", "cuts"), 0, 0, tiled=True)
     new_volume = volume_update(angle_ids, back_sums, ray_weights, volume)
     new_volume, steps = lax.optimization_barrier((new_volume, steps))

time: 113 us -> 110 us (0.973)
  starting transfers between devices: 37.8 us -> 35.4 us
    pallas_call x1, Pallas kernels: 7.12 us -> 9.67 us  [patch_updates(): pl.pallas_call(patch_kernel, in_specs=[SCALARS] * 4 + [ANYWHERE] * 7, out...]
    all_to_all x1, starting transfers between devices: 11.4 us -> 9.01 us  [on_device(): residual = lax.all_to_all(copies, flat_axes, 0, 0, tiled=True)]
    pallas_call x1, Pallas kernels: 13.1 us -> 11.7 us  [volume_update(): pl.pallas_call(update_kernel, in_specs=[SCALARS, WHOLE] + [ANYWHERE] * 2,...]
  transfers between devices with their start and end apart: 10 -> 10, of which waited for: 5 -> 5; matrix products, arithmetic and copies ran while one was open for 1% -> 1% of each run, Pallas kernels for 37% -> 40%
where the time goes in v6:
time: 110 us; the launch traced here: 109 us
  Pallas kernels  43.1 us (39%)
  starting transfers between devices  35.4 us (32%)
  waiting for transfers between devices  12.1 us (11%)
  blocking collectives  11.5 us (10%)
  local copies, waits for them, and re-layouts  2.77 us (3%)
  other arithmetic  2.23 us (2%)
  between operations  1.51 us (1%)
    pallas_call x1, Pallas kernels, forward_parts(): pl.pallas_call(forward_kernel, in_specs=[SCALARS] + [ANYWHERE] * 3, out_s...  13.3 us
    ppermute x4, starting transfers between devices, shifted(): lax.ppermute(value, axis, [(source, source + steps) for source in range(l...  12 us
    pallas_call x1, Pallas kernels, volume_update(): pl.pallas_call(update_kernel, in_specs=[SCALARS, WHOLE] + [ANYWHERE] * 2,...  11.7 us
    all_to_all x1, blocking collectives, on_device(): pieces = lax.all_to_all(pieces, ('proj', 'cuts'), 0, 0, tiled=True)  11.5 us
    pallas_call x1, Pallas kernels, patch_updates(): pl.pallas_call(patch_kernel, in_specs=[SCALARS] * 4 + [ANYWHERE] * 7, out...  9.67 us
    all_to_all x1, starting transfers between devices, on_device(): residual = lax.all_to_all(copies, flat_axes, 0, 0, tiled=True)  9.01 us
    pallas_call x1, Pallas kernels, backward_sums(): pl.pallas_call(backward_kernel, in_specs=[SCALARS, ANYWHERE, ANYWHERE], o...  6.72 us
    all_to_all x1, waiting for transfers between devices, on_device(): residual = lax.all_to_all(copies, flat_axes, 0, 0, tiled=True)  6.15 us
  transfers between devices with their start and end apart: 10, of which 5 were waited for; matrix products, arithmetic and copies ran while one was open for 1% of the time, Pallas kernels for 40%

profile of v6, /device:TPU:0, one launch (start us, length us, event | category | flops | bytes accessed | tf_op | source)
XLA Modules:
  0.0 108.7 jit_solution(10012157623547645749)
XLA Ops:
  0.6 1.2 %fusion = (f32[2,384,128]{2,1,0:T(8,128)S(1)}, f32[2,384,128]{2,1,0:T(8,128)S(1)}) fusion(f32[2,384,512]{2,1,0:T(8,128)} %bitcast.15), kind=kLoop, calls=%fused_computation.3 | loop fusion | bytes 1572864 | tf_op jit(solution)/shard_map/slice | solution.py:729
  1.8 1.3 %collective-permute-start.1 = (f32[2,384,128]{2,1,0:T(8,128)S(1)}, f32[2,384,128]{2,1,0:T(8,128)S(1)}, u32[]{:S(2)}, u32[]{:S(2)}) collective-permute-start(f32[2,384,128]{2,1,0:T(8,128)S(1)} %get-tuple-element.59), channel_id=1, source_target_pairs={{8,0},{16,8},{24,16},{9,1},{17,9},{25,17},{10,2},{18,10},{26,18},{... | collective-permute-start | bytes 1179656 | tf_op jit(solution)/shard_map/ppermute | solution.py:32
  3.1 5.5 %collective-permute-start = (f32[2,384,128]{2,1,0:T(8,128)S(1)}, f32[2,384,128]{2,1,0:T(8,128)S(1)}, u32[]{:S(2)}, u32[]{:S(2)}) collective-permute-start(f32[2,384,128]{2,1,0:T(8,128)S(1)} %get-tuple-element.60), channel_id=1, source_target_pairs={{0,8},{8,16},{16,24},{1,9},{9,17},{17,25},{2,10},{10,18},{18,26},{... | collective-permute-start | bytes 1179656 | tf_op jit(solution)/shard_map/ppermute | solution.py:32
  8.6 13.3 %forward.1 = f32[8,8,8,256]{3,2,1,0:T(8,128)} custom-call(s32[8]{0:T(128)} %ids_ref.5, f32[16,2048]{1,0:T(8,128)} %rays_hbm.3, f32[8,256,2048]{2,1,0:T(8,128)} %volume_hbm.3, bf16[16,256,2048]{2,1,0:T(8,128)(2,1)} %weights_hbm.3), custom_call_target="tpu_custom_call" | custom-call | flops 2147483648 | bytes 25165824 | tf_op jit(solution)/shard_map/forward/pallas_call | solution.py:151
  21.9 4.2 %all-to-all-start = ((f32[8,8,8,256]{3,2,1,0:T(8,128)}), f32[8,8,8,256]{3,2,1,0:T(8,128)S(1)}, u32[]{:S(2)}, u32[]{:S(2)}) async-start(f32[8,8,8,256]{3,2,1,0:T(8,128)} %forward.1), calls=%async_computation | async-start | bytes 1048576 | tf_op jit(solution)/shard_map/all_to_all | solution.py:732
  26.7 0.0 collective-permute-done.1.right_hbm
  26.8 0.0 copy-start.6
  26.8 0.0 collective-permute-done.left_hbm
  26.8 0.0 copy-start.7
  26.8 0.7 copy-done.6
  27.5 0.1 copy-done.7
  27.6 9.7 %patches.1 = (f32[2,384,512]{2,1,0:T(8,128)}, f32[2,384,128]{2,1,0:T(8,128)}, f32[2,384,128]{2,1,0:T(8,128)}, f32[2,4,8,384]{3,2,1,0:T(8,128)}, f32[264,256]{1,0:T(8,128)}, /*index=5*/f32[264,256]{1,0:T(8,128)}) custom-call(s32[6]{0:T(128)} %bitcast.20, s32[6]{0:T(128)} %bitcast.21, s32[1]{0:T(128)} %bitcast.13.count_ref, s32[1]{0:T(128)} %bitcast.3.place_ref, ...), custom_call_target="tpu_custom_call" | custom-call | flops 3221225472 | bytes 6291456 | tf_op jit(solution)/shard_map/patches/pallas_call | solution.py:426
  37.3 0.0 copy-start
  37.3 0.0 all-to-all-done
  37.3 11.5 %all_to_all.25 = f32[8,8,384]{2,1,0:T(8,128)S(1)} all-to-all(f32[8,8,384]{2,1,0:T(8,128)} %bitcast.17), channel_id=1, replica_groups=mesh['tile'=4,'proj'=2,'cuts'=4] {'proj','cuts'}, dimensions={0} | all-to-all | bytes 196608 | tf_op jit(solution)/shard_map/all_to_all | solution.py:754
  48.8 0.1 collective-permute-start.3
  49.0 0.0 copy-start.5
  49.0 0.8 collective-permute-start.2
  49.8 0.0 collective-permute-done.2
  49.8 0.8 collective-permute-done.3.refs_1_
  50.6 0.7 broadcast_in_dim.13
  51.3 9.0 %all-to-all-start.2 = ((bf16[8,8,8,256]{3,2,1,0:T(8,128)(2,1)}), bf16[8,8,8,256]{3,2,1,0:T(8,128)(2,1)S(1)}, u32[]{:S(2)}, u32[]{:S(2)}) async-start(bf16[8,8,8,256]{3,2,1,0:T(8,128)(2,1)} %broadcast_in_dim.13), calls=%async_computation.2 | async-start | bytes 524288 | tf_op jit(solution)/shard_map/all_to_all | solution.py:775
  60.3 0.0 copy-done
  60.3 0.8 probe_parts.1
  61.1 6.2 %all-to-all-done.2.residual_hbm = bf16[8,8,8,256]{3,2,1,0:T(8,128)(2,1)S(1)} async-done(((bf16[8,8,8,256]{3,2,1,0:T(8,128)(2,1)}), bf16[8,8,8,256]{3,2,1,0:T(8,128)(2,1)S(1)}, u32[]{:S(2)}, u32[]{:S(2)}) %all-to-all-start.2) | async-done | bytes 262176 | tf_op jit(solution)/shard_map/all_to_all | solution.py:775
  67.3 0.0 copy-start.2
  67.3 3.5 %all-to-all-start.3 = ((f32[16,40,128]{2,1,0:T(8,128)}), f32[16,40,128]{2,1,0:T(8,128)S(1)}, u32[]{:S(2)}, u32[]{:S(2)}) async-start(f32[16,40,128]{2,1,0:T(8,128)} %probe_parts.1), calls=%async_computation.3 | async-start | bytes 655360 | tf_op jit(solution)/shard_map/all_to_all | solution.py:780
  70.8 0.0 copy-done.5
  70.8 3.8 %collective-permute-start.4 = (f32[2,384,128]{2,1,0:T(8,128)S(1)}, f32[2,384,128]{2,1,0:T(8,128)S(1)}, u32[]{:S(2)}, u32[]{:S(2)}) collective-permute-start(f32[2,384,128]{2,1,0:T(8,128)S(1)} %copy-done.5), channel_id=1, source_target_pairs={{0,8},{8,16},{16,24},{1,9},{9,17},{17,25},{2,10},{10,18},{18,26},{... | collective-permute-start | bytes 1179656 | tf_op jit(solution)/shard_map/ppermute | solution.py:32
  74.6 0.0 copy-done.2
  74.6 6.7 %backward.1.sums_ref = f32[256,64]{1,0:T(8,128)} custom-call(s32[8]{0:T(128)} %ids_ref.5, bf16[8,8,8,256]{3,2,1,0:T(8,128)(2,1)} %copy-done.2, bf16[16,256,2048]{2,1,0:T(8,128)(2,1)} %weights_hbm.3), custom_call_target="tpu_custom_call" | custom-call | flops 536870912 | bytes 8388608 | tf_op jit(solution)/shard_map/backward/pallas_call | solution.py:521
  81.3 0.0 copy-start.4
  81.3 1.0 all-to-all-done.3.given_ref
  82.4 1.0 probe_rows.1
  83.4 0.4 collective-permute-done.4
  83.8 5.9 %all-to-all-start.4 = ((f32[32,16,256]{2,1,0:T(8,128)}), f32[32,16,256]{2,1,0:T(8,128)S(1)}, u32[]{:S(2)}, u32[]{:S(2)}) async-start(f32[32,16,256]{2,1,0:T(8,128)} %probe_rows.1), calls=%async_computation.4 | async-start | bytes 1048576 | tf_op jit(solution)/shard_map/all_to_all | solution.py:789
  89.6 0.0 copy-done.4
  89.6 0.0 copy-start.1
  89.6 1.4 %collective-permute-start.5 = (f32[2,384,128]{2,1,0:T(8,128)S(1)}, f32[2,384,128]{2,1,0:T(8,128)S(1)}, u32[]{:S(2)}, u32[]{:S(2)}) collective-permute-start(f32[2,384,128]{2,1,0:T(8,128)S(1)} %copy-done.4), channel_id=1, source_target_pairs={{8,0},{16,8},{24,16},{9,1},{17,9},{25,17},{10,2},{18,10},{26,18},{... | collective-permute-start | bytes 1179656 | tf_op jit(solution)/shard_map/ppermute | solution.py:32
  91.1 11.7 %update.1 = f32[8,256,2048]{2,1,0:T(8,128)} custom-call(s32[8]{0:T(128)} %ids_ref.5, f32[256,64]{1,0:T(8,128)} %backward.1.sums_ref, f32[16,2048]{1,0:T(8,128)} %rays_hbm.3, f32[8,256,2048]{2,1,0:T(8,128)} %volume_hbm.3), custom_call_target="tpu_custom_call" | custom-call | flops 2147483648 | bytes 33554432 | tf_op jit(solution)/shard_map/update/pallas_call | solution.py:611
  102.8 3.8 %collective-permute-done.5 = f32[2,384,128]{2,1,0:T(8,128)S(1)} collective-permute-done((f32[2,384,128]{2,1,0:T(8,128)S(1)}, f32[2,384,128]{2,1,0:T(8,128)S(1)}, u32[]{:S(2)}, u32[]{:S(2)}) %collective-permute-start.5) | collective-permute-done | bytes 393248 | tf_op jit(solution)/shard_map/ppermute | solution.py:32
  106.5 0.0 copy-done.1
  106.5 0.0 copy-start.3
  106.5 1.3 %add_bitcast_fusion = f32[1,2,384,512]{3,2,1,0:T(8,128)} fusion(f32[2,384,128]{2,1,0:T(8,128)S(1)} %collective-permute-done.5, f32[2,384,512]{2,1,0:T(8,128)S(1)} %copy-done.1, f32[2,384,128]{2,1,0:T(8,128)S(1)} %collective-permute-done.4), kind=kLoop, calls=%fused_computation | loop fusion | flops 786432 | bytes 3932160 | tf_op jit(solution)/shard_map/broadcast_in_dim | solution.py:799
  107.9 0.0 all-to-all-done.4
  107.9 0.0 copy-done.3
  107.9 0.9 bitcast_add_fusion
  (3 shorter events, 0.1 us)
Async XLA Ops:
  1.8 24.9 %collective-permute-start.1 = (f32[2,384,128]{2,1,0:T(8,128)S(1)}, f32[2,384,128]{2,1,0:T(8,128)S(1)}, u32[]{:S(2)}, u32[]{:S(2)}) collective-permute-start(f32[2,384,128]{2,1,0:T(8,128)S(1)} %get-tuple-element.59), channel_id=1, source_target_pairs={{8,0},{16,8},{24,16},{9,1},{17,9},{25,17},{10,2},{18,10},{26,18},{... | collective-permute-start | bytes 1179656 | tf_op jit(solution)/shard_map/ppermute | solution.py:32
  3.1 23.7 %collective-permute-start = (f32[2,384,128]{2,1,0:T(8,128)S(1)}, f32[2,384,128]{2,1,0:T(8,128)S(1)}, u32[]{:S(2)}, u32[]{:S(2)}) collective-permute-start(f32[2,384,128]{2,1,0:T(8,128)S(1)} %get-tuple-element.60), channel_id=1, source_target_pairs={{0,8},{8,16},{16,24},{1,9},{9,17},{17,25},{2,10},{10,18},{18,26},{... | collective-permute-start | bytes 1179656 | tf_op jit(solution)/shard_map/ppermute | solution.py:32
  21.9 15.4 %all-to-all-start = ((f32[8,8,8,256]{3,2,1,0:T(8,128)}), f32[8,8,8,256]{3,2,1,0:T(8,128)S(1)}, u32[]{:S(2)}, u32[]{:S(2)}) async-start(f32[8,8,8,256]{3,2,1,0:T(8,128)} %forward.1), calls=%async_computation | async-start | bytes 1048576 | tf_op jit(solution)/shard_map/all_to_all | solution.py:732
  26.8 0.8 copy-start.6
  26.8 0.9 copy-start.7
  37.3 23.0 %copy-start = (f32[264,256]{1,0:T(8,128)S(1)}, f32[264,256]{1,0:T(8,128)}, u32[]{:S(2)}) copy-start(f32[264,256]{1,0:T(8,128)} %get-tuple-element.43.refs_0_) | copy-start | bytes 811012
  48.8 1.8 %collective-permute-start.3 = (f32[264,256]{1,0:T(8,128)}, f32[264,256]{1,0:T(8,128)S(1)}, u32[]{:S(2)}, u32[]{:S(2)}) collective-permute-start(f32[264,256]{1,0:T(8,128)} %get-tuple-element.41), channel_id=1, source_target_pairs={{0,4},{4,0},{1,5},{5,1},{2,6},{6,2},{3,7},{7,3},{8,12},{12,8},{9,1... | collective-permute-start | bytes 811016 | tf_op jit(solution)/shard_map/ppermute | solution.py:705
  49.0 21.9 %copy-start.5 = (f32[2,384,128]{2,1,0:T(8,128)S(1)}, f32[2,384,128]{2,1,0:T(8,128)}, u32[]{:S(2)}) copy-start(f32[2,384,128]{2,1,0:T(8,128)} %get-tuple-element.52) | copy-start | bytes 1179652
  49.0 0.8 collective-permute-start.2
  51.3 16.0 %all-to-all-start.2 = ((bf16[8,8,8,256]{3,2,1,0:T(8,128)(2,1)}), bf16[8,8,8,256]{3,2,1,0:T(8,128)(2,1)S(1)}, u32[]{:S(2)}, u32[]{:S(2)}) async-start(bf16[8,8,8,256]{3,2,1,0:T(8,128)(2,1)} %broadcast_in_dim.13), calls=%async_computation.2 | async-start | bytes 524288 | tf_op jit(solution)/shard_map/all_to_all | solution.py:775
  67.3 7.3 %copy-start.2 = (bf16[8,8,8,256]{3,2,1,0:T(8,128)(2,1)}, bf16[8,8,8,256]{3,2,1,0:T(8,128)(2,1)S(1)}, u32[]{:S(2)}) copy-start(bf16[8,8,8,256]{3,2,1,0:T(8,128)(2,1)S(1)} %all-to-all-done.2.residual_hbm) | copy-start | bytes 786436
  67.3 15.1 %all-to-all-start.3 = ((f32[16,40,128]{2,1,0:T(8,128)}), f32[16,40,128]{2,1,0:T(8,128)S(1)}, u32[]{:S(2)}, u32[]{:S(2)}) async-start(f32[16,40,128]{2,1,0:T(8,128)} %probe_parts.1), calls=%async_computation.3 | async-start | bytes 655360 | tf_op jit(solution)/shard_map/all_to_all | solution.py:780
  70.8 12.9 %collective-permute-start.4 = (f32[2,384,128]{2,1,0:T(8,128)S(1)}, f32[2,384,128]{2,1,0:T(8,128)S(1)}, u32[]{:S(2)}, u32[]{:S(2)}) collective-permute-start(f32[2,384,128]{2,1,0:T(8,128)S(1)} %copy-done.5), channel_id=1, source_target_pairs={{0,8},{8,16},{16,24},{1,9},{9,17},{17,25},{2,10},{10,18},{18,26},{... | collective-permute-start | bytes 1179656 | tf_op jit(solution)/shard_map/ppermute | solution.py:32
  81.3 8.3 %copy-start.4 = (f32[2,384,128]{2,1,0:T(8,128)S(1)}, f32[2,384,128]{2,1,0:T(8,128)}, u32[]{:S(2)}) copy-start(f32[2,384,128]{2,1,0:T(8,128)} %get-tuple-element.54) | copy-start | bytes 1179652
  83.8 24.1 %all-to-all-start.4 = ((f32[32,16,256]{2,1,0:T(8,128)}), f32[32,16,256]{2,1,0:T(8,128)S(1)}, u32[]{:S(2)}, u32[]{:S(2)}) async-start(f32[32,16,256]{2,1,0:T(8,128)} %probe_rows.1), calls=%async_computation.4 | async-start | bytes 1048576 | tf_op jit(solution)/shard_map/all_to_all | solution.py:789
  89.6 16.9 %copy-start.1 = (f32[2,384,512]{2,1,0:T(8,128)S(1)}, f32[2,384,512]{2,1,0:T(8,128)}, u32[]{:S(2)}) copy-start(f32[2,384,512]{2,1,0:T(8,128)} %get-tuple-element.33) | copy-start | bytes 4718596
  89.6 16.9 %collective-permute-start.5 = (f32[2,384,128]{2,1,0:T(8,128)S(1)}, f32[2,384,128]{2,1,0:T(8,128)S(1)}, u32[]{:S(2)}, u32[]{:S(2)}) collective-permute-start(f32[2,384,128]{2,1,0:T(8,128)S(1)} %copy-done.4), channel_id=1, source_target_pairs={{8,0},{16,8},{24,16},{9,1},{17,9},{25,17},{10,2},{18,10},{26,18},{... | collective-permute-start | bytes 1179656 | tf_op jit(solution)/shard_map/ppermute | solution.py:32
  106.5 1.3 %copy-start.3 = (f32[2,256,256]{2,1,0:T(8,128)S(1)}, f32[2,256,256]{2,1,0:T(8,128)}, u32[]{:S(2)}) copy-start(f32[2,256,256]{2,1,0:T(8,128)} %probe_hbm.1) | copy-start | bytes 1572868

commit v7 on v6

--- a/solution.py
+++ b/solution.py
@@ -15,7 +15,7 @@
 BF16 = jnp.bfloat16
 LANES = 128
 SUBLANES = 8
-AHEAD = 3
+AHEAD = 4
 UPDATE_AHEAD = 6
 SMALL_LIMIT = 16 * 1024 * 1024
 ANYWHERE = pl.BlockSpec(memory_space=pl.ANY)
@@ -99,44 +99,57 @@
         stacked.append(jnp.zeros((lanes - 2 * projections, width), F32))
     table_ref[...] = jnp.concatenate(stacked, axis=0).T.astype(BF16)
 
-    @pl.loop(0, depth)
-    def _(z):
-        volume_copy(z).wait()
-
-        @pl.when(z + AHEAD < depth)
-        def _():
-            volume_copy(z + AHEAD).start()
-
-        @pl.when(jnp.logical_and(z + AHEAD >= depth, z + AHEAD - depth < projections))
-        def _():
-            weights_copy(z + AHEAD - depth).start()
-
-        piece = min(512, width)
-        total = None
-        for k in range(0, width, piece):
-            block = volume_ref[z, :, k : k + piece]
-            high = block.astype(BF16)
-            low = (block - high.astype(F32)).astype(BF16)
-            stacked = jnp.concatenate([high, low], axis=0)
-            part = dot(stacked, table_ref[k : k + piece, :])
-            total = part if total is None else total + part
-        rows = volume_ref.shape[1]
-        total = (total[:rows] + total[rows:]).T
-        sums_ref[z] = total[:projections] + total[projections : 2 * projections]
-
-    @pl.loop(0, projections)
-    def _(a):
-        weights_copy(a).wait()
-
-        @pl.when(a + AHEAD < projections)
-        def _():
-            weights_copy(a + AHEAD).start()
-
-        rows = sums_ref[:, pl.ds(a, 1), :].reshape(depth, sums_ref.shape[2])
-        result = dot(rows.astype(BF16), weights_ref[a])
-        for part in range(parts):
-            out_ref[part, a] = result[:, part * share : (part + 1) * share]
-        out_copy(a).start()
+    rows = volume_ref.shape[1]
+    piece = min(512, width)
+    group = math.gcd(depth, 2)
+
+    @pl.loop(0, depth, step=group)
+    def _(first):
+        for z in range(group):
+            volume_copy(first + z).wait()
+        for z in range(group):
+            item = first + z + AHEAD
+
+            @pl.when(item < depth)
+            def _():
+                volume_copy(item).start()
+
+            @pl.when(jnp.logical_and(item >= depth, item - depth < projections))
+            def _():
+                weights_copy(item - depth).start()
+
+        for z in range(group):
+            total = None
+            for k in range(0, width, piece):
+                block = volume_ref[first + z, :, k : k + piece]
+                high = block.astype(BF16)
+                low = (block - high.astype(F32)).astype(BF16)
+                stacked = jnp.concatenate([high, low], axis=0)
+                part = dot(stacked, table_ref[k : k + piece, :])
+                total = part if total is None else total + part
+            total = (total[:rows] + total[rows:]).T
+            sums_ref[first + z] = total[:projections] + total[projections : 2 * projections]
+
+    members = math.gcd(projections, AHEAD)
+
+    @pl.loop(0, projections, step=members)
+    def _(first):
+        for a in range(members):
+            weights_copy(first + a).wait()
+        for a in range(members):
+            item = first + a + AHEAD
+
+            @pl.when(item < projections)
+            def _():
+                weights_copy(item).start()
+
+        for a in range(members):
+            sums = sums_ref[:, pl.ds(first + a, 1), :].reshape(depth, rows)
+            result = dot(sums.astype(BF16), weights_ref[first + a])
+            for part in range(parts):
+                out_ref[part, first + a] = result[:, part * share : (part + 1) * share]
+        for a in range(members):
+            out_copy(first + a).start()
 
     @pl.loop(0, projections)
     def _(a):
@@ -500,19 +513,27 @@
         turned_ref[part * share : (part + 1) * share, :] = block.T
     out_ref[...] = jnp.zeros(out_ref.shape, F32)
 
-    @pl.loop(0, projections)
-    def _(a):
-        weights_copy(a).wait()
-
-        @pl.when(a + AHEAD < projections)
-        def _():
-            weights_copy(a + AHEAD).start()
+    members = math.gcd(projections, 2)
+
+    @pl.loop(0, projections, step=members)
+    def _(first):
+        for a in range(members):
+            weights_copy(first + a).wait()
+        for a in range(members):
+            item = first + a + AHEAD
+
+            @pl.when(item < projections)
+            def _():
+                weights_copy(item).start()
 
         lane = lax.broadcasted_iota(jnp.int32, turned_ref.shape, 1)
-        begin = a * depth
-        kept = jnp.logical_and(lane >= begin, lane < begin + depth)
-        chosen = jnp.where(kept, turned_ref[...], 0.0).astype(BF16)
-        out_ref[...] += dot(weights_ref[a], chosen)
+        total = out_ref[...]
+        for a in range(members):
+            begin = (first + a) * depth
+            kept = jnp.logical_and(lane >= begin, lane < begin + depth)
+            chosen = jnp.where(kept, turned_ref[...], 0.0).astype(BF16)
+            total += dot(weights_ref[first + a], chosen)
+        out_ref[...] = total
 
 
 def backward_sums(angle_ids, residual, proj_weights):

time: 110 us -> 111 us (level); the launches traced: 109 us -> 109 us
  Pallas kernels: 43.1 us -> 41.4 us
  waiting for transfers between devices: 12.1 us -> 13.3 us
    pallas_call x1, Pallas kernels: 9.67 us -> 7.14 us  [patch_updates(): pl.pallas_call(patch_kernel, in_specs=[SCALARS] * 4 + [ANYWHERE] * 7, out...]
  transfers between devices with their start and end apart: 10 -> 10, of which waited for: 5 -> 6; matrix products, arithmetic and copies ran while one was open for 1% -> 1% of each run, Pallas kernels for 40% -> 38%
where the time goes in v7:
time: 111 us; the launch traced here: 109 us
  Pallas kernels  41.4 us (37%)
  starting transfers between devices  34.9 us (31%)
  waiting for transfers between devices  13.3 us (12%)
  blocking collectives  12.5 us (11%)
  local copies, waits for them, and re-layouts  2.77 us (2%)
  other arithmetic  2.23 us (2%)
  between operations  1.51 us (1%)
    pallas_call x1, Pallas kernels, forward_parts(): pl.pallas_call(forward_kernel, in_specs=[SCALARS] + [ANYWHERE] * 3, out_s...  14.2 us
    all_to_all x1, blocking collectives, on_device(): pieces = lax.all_to_all(pieces, ('proj', 'cuts'), 0, 0, tiled=True)  12.5 us
    ppermute x4, starting transfers between devices, shifted(): lax.ppermute(value, axis, [(source, source + steps) for source in range(l...  12 us
    pallas_call x1, Pallas kernels, volume_update(): pl.pallas_call(update_kernel, in_specs=[SCALARS, WHOLE] + [ANYWHERE] * 2,...  11.7 us
    all_to_all x1, starting transfers between devices, on_device(): residual = lax.all_to_all(copies, flat_axes, 0, 0, tiled=True)  8.49 us
    pallas_call x1, Pallas kernels, patch_updates(): pl.pallas_call(patch_kernel, in_specs=[SCALARS] * 4 + [ANYWHERE] * 7, out...  7.14 us
    pallas_call x1, Pallas kernels, backward_sums(): pl.pallas_call(backward_kernel, in_specs=[SCALARS, ANYWHERE, ANYWHERE], o...  6.61 us
    all_to_all x1, waiting for transfers between devices, on_device(): residual = lax.all_to_all(copies, flat_axes, 0, 0, tiled=True)  6.15 us
  transfers between devices with their start and end apart: 10, of which 6 were waited for; matrix products, arithmetic and copies ran while one was open for 1% of the time, Pallas kernels for 38%

profile of v7, /device:TPU:0, one launch (start us, length us, event | category | flops | bytes accessed | tf_op | source)
XLA Modules:
  0.0 108.6 jit_solution(3301323178886497567)
XLA Ops:
  0.6 1.2 %fusion = (f32[2,384,128]{2,1,0:T(8,128)S(1)}, f32[2,384,128]{2,1,0:T(8,128)S(1)}) fusion(f32[2,384,512]{2,1,0:T(8,128)} %bitcast.15), kind=kLoop, calls=%fused_computation.3 | loop fusion | bytes 1572864 | tf_op jit(solution)/shard_map/slice | solution.py:750
  1.8 1.3 %collective-permute-start.1 = (f32[2,384,128]{2,1,0:T(8,128)S(1)}, f32[2,384,128]{2,1,0:T(8,128)S(1)}, u32[]{:S(2)}, u32[]{:S(2)}) collective-permute-start(f32[2,384,128]{2,1,0:T(8,128)S(1)} %get-tuple-element.59), channel_id=1, source_target_pairs={{8,0},{16,8},{24,16},{9,1},{17,9},{25,17},{10,2},{18,10},{26,18},{... | collective-permute-start | bytes 1179656 | tf_op jit(solution)/shard_map/ppermute | solution.py:32
  3.1 5.5 %collective-permute-start = (f32[2,384,128]{2,1,0:T(8,128)S(1)}, f32[2,384,128]{2,1,0:T(8,128)S(1)}, u32[]{:S(2)}, u32[]{:S(2)}) collective-permute-start(f32[2,384,128]{2,1,0:T(8,128)S(1)} %get-tuple-element.60), channel_id=1, source_target_pairs={{0,8},{8,16},{16,24},{1,9},{9,17},{17,25},{2,10},{10,18},{18,26},{... | collective-permute-start | bytes 1179656 | tf_op jit(solution)/shard_map/ppermute | solution.py:32
  8.6 14.2 %forward.1 = f32[8,8,8,256]{3,2,1,0:T(8,128)} custom-call(s32[8]{0:T(128)} %ids_ref.5, f32[16,2048]{1,0:T(8,128)} %rays_hbm.3, f32[8,256,2048]{2,1,0:T(8,128)} %volume_hbm.3, bf16[16,256,2048]{2,1,0:T(8,128)(2,1)} %weights_hbm.3), custom_call_target="tpu_custom_call" | custom-call | flops 2147483648 | bytes 25165824 | tf_op jit(solution)/shard_map/forward/pallas_call | solution.py:164
  22.8 4.2 %all-to-all-start = ((f32[8,8,8,256]{3,2,1,0:T(8,128)}), f32[8,8,8,256]{3,2,1,0:T(8,128)S(1)}, u32[]{:S(2)}, u32[]{:S(2)}) async-start(f32[8,8,8,256]{3,2,1,0:T(8,128)} %forward.1), calls=%async_computation | async-start | bytes 1048576 | tf_op jit(solution)/shard_map/all_to_all | solution.py:753
  27.7 0.0 collective-permute-done.1.right_hbm
  27.7 0.0 copy-start.6
  27.7 0.0 collective-permute-done.left_hbm
  27.7 0.0 copy-start.7
  27.7 0.7 copy-done.6
  28.4 0.1 copy-done.7
  28.5 7.1 %patches.1 = (f32[2,384,512]{2,1,0:T(8,128)}, f32[2,384,128]{2,1,0:T(8,128)}, f32[2,384,128]{2,1,0:T(8,128)}, f32[2,4,8,384]{3,2,1,0:T(8,128)}, f32[264,256]{1,0:T(8,128)}, /*index=5*/f32[264,256]{1,0:T(8,128)}) custom-call(s32[6]{0:T(128)} %bitcast.20, s32[6]{0:T(128)} %bitcast.21, s32[1]{0:T(128)} %bitcast.13.count_ref, s32[1]{0:T(128)} %bitcast.3.place_ref, ...), custom_call_target="tpu_custom_call" | custom-call | flops 3221225472 | bytes 6291456 | tf_op jit(solution)/shard_map/patches/pallas_call | solution.py:439
  35.7 0.0 copy-start
  35.7 1.0 all-to-all-done
  36.7 12.5 %all_to_all.25 = f32[8,8,384]{2,1,0:T(8,128)S(1)} all-to-all(f32[8,8,384]{2,1,0:T(8,128)} %bitcast.17), channel_id=1, replica_groups=mesh['tile'=4,'proj'=2,'cuts'=4] {'proj','cuts'}, dimensions={0} | all-to-all | bytes 196608 | tf_op jit(solution)/shard_map/all_to_all | solution.py:775
  49.2 0.1 collective-permute-start.3
  49.3 0.0 copy-start.5
  49.3 0.8 collective-permute-start.2
  50.2 0.0 collective-permute-done.2
  50.2 0.8 collective-permute-done.3.refs_1_
  51.0 0.7 broadcast_in_dim.13
  51.7 8.5 %all-to-all-start.2 = ((bf16[8,8,8,256]{3,2,1,0:T(8,128)(2,1)}), bf16[8,8,8,256]{3,2,1,0:T(8,128)(2,1)S(1)}, u32[]{:S(2)}, u32[]{:S(2)}) async-start(bf16[8,8,8,256]{3,2,1,0:T(8,128)(2,1)} %broadcast_in_dim.13), calls=%async_computation.2 | async-start | bytes 524288 | tf_op jit(solution)/shard_map/all_to_all | solution.py:796
  60.2 0.0 copy-done
  60.2 0.8 probe_parts.1
  61.0 6.2 %all-to-all-done.2.residual_hbm = bf16[8,8,8,256]{3,2,1,0:T(8,128)(2,1)S(1)} async-done(((bf16[8,8,8,256]{3,2,1,0:T(8,128)(2,1)}), bf16[8,8,8,256]{3,2,1,0:T(8,128)(2,1)S(1)}, u32[]{:S(2)}, u32[]{:S(2)}) %all-to-all-start.2) | async-done | bytes 262176 | tf_op jit(solution)/shard_map/all_to_all | solution.py:796
  67.1 0.0 copy-start.2
  67.1 3.5 %all-to-all-start.3 = ((f32[16,40,128]{2,1,0:T(8,128)}), f32[16,40,128]{2,1,0:T(8,128)S(1)}, u32[]{:S(2)}, u32[]{:S(2)}) async-start(f32[16,40,128]{2,1,0:T(8,128)} %probe_parts.1), calls=%async_computation.3 | async-start | bytes 655360 | tf_op jit(solution)/shard_map/all_to_all | solution.py:801
  70.7 0.0 copy-done.5
  70.7 3.8 %collective-permute-start.4 = (f32[2,384,128]{2,1,0:T(8,128)S(1)}, f32[2,384,128]{2,1,0:T(8,128)S(1)}, u32[]{:S(2)}, u32[]{:S(2)}) collective-permute-start(f32[2,384,128]{2,1,0:T(8,128)S(1)} %copy-done.5), channel_id=1, source_target_pairs={{0,8},{8,16},{16,24},{1,9},{9,17},{17,25},{2,10},{10,18},{18,26},{... | collective-permute-start | bytes 1179656 | tf_op jit(solution)/shard_map/ppermute | solution.py:32
  74.4 0.0 copy-done.2
  74.4 6.6 %backward.1.sums_ref = f32[256,64]{1,0:T(8,128)} custom-call(s32[8]{0:T(128)} %ids_ref.5, bf16[8,8,8,256]{3,2,1,0:T(8,128)(2,1)} %copy-done.2, bf16[16,256,2048]{2,1,0:T(8,128)(2,1)} %weights_hbm.3), custom_call_target="tpu_custom_call" | custom-call | flops 536870912 | bytes 8388608 | tf_op jit(solution)/shard_map/backward/pallas_call | solution.py:542
  81.1 0.0 copy-start.4
  81.1 1.2 %all-to-all-done.3.given_ref = f32[16,40,128]{2,1,0:T(8,128)S(1)} async-done(((f32[16,40,128]{2,1,0:T(8,128)}), f32[16,40,128]{2,1,0:T(8,128)S(1)}, u32[]{:S(2)}, u32[]{:S(2)}) %all-to-all-start.3) | async-done | bytes 327712 | tf_op jit(solution)/shard_map/all_to_all | solution.py:801
  82.2 1.0 probe_rows.1
  83.2 0.4 collective-permute-done.4
  83.6 5.9 %all-to-all-start.4 = ((f32[32,16,256]{2,1,0:T(8,128)}), f32[32,16,256]{2,1,0:T(8,128)S(1)}, u32[]{:S(2)}, u32[]{:S(2)}) async-start(f32[32,16,256]{2,1,0:T(8,128)} %probe_rows.1), calls=%async_computation.4 | async-start | bytes 1048576 | tf_op jit(solution)/shard_map/all_to_all | solution.py:810
  89.5 0.0 copy-done.4
  89.5 0.0 copy-start.1
  89.5 1.4 %collective-permute-start.5 = (f32[2,384,128]{2,1,0:T(8,128)S(1)}, f32[2,384,128]{2,1,0:T(8,128)S(1)}, u32[]{:S(2)}, u32[]{:S(2)}) collective-permute-start(f32[2,384,128]{2,1,0:T(8,128)S(1)} %copy-done.4), channel_id=1, source_target_pairs={{8,0},{16,8},{24,16},{9,1},{17,9},{25,17},{10,2},{18,10},{26,18},{... | collective-permute-start | bytes 1179656 | tf_op jit(solution)/shard_map/ppermute | solution.py:32
  90.9 11.7 %update.1 = f32[8,256,2048]{2,1,0:T(8,128)} custom-call(s32[8]{0:T(128)} %ids_ref.5, f32[256,64]{1,0:T(8,128)} %backward.1.sums_ref, f32[16,2048]{1,0:T(8,128)} %rays_hbm.3, f32[8,256,2048]{2,1,0:T(8,128)} %volume_hbm.3), custom_call_target="tpu_custom_call" | custom-call | flops 2147483648 | bytes 33554432 | tf_op jit(solution)/shard_map/update/pallas_call | solution.py:632
  102.6 3.8 %collective-permute-done.5 = f32[2,384,128]{2,1,0:T(8,128)S(1)} collective-permute-done((f32[2,384,128]{2,1,0:T(8,128)S(1)}, f32[2,384,128]{2,1,0:T(8,128)S(1)}, u32[]{:S(2)}, u32[]{:S(2)}) %collective-permute-start.5) | collective-permute-done | bytes 393248 | tf_op jit(solution)/shard_map/ppermute | solution.py:32
  106.4 0.0 copy-done.1
  106.4 0.0 copy-start.3
  106.4 1.3 %add_bitcast_fusion = f32[1,2,384,512]{3,2,1,0:T(8,128)} fusion(f32[2,384,128]{2,1,0:T(8,128)S(1)} %collective-permute-done.5, f32[2,384,512]{2,1,0:T(8,128)S(1)} %copy-done.1, f32[2,384,128]{2,1,0:T(8,128)S(1)} %collective-permute-done.4), kind=kLoop, calls=%fused_computation | loop fusion | flops 786432 | bytes 3932160 | tf_op jit(solution)/shard_map/broadcast_in_dim | solution.py:820
  107.7 0.0 all-to-all-done.4
  107.7 0.0 copy-done.3
  107.7 0.9 bitcast_add_fusion
  (3 shorter events, 0.1 us)
Async XLA Ops:
  1.8 25.8 %collective-permute-start.1 = (f32[2,384,128]{2,1,0:T(8,128)S(1)}, f32[2,384,128]{2,1,0:T(8,128)S(1)}, u32[]{:S(2)}, u32[]{:S(2)}) collective-permute-start(f32[2,384,128]{2,1,0:T(8,128)S(1)} %get-tuple-element.59), channel_id=1, source_target_pairs={{8,0},{16,8},{24,16},{9,1},{17,9},{25,17},{10,2},{18,10},{26,18},{... | collective-permute-start | bytes 1179656 | tf_op jit(solution)/shard_map/ppermute | solution.py:32
  3.1 24.6 %collective-permute-start = (f32[2,384,128]{2,1,0:T(8,128)S(1)}, f32[2,384,128]{2,1,0:T(8,128)S(1)}, u32[]{:S(2)}, u32[]{:S(2)}) collective-permute-start(f32[2,384,128]{2,1,0:T(8,128)S(1)} %get-tuple-element.60), channel_id=1, source_target_pairs={{0,8},{8,16},{16,24},{1,9},{9,17},{17,25},{2,10},{10,18},{18,26},{... | collective-permute-start | bytes 1179656 | tf_op jit(solution)/shard_map/ppermute | solution.py:32
  22.8 13.9 %all-to-all-start = ((f32[8,8,8,256]{3,2,1,0:T(8,128)}), f32[8,8,8,256]{3,2,1,0:T(8,128)S(1)}, u32[]{:S(2)}, u32[]{:S(2)}) async-start(f32[8,8,8,256]{3,2,1,0:T(8,128)} %forward.1), calls=%async_computation | async-start | bytes 1048576 | tf_op jit(solution)/shard_map/all_to_all | solution.py:753
  27.7 0.8 copy-start.6
  27.7 0.9 copy-start.7
  35.7 24.5 %copy-start = (f32[264,256]{1,0:T(8,128)S(1)}, f32[264,256]{1,0:T(8,128)}, u32[]{:S(2)}) copy-start(f32[264,256]{1,0:T(8,128)} %get-tuple-element.43.refs_0_) | copy-start | bytes 811012
  49.2 1.8 %collective-permute-start.3 = (f32[264,256]{1,0:T(8,128)}, f32[264,256]{1,0:T(8,128)S(1)}, u32[]{:S(2)}, u32[]{:S(2)}) collective-permute-start(f32[264,256]{1,0:T(8,128)} %get-tuple-element.41), channel_id=1, source_target_pairs={{0,4},{4,0},{1,5},{5,1},{2,6},{6,2},{3,7},{7,3},{8,12},{12,8},{9,1... | collective-permute-start | bytes 811016 | tf_op jit(solution)/shard_map/ppermute | solution.py:726
  49.3 21.3 %copy-start.5 = (f32[2,384,128]{2,1,0:T(8,128)S(1)}, f32[2,384,128]{2,1,0:T(8,128)}, u32[]{:S(2)}) copy-start(f32[2,384,128]{2,1,0:T(8,128)} %get-tuple-element.52) | copy-start | bytes 1179652
  49.3 0.8 collective-permute-start.2
  51.7 15.4 %all-to-all-start.2 = ((bf16[8,8,8,256]{3,2,1,0:T(8,128)(2,1)}), bf16[8,8,8,256]{3,2,1,0:T(8,128)(2,1)S(1)}, u32[]{:S(2)}, u32[]{:S(2)}) async-start(bf16[8,8,8,256]{3,2,1,0:T(8,128)(2,1)} %broadcast_in_dim.13), calls=%async_computation.2 | async-start | bytes 524288 | tf_op jit(solution)/shard_map/all_to_all | solution.py:796
  67.1 7.3 %copy-start.2 = (bf16[8,8,8,256]{3,2,1,0:T(8,128)(2,1)}, bf16[8,8,8,256]{3,2,1,0:T(8,128)(2,1)S(1)}, u32[]{:S(2)}) copy-start(bf16[8,8,8,256]{3,2,1,0:T(8,128)(2,1)S(1)} %all-to-all-done.2.residual_hbm) | copy-start | bytes 786436
  67.1 15.1 %all-to-all-start.3 = ((f32[16,40,128]{2,1,0:T(8,128)}), f32[16,40,128]{2,1,0:T(8,128)S(1)}, u32[]{:S(2)}, u32[]{:S(2)}) async-start(f32[16,40,128]{2,1,0:T(8,128)} %probe_parts.1), calls=%async_computation.3 | async-start | bytes 655360 | tf_op jit(solution)/shard_map/all_to_all | solution.py:801
  70.7 12.9 %collective-permute-start.4 = (f32[2,384,128]{2,1,0:T(8,128)S(1)}, f32[2,384,128]{2,1,0:T(8,128)S(1)}, u32[]{:S(2)}, u32[]{:S(2)}) collective-permute-start(f32[2,384,128]{2,1,0:T(8,128)S(1)} %copy-done.5), channel_id=1, source_target_pairs={{0,8},{8,16},{16,24},{1,9},{9,17},{17,25},{2,10},{10,18},{18,26},{... | collective-permute-start | bytes 1179656 | tf_op jit(solution)/shard_map/ppermute | solution.py:32
  81.1 8.4 %copy-start.4 = (f32[2,384,128]{2,1,0:T(8,128)S(1)}, f32[2,384,128]{2,1,0:T(8,128)}, u32[]{:S(2)}) copy-start(f32[2,384,128]{2,1,0:T(8,128)} %get-tuple-element.54) | copy-start | bytes 1179652
  83.6 24.1 %all-to-all-start.4 = ((f32[32,16,256]{2,1,0:T(8,128)}), f32[32,16,256]{2,1,0:T(8,128)S(1)}, u32[]{:S(2)}, u32[]{:S(2)}) async-start(f32[32,16,256]{2,1,0:T(8,128)} %probe_rows.1), calls=%async_computation.4 | async-start | bytes 1048576 | tf_op jit(solution)/shard_map/all_to_all | solution.py:810
  89.5 16.9 %copy-start.1 = (f32[2,384,512]{2,1,0:T(8,128)S(1)}, f32[2,384,512]{2,1,0:T(8,128)}, u32[]{:S(2)}) copy-start(f32[2,384,512]{2,1,0:T(8,128)} %get-tuple-element.33) | copy-start | bytes 4718596
  89.5 16.9 %collective-permute-start.5 = (f32[2,384,128]{2,1,0:T(8,128)S(1)}, f32[2,384,128]{2,1,0:T(8,128)S(1)}, u32[]{:S(2)}, u32[]{:S(2)}) collective-permute-start(f32[2,384,128]{2,1,0:T(8,128)S(1)} %copy-done.4), channel_id=1, source_target_pairs={{8,0},{16,8},{24,16},{9,1},{17,9},{25,17},{10,2},{18,10},{26,18},{... | collective-permute-start | bytes 1179656 | tf_op jit(solution)/shard_map/ppermute | solution.py:32
  106.4 1.3 %copy-start.3 = (f32[2,256,256]{2,1,0:T(8,128)S(1)}, f32[2,256,256]{2,1,0:T(8,128)}, u32[]{:S(2)}) copy-start(f32[2,256,256]{2,1,0:T(8,128)} %probe_hbm.1) | copy-start | bytes 1572868

commit v8 on v6

--- a/solution.py
+++ b/solution.py
@@ -15,8 +15,9 @@
 BF16 = jnp.bfloat16
 LANES = 128
 SUBLANES = 8
-AHEAD = 3
+AHEAD = 4
 UPDATE_AHEAD = 6
+FORWARD_LIMIT = 44 * 1024 * 1024
 SMALL_LIMIT = 16 * 1024 * 1024
 ANYWHERE = pl.BlockSpec(memory_space=pl.ANY)
 WHOLE = pl.BlockSpec(memory_space=pltpu.VMEM)
@@ -165,7 +166,7 @@
             pltpu.SemaphoreType.DMA((projections,)),
             pltpu.SemaphoreType.DMA((projections,)),
         ],
-        compiler_params=pltpu.CompilerParams(vmem_limit_bytes=VMEM_LIMIT),
+        compiler_params=pltpu.CompilerParams(vmem_limit_bytes=FORWARD_LIMIT),
         cost_estimate=pl.CostEstimate(
             flops=4 * depth * rows * width * lanes,
             bytes_accessed=depth * rows * width * 4 + projections * rows * width * 2,
@@ -390,8 +391,8 @@
         last_copies.append(copy)
     for c in range(2):
         new_ref[c] = ext_ref[c, inner, mid] + sum_ref[c, inner, mid] * wide
-        edge_left_ref[c] = sum_ref[c, inner, :margin] * scale
-        edge_right_ref[c] = sum_ref[c, inner, far_side] * scale
+        edge_left_ref[c] = (sum_ref[c, inner, :margin] * scale).astype(BF16)
+        edge_right_ref[c] = (sum_ref[c, inner, far_side] * scale).astype(BF16)
     for k, (source, target) in enumerate(
         ((new_ref, new_hbm), (edge_left_ref, edge_left_hbm), (edge_right_ref, edge_right_hbm))
     ):
@@ -429,8 +430,8 @@
         out_specs=[ANYWHERE] * (4 + shares),
         out_shape=[
             shape((2, height, tile_cols), F32),
-            shape((2, height, margin), F32),
-            shape((2, height, margin), F32),
+            shape((2, height, margin), BF16),
+            shape((2, height, margin), BF16),
             shape(slab_shape, F32),
         ]
         + [shape((part_rows, side), F32)] * shares,
@@ -442,8 +443,8 @@
             VMEM((2 * side, 2 * side), BF16),
             VMEM(dual.shape, F32),
             VMEM((2, height, tile_cols), F32),
-            VMEM((2, height, margin), F32),
-            VMEM((2, height, margin), F32),
+            VMEM((2, height, margin), BF16),
+            VMEM((2, height, margin), BF16),
             VMEM(slab_shape, F32),
             VMEM((shares, part_rows, side), F32),
             VMEM((2, height + SUBLANES, extent), F32),
@@ -500,19 +501,27 @@
         turned_ref[part * share : (part + 1) * share, :] = block.T
     out_ref[...] = jnp.zeros(out_ref.shape, F32)
 
-    @pl.loop(0, projections)
-    def _(a):
-        weights_copy(a).wait()
-
-        @pl.when(a + AHEAD < projections)
-        def _():
-            weights_copy(a + AHEAD).start()
+    members = math.gcd(projections, 2)
+
+    @pl.loop(0, projections, step=members)
+    def _(first):
+        for a in range(members):
+            weights_copy(first + a).wait()
+        for a in range(members):
+            item = first + a + AHEAD
+
+            @pl.when(item < projections)
+            def _():
+                weights_copy(item).start()
 
         lane = lax.broadcasted_iota(jnp.int32, turned_ref.shape, 1)
-        begin = a * depth
-        kept = jnp.logical_and(lane >= begin, lane < begin + depth)
-        chosen = jnp.where(kept, turned_ref[...], 0.0).astype(BF16)
-        out_ref[...] += dot(weights_ref[a], chosen)
+        total = out_ref[...]
+        for a in range(members):
+            begin = (first + a) * depth
+            kept = jnp.logical_and(lane >= begin, lane < begin + depth)
+            chosen = jnp.where(kept, turned_ref[...], 0.0).astype(BF16)
+            total += dot(weights_ref[first + a], chosen)
+        out_ref[...] = total
 
 
 def backward_sums(angle_ids, residual, proj_weights):
@@ -793,8 +802,8 @@
     rest = tile_cols - margin
     new_object = (
         partial_object
-        + jnp.pad(edge_from_left, ((0, 0), (0, 0), (0, rest)))
-        + jnp.pad(edge_from_right, ((0, 0), (0, 0), (rest, 0)))
+        + jnp.pad(edge_from_left.astype(F32), ((0, 0), (0, 0), (0, rest)))
+        + jnp.pad(edge_from_right.astype(F32), ((0, 0), (0, 0), (rest, 0)))
     )
     return (new_object[None], new_probe, new_volume)
 

time: 110 us -> 104 us (0.945); the launches traced: 109 us -> 102 us
  starting transfers between devices: 35.4 us -> 29.5 us
  blocking collectives: 11.5 us -> 14.1 us
  waiting for transfers between devices: 12.1 us -> 9.86 us
  Pallas kernels: 43.1 us -> 41.5 us
    ppermute x4, waiting for transfers between devices: 4.16 us -> 0.01 us  [shifted(): lax.ppermute(value, axis, [(source, source + steps) for source in range(l...]
    all_to_all x1, starting transfers between devices: 9.01 us -> 5.49 us  [on_device(): residual = lax.all_to_all(copies, flat_axes, 0, 0, tiled=True)]
    all_to_all x1, blocking collectives: 11.5 us -> 14.1 us  [on_device(): pieces = lax.all_to_all(pieces, ('proj', 'cuts'), 0, 0, tiled=True)]
    all_to_all x1, starting transfers between devices: 5.86 us -> 3.43 us  [on_device(): steps = lax.all_to_all(steps, ('proj', 'tile', 'cuts'), 0, 0, tiled=True)]
    all_to_all x1, waiting for transfers between devices: 0.01 us -> 1.76 us  [on_device(): steps = lax.all_to_all(steps, ('proj', 'tile', 'cuts'), 0, 0, tiled=True)]
    pallas_call x1, Pallas kernels: 13.3 us -> 11.9 us  [forward_parts(): pl.pallas_call(forward_kernel, in_specs=[SCALARS] + [ANYWHERE] * 3, out_s...]
  transfers between devices with their start and end apart: 10 -> 10, of which waited for: 5 -> 4; matrix products, arithmetic and copies ran while one was open for 1% -> 1% of each run, Pallas kernels for 40% -> 41%
where the time goes in v8:
time: 104 us; the launch traced here: 102 us
  Pallas kernels  41.5 us (40%)
  starting transfers between devices  29.5 us (28%)
  blocking collectives  14.1 us (14%)
  waiting for transfers between devices  9.86 us (9%)
  local copies, waits for them, and re-layouts  2.82 us (3%)
  other arithmetic  2.24 us (2%)
  between operations  1.58 us (2%)
    all_to_all x1, blocking collectives, on_device(): pieces = lax.all_to_all(pieces, ('proj', 'cuts'), 0, 0, tiled=True)  14.1 us
    ppermute x4, starting transfers between devices, shifted(): lax.ppermute(value, axis, [(source, source + steps) for source in range(l...  11.9 us
    pallas_call x1, Pallas kernels, forward_parts(): pl.pallas_call(forward_kernel, in_specs=[SCALARS] + [ANYWHERE] * 3, out_s...  11.9 us
    pallas_call x1, Pallas kernels, volume_update(): pl.pallas_call(update_kernel, in_specs=[SCALARS, WHOLE] + [ANYWHERE] * 2,...  11.7 us
    pallas_call x1, Pallas kernels, patch_updates(): pl.pallas_call(patch_kernel, in_specs=[SCALARS] * 4 + [ANYWHERE] * 7, out...  9.56 us
    pallas_call x1, Pallas kernels, backward_sums(): pl.pallas_call(backward_kernel, in_specs=[SCALARS, ANYWHERE, ANYWHERE], o...  6.6 us
    all_to_all x1, waiting for transfers between devices, on_device(): residual = lax.all_to_all(copies, flat_axes, 0, 0, tiled=True)  6.15 us
    all_to_all x1, starting transfers between devices, on_device(): residual = lax.all_to_all(copies, flat_axes, 0, 0, tiled=True)  5.49 us
  transfers between devices with their start and end apart: 10, of which 4 were waited for; matrix products, arithmetic and copies ran while one was open for 1% of the time, Pallas kernels for 41%

profile of v8, /device:TPU:0, one launch (start us, length us, event | category | flops | bytes accessed | tf_op | source)
XLA Modules:
  0.0 101.6 jit_solution(10782352387409082488)
XLA Ops:
  0.6 0.0 copy-start.2
  0.6 0.0 copy-start
  0.7 1.2 %fusion = (f32[2,384,128]{2,1,0:T(8,128)S(1)}, f32[2,384,128]{2,1,0:T(8,128)S(1)}) fusion(f32[2,384,512]{2,1,0:T(8,128)} %bitcast.15), kind=kLoop, calls=%fused_computation.3 | loop fusion | bytes 1572864 | tf_op jit(solution)/shard_map/slice | solution.py:738
  1.9 1.3 %collective-permute-start.1 = (f32[2,384,128]{2,1,0:T(8,128)S(1)}, f32[2,384,128]{2,1,0:T(8,128)S(1)}, u32[]{:S(2)}, u32[]{:S(2)}) collective-permute-start(f32[2,384,128]{2,1,0:T(8,128)S(1)} %get-tuple-element.59), channel_id=1, source_target_pairs={{8,0},{16,8},{24,16},{9,1},{17,9},{25,17},{10,2},{18,10},{26,18},{... | collective-permute-start | bytes 1179656 | tf_op jit(solution)/shard_map/ppermute | solution.py:33
  3.2 5.5 %collective-permute-start = (f32[2,384,128]{2,1,0:T(8,128)S(1)}, f32[2,384,128]{2,1,0:T(8,128)S(1)}, u32[]{:S(2)}, u32[]{:S(2)}) collective-permute-start(f32[2,384,128]{2,1,0:T(8,128)S(1)} %get-tuple-element.60), channel_id=1, source_target_pairs={{0,8},{8,16},{16,24},{1,9},{9,17},{17,25},{2,10},{10,18},{18,26},{... | collective-permute-start | bytes 1179656 | tf_op jit(solution)/shard_map/ppermute | solution.py:33
  8.7 0.0 copy-done.2
  8.7 0.0 copy-done
  8.7 11.9 %forward.1 = f32[8,8,8,256]{3,2,1,0:T(8,128)} custom-call(s32[8]{0:T(128)S(1)} %copy-done.2, f32[16,2048]{1,0:T(8,128)S(1)} %copy-done, f32[8,256,2048]{2,1,0:T(8,128)} %volume_hbm.3, bf16[16,256,2048]{2,1,0:T(8,128)(2,1)} %weights_hbm.3), custom_call_target="tpu_custom_call" | custom-call | flops 2147483648 | bytes 25165824 | tf_op jit(solution)/shard_map/forward/pallas_call | solution.py:152
  20.6 4.2 %all-to-all-start = ((f32[8,8,8,256]{3,2,1,0:T(8,128)}), f32[8,8,8,256]{3,2,1,0:T(8,128)S(1)}, u32[]{:S(2)}, u32[]{:S(2)}) async-start(f32[8,8,8,256]{3,2,1,0:T(8,128)} %forward.1), calls=%async_computation | async-start | bytes 1048576 | tf_op jit(solution)/shard_map/all_to_all | solution.py:741
  25.4 0.0 collective-permute-done.1.right_hbm
  25.4 0.0 copy-start.6
  25.5 0.0 collective-permute-done.left_hbm
  25.5 0.0 copy-start.7
  25.5 0.7 copy-done.6
  26.2 0.1 copy-done.7
  26.3 9.6 %patches.1 = (f32[2,384,512]{2,1,0:T(8,128)}, bf16[2,384,128]{2,1,0:T(8,128)(2,1)}, bf16[2,384,128]{2,1,0:T(8,128)(2,1)}, f32[2,4,8,384]{3,2,1,0:T(8,128)}, f32[264,256]{1,0:T(8,128)}, /*index=5*/f32[264,256]{1,0:T(8,128)}) custom-call(s32[6]{0:T(128)} %bitcast.20, s32[6]{0:T(128)} %bitcast.21, s32[1]{0:T(128)} %bitcast.13.count_ref, s32[1]{0:T(128)} %bitcast.3.place_ref, ...), custom_call_target="tpu_custom_call" | custom-call | flops 3221225472 | bytes 6291456 | tf_op jit(solution)/shard_map/patches/pallas_call | solution.py:427
  35.9 0.0 copy-start.1
  35.9 0.0 all-to-all-done
  35.9 14.1 %all_to_all.25 = f32[8,8,384]{2,1,0:T(8,128)S(1)} all-to-all(f32[8,8,384]{2,1,0:T(8,128)} %bitcast.17), channel_id=1, replica_groups=mesh['tile'=4,'proj'=2,'cuts'=4] {'proj','cuts'}, dimensions={0} | all-to-all | bytes 196608 | tf_op jit(solution)/shard_map/all_to_all | solution.py:763
  50.0 0.1 collective-permute-start.3
  50.1 0.8 collective-permute-start.2
  51.0 0.0 collective-permute-done.2
  51.0 0.8 collective-permute-done.3.refs_1_
  51.8 0.7 broadcast_in_dim.13
  52.5 5.5 %all-to-all-start.2 = ((bf16[8,8,8,256]{3,2,1,0:T(8,128)(2,1)}), bf16[8,8,8,256]{3,2,1,0:T(8,128)(2,1)S(1)}, u32[]{:S(2)}, u32[]{:S(2)}) async-start(bf16[8,8,8,256]{3,2,1,0:T(8,128)(2,1)} %broadcast_in_dim.13), calls=%async_computation.2 | async-start | bytes 524288 | tf_op jit(solution)/shard_map/all_to_all | solution.py:784
  58.0 0.0 copy-done.1
  58.0 0.8 probe_parts.1
  58.8 6.2 %all-to-all-done.2.residual_hbm = bf16[8,8,8,256]{3,2,1,0:T(8,128)(2,1)S(1)} async-done(((bf16[8,8,8,256]{3,2,1,0:T(8,128)(2,1)}), bf16[8,8,8,256]{3,2,1,0:T(8,128)(2,1)S(1)}, u32[]{:S(2)}, u32[]{:S(2)}) %all-to-all-start.2) | async-done | bytes 262176 | tf_op jit(solution)/shard_map/all_to_all | solution.py:784
  64.9 3.5 %all-to-all-start.3 = ((f32[16,40,128]{2,1,0:T(8,128)}), f32[16,40,128]{2,1,0:T(8,128)S(1)}, u32[]{:S(2)}, u32[]{:S(2)}) async-start(f32[16,40,128]{2,1,0:T(8,128)} %probe_parts.1), calls=%async_computation.3 | async-start | bytes 655360 | tf_op jit(solution)/shard_map/all_to_all | solution.py:789
  68.5 0.0 copy-done.9
  68.5 3.7 %collective-permute-start.4 = (bf16[2,384,128]{2,1,0:T(8,128)(2,1)S(1)}, bf16[2,384,128]{2,1,0:T(8,128)(2,1)S(1)}, u32[]{:S(2)}, u32[]{:S(2)}) collective-permute-start(bf16[2,384,128]{2,1,0:T(8,128)(2,1)S(1)} %copy-done.9), channel_id=1, source_target_pairs={{0,8},{8,16},{16,24},{1,9},{9,17},{17,25},{2,10},{10,18},{18,26},{... | collective-permute-start | bytes 589832 | tf_op jit(solution)/shard_map/ppermute | solution.py:33
  72.2 0.0 copy-done.4
  72.2 6.6 %backward.1.sums_ref = f32[256,64]{1,0:T(8,128)} custom-call(s32[8]{0:T(128)} %ids_ref.5, bf16[8,8,8,256]{3,2,1,0:T(8,128)(2,1)} %copy-done.4, bf16[16,256,2048]{2,1,0:T(8,128)(2,1)} %weights_hbm.3), custom_call_target="tpu_custom_call" | custom-call | flops 536870912 | bytes 8388608 | tf_op jit(solution)/shard_map/backward/pallas_call | solution.py:530
  78.8 0.0 copy-start.8
  78.9 1.2 %all-to-all-done.3.given_ref = f32[16,40,128]{2,1,0:T(8,128)S(1)} async-done(((f32[16,40,128]{2,1,0:T(8,128)}), f32[16,40,128]{2,1,0:T(8,128)S(1)}, u32[]{:S(2)}, u32[]{:S(2)}) %all-to-all-start.3) | async-done | bytes 327712 | tf_op jit(solution)/shard_map/all_to_all | solution.py:789
  80.0 1.0 probe_rows.1
  81.0 0.0 collective-permute-done.4
  81.0 3.4 %all-to-all-start.4 = ((f32[32,16,256]{2,1,0:T(8,128)}), f32[32,16,256]{2,1,0:T(8,128)S(1)}, u32[]{:S(2)}, u32[]{:S(2)}) async-start(f32[32,16,256]{2,1,0:T(8,128)} %probe_rows.1), calls=%async_computation.4 | async-start | bytes 1048576 | tf_op jit(solution)/shard_map/all_to_all | solution.py:798
  84.5 0.0 copy-done.8
  84.5 0.0 copy-start.3
  84.5 1.4 %collective-permute-start.5 = (bf16[2,384,128]{2,1,0:T(8,128)(2,1)S(1)}, bf16[2,384,128]{2,1,0:T(8,128)(2,1)S(1)}, u32[]{:S(2)}, u32[]{:S(2)}) collective-permute-start(bf16[2,384,128]{2,1,0:T(8,128)(2,1)S(1)} %copy-done.8), channel_id=1, source_target_pairs={{8,0},{16,8},{24,16},{9,1},{17,9},{25,17},{10,2},{18,10},{26,18},{... | collective-permute-start | bytes 589832 | tf_op jit(solution)/shard_map/ppermute | solution.py:33
  85.9 11.7 %update.1 = f32[8,256,2048]{2,1,0:T(8,128)} custom-call(s32[8]{0:T(128)} %ids_ref.5, f32[256,64]{1,0:T(8,128)} %backward.1.sums_ref, f32[16,2048]{1,0:T(8,128)} %rays_hbm.3, f32[8,256,2048]{2,1,0:T(8,128)} %volume_hbm.3), custom_call_target="tpu_custom_call" | custom-call | flops 2147483648 | bytes 33554432 | tf_op jit(solution)/shard_map/update/pallas_call | solution.py:620
  97.6 0.0 collective-permute-done.5
  97.6 0.0 copy-done.3
  97.6 0.0 copy-start.5
  97.6 1.3 %add_bitcast_fusion = f32[1,2,384,512]{3,2,1,0:T(8,128)} fusion(f32[2,384,512]{2,1,0:T(8,128)S(1)} %copy-done.3, bf16[2,384,128]{2,1,0:T(8,128)(2,1)S(1)} %collective-permute-done.5, bf16[2,384,128]{2,1,0:T(8,128)(2,1)S(1)} %collective-permute-done.4), kind=kLoop, calls=%fused_computation | loop fusion | flops 1572864 | bytes 3538944 | tf_op jit(solution)/shard_map/broadcast_in_dim | solution.py:808
  99.0 1.8 %all-to-all-done.4 = f32[32,16,256]{2,1,0:T(8,128)S(1)} async-done(((f32[32,16,256]{2,1,0:T(8,128)}), f32[32,16,256]{2,1,0:T(8,128)S(1)}, u32[]{:S(2)}, u32[]{:S(2)}) %all-to-all-start.4) | async-done | bytes 524320 | tf_op jit(solution)/shard_map/all_to_all | solution.py:798
  100.7 0.9 bitcast_add_fusion
  (6 shorter events, 0.1 us)
Async XLA Ops:
  0.6 8.0 %copy-start.2 = (s32[8]{0:T(128)S(1)}, s32[8]{0:T(128)}, u32[]{:S(2)}) copy-start(s32[8]{0:T(128)} %ids_ref.5) | copy-start | bytes 100
  0.6 8.0 %copy-start = (f32[16,2048]{1,0:T(8,128)S(1)}, f32[16,2048]{1,0:T(8,128)}, u32[]{:S(2)}) copy-start(f32[16,2048]{1,0:T(8,128)} %rays_hbm.3) | copy-start | bytes 393220
  1.9 23.6 %collective-permute-start.1 = (f32[2,384,128]{2,1,0:T(8,128)S(1)}, f32[2,384,128]{2,1,0:T(8,128)S(1)}, u32[]{:S(2)}, u32[]{:S(2)}) collective-permute-start(f32[2,384,128]{2,1,0:T(8,128)S(1)} %get-tuple-element.59), channel_id=1, source_target_pairs={{8,0},{16,8},{24,16},{9,1},{17,9},{25,17},{10,2},{18,10},{26,18},{... | collective-permute-start | bytes 1179656 | tf_op jit(solution)/shard_map/ppermute | solution.py:33
  3.2 22.3 %collective-permute-start = (f32[2,384,128]{2,1,0:T(8,128)S(1)}, f32[2,384,128]{2,1,0:T(8,128)S(1)}, u32[]{:S(2)}, u32[]{:S(2)}) collective-permute-start(f32[2,384,128]{2,1,0:T(8,128)S(1)} %get-tuple-element.60), channel_id=1, source_target_pairs={{0,8},{8,16},{16,24},{1,9},{9,17},{17,25},{2,10},{10,18},{18,26},{... | collective-permute-start | bytes 1179656 | tf_op jit(solution)/shard_map/ppermute | solution.py:33
  20.6 15.3 %all-to-all-start = ((f32[8,8,8,256]{3,2,1,0:T(8,128)}), f32[8,8,8,256]{3,2,1,0:T(8,128)S(1)}, u32[]{:S(2)}, u32[]{:S(2)}) async-start(f32[8,8,8,256]{3,2,1,0:T(8,128)} %forward.1), calls=%async_computation | async-start | bytes 1048576 | tf_op jit(solution)/shard_map/all_to_all | solution.py:741
  25.4 0.7 copy-start.6
  25.5 0.9 copy-start.7
  35.9 22.1 %copy-start.1 = (f32[264,256]{1,0:T(8,128)S(1)}, f32[264,256]{1,0:T(8,128)}, u32[]{:S(2)}) copy-start(f32[264,256]{1,0:T(8,128)} %get-tuple-element.43.refs_0_) | copy-start | bytes 811012
  50.0 1.8 %collective-permute-start.3 = (f32[264,256]{1,0:T(8,128)}, f32[264,256]{1,0:T(8,128)S(1)}, u32[]{:S(2)}, u32[]{:S(2)}) collective-permute-start(f32[264,256]{1,0:T(8,128)} %get-tuple-element.41), channel_id=1, source_target_pairs={{0,4},{4,0},{1,5},{5,1},{2,6},{6,2},{3,7},{7,3},{8,12},{12,8},{9,1... | collective-permute-start | bytes 811016 | tf_op jit(solution)/shard_map/ppermute | solution.py:714
  50.1 18.3 %copy-start.9 = (bf16[2,384,128]{2,1,0:T(8,128)(2,1)S(1)}, bf16[2,384,128]{2,1,0:T(8,128)(2,1)}, u32[]{:S(2)}) copy-start(bf16[2,384,128]{2,1,0:T(8,128)(2,1)} %get-tuple-element.52) | copy-start | bytes 589828
  50.1 0.8 collective-permute-start.2
  52.5 12.4 %all-to-all-start.2 = ((bf16[8,8,8,256]{3,2,1,0:T(8,128)(2,1)}), bf16[8,8,8,256]{3,2,1,0:T(8,128)(2,1)S(1)}, u32[]{:S(2)}, u32[]{:S(2)}) async-start(bf16[8,8,8,256]{3,2,1,0:T(8,128)(2,1)} %broadcast_in_dim.13), calls=%async_computation.2 | async-start | bytes 524288 | tf_op jit(solution)/shard_map/all_to_all | solution.py:784
  64.9 7.3 %copy-start.4 = (bf16[8,8,8,256]{3,2,1,0:T(8,128)(2,1)}, bf16[8,8,8,256]{3,2,1,0:T(8,128)(2,1)S(1)}, u32[]{:S(2)}) copy-start(bf16[8,8,8,256]{3,2,1,0:T(8,128)(2,1)S(1)} %all-to-all-done.2.residual_hbm) | copy-start | bytes 786436
  64.9 15.1 %all-to-all-start.3 = ((f32[16,40,128]{2,1,0:T(8,128)}), f32[16,40,128]{2,1,0:T(8,128)S(1)}, u32[]{:S(2)}, u32[]{:S(2)}) async-start(f32[16,40,128]{2,1,0:T(8,128)} %probe_parts.1), calls=%async_computation.3 | async-start | bytes 655360 | tf_op jit(solution)/shard_map/all_to_all | solution.py:789
  68.5 12.5 %collective-permute-start.4 = (bf16[2,384,128]{2,1,0:T(8,128)(2,1)S(1)}, bf16[2,384,128]{2,1,0:T(8,128)(2,1)S(1)}, u32[]{:S(2)}, u32[]{:S(2)}) collective-permute-start(bf16[2,384,128]{2,1,0:T(8,128)(2,1)S(1)} %copy-done.9), channel_id=1, source_target_pairs={{0,8},{8,16},{16,24},{1,9},{9,17},{17,25},{2,10},{10,18},{18,26},{... | collective-permute-start | bytes 589832 | tf_op jit(solution)/shard_map/ppermute | solution.py:33
  78.8 5.6 %copy-start.8 = (bf16[2,384,128]{2,1,0:T(8,128)(2,1)S(1)}, bf16[2,384,128]{2,1,0:T(8,128)(2,1)}, u32[]{:S(2)}) copy-start(bf16[2,384,128]{2,1,0:T(8,128)(2,1)} %get-tuple-element.54) | copy-start | bytes 589828
  81.0 19.7 %all-to-all-start.4 = ((f32[32,16,256]{2,1,0:T(8,128)}), f32[32,16,256]{2,1,0:T(8,128)S(1)}, u32[]{:S(2)}, u32[]{:S(2)}) async-start(f32[32,16,256]{2,1,0:T(8,128)} %probe_rows.1), calls=%async_computation.4 | async-start | bytes 1048576 | tf_op jit(solution)/shard_map/all_to_all | solution.py:798
  84.5 13.1 %copy-start.3 = (f32[2,384,512]{2,1,0:T(8,128)S(1)}, f32[2,384,512]{2,1,0:T(8,128)}, u32[]{:S(2)}) copy-start(f32[2,384,512]{2,1,0:T(8,128)} %get-tuple-element.33) | copy-start | bytes 4718596
  84.5 13.1 %collective-permute-start.5 = (bf16[2,384,128]{2,1,0:T(8,128)(2,1)S(1)}, bf16[2,384,128]{2,1,0:T(8,128)(2,1)S(1)}, u32[]{:S(2)}, u32[]{:S(2)}) collective-permute-start(bf16[2,384,128]{2,1,0:T(8,128)(2,1)S(1)} %copy-done.8), channel_id=1, source_target_pairs={{8,0},{16,8},{24,16},{9,1},{17,9},{25,17},{10,2},{18,10},{26,18},{... | collective-permute-start | bytes 589832 | tf_op jit(solution)/shard_map/ppermute | solution.py:33
  97.6 3.1 %copy-start.5 = (f32[2,256,256]{2,1,0:T(8,128)S(1)}, f32[2,256,256]{2,1,0:T(8,128)}, u32[]{:S(2)}) copy-start(f32[2,256,256]{2,1,0:T(8,128)} %probe_hbm.1) | copy-start | bytes 1572868

commit v9 on v8

--- a/solution.py
+++ b/solution.py
@@ -17,6 +17,7 @@
 SUBLANES = 8
 AHEAD = 4
 UPDATE_AHEAD = 6
+TOMO_LIMIT = 50 * 1024 * 1024
 FORWARD_LIMIT = 44 * 1024 * 1024
 SMALL_LIMIT = 16 * 1024 * 1024
 ANYWHERE = pl.BlockSpec(memory_space=pl.ANY)
@@ -539,7 +540,7 @@
             DMA,
             pltpu.SemaphoreType.DMA((projections,)),
         ],
-        compiler_params=pltpu.CompilerParams(vmem_limit_bytes=VMEM_LIMIT),
+        compiler_params=pltpu.CompilerParams(vmem_limit_bytes=TOMO_LIMIT),
         cost_estimate=pl.CostEstimate(
             flops=2 * rows * width * projections * projections * depth,
             bytes_accessed=projections * rows * width * 2,
@@ -632,7 +633,7 @@
             pltpu.SemaphoreType.DMA((depth,)),
             pltpu.SemaphoreType.DMA((slots,)),
         ],
-        compiler_params=pltpu.CompilerParams(vmem_limit_bytes=VMEM_LIMIT),
+        compiler_params=pltpu.CompilerParams(vmem_limit_bytes=TOMO_LIMIT),
         cost_estimate=pl.CostEstimate(
             flops=8 * rows * width * sums.shape[1] * depth,
             bytes_accessed=2 * depth * rows * width * 4,

time: 104 us -> 104 us (level); the launches traced: 102 us -> 103 us
  starting transfers between devices: 29.5 us -> 33.5 us
  blocking collectives: 14.1 us -> 11.5 us
    all_to_all x1, starting transfers between devices: 5.49 us -> 10.3 us  [on_device(): residual = lax.all_to_all(copies, flat_axes, 0, 0, tiled=True)]
    all_to_all x1, blocking collectives: 14.1 us -> 11.5 us  [on_device(): pieces = lax.all_to_all(pieces, ('proj', 'cuts'), 0, 0, tiled=True)]
    all_to_all x1, waiting for transfers between devices: 1.76 us -> 0.42 us  [on_device(): steps = lax.all_to_all(steps, ('proj', 'tile', 'cuts'), 0, 0, tiled=True)]
    pallas_call x1, Pallas kernels: 11.7 us -> 13 us  [volume_update(): pl.pallas_call(update_kernel, in_specs=[SCALARS, WHOLE] + [ANYWHERE] * 2,...]
    all_to_all x1, waiting for transfers between devices: 1.18 us -> 2.51 us  [on_device(): received = lax.all_to_all(by_receiver, group_axes, 0, 0, tiled=True)]
    pallas_call x1, Pallas kernels: 6.6 us -> 5.29 us  [backward_sums(): pl.pallas_call(backward_kernel, in_specs=[SCALARS, ANYWHERE, ANYWHERE], o...]
  transfers between devices with their start and end apart: 10 -> 10, of which waited for: 4 -> 4; matrix products, arithmetic and copies ran while one was open for 1% -> 1% of each run, Pallas kernels for 41% -> 40%
where the time goes in v9:
time: 104 us; the launch traced here: 103 us
  Pallas kernels  41.5 us (40%)
  starting transfers between devices  33.5 us (32%)
  blocking collectives  11.5 us (11%)
  waiting for transfers between devices  9.87 us (9%)
  local copies, waits for them, and re-layouts  2.82 us (3%)
  other arithmetic  2.24 us (2%)
  between operations  1.57 us (2%)
    pallas_call x1, Pallas kernels, volume_update(): pl.pallas_call(update_kernel, in_specs=[SCALARS, WHOLE] + [ANYWHERE] * 2,...  13 us
    ppermute x4, starting transfers between devices, shifted(): lax.ppermute(value, axis, [(source, source + steps) for source in range(l...  11.9 us
    pallas_call x1, Pallas kernels, forward_parts(): pl.pallas_call(forward_kernel, in_specs=[SCALARS] + [ANYWHERE] * 3, out_s...  11.9 us
    all_to_all x1, blocking collectives, on_device(): pieces = lax.all_to_all(pieces, ('proj', 'cuts'), 0, 0, tiled=True)  11.5 us
    all_to_all x1, starting transfers between devices, on_device(): residual = lax.all_to_all(copies, flat_axes, 0, 0, tiled=True)  10.3 us
    pallas_call x1, Pallas kernels, patch_updates(): pl.pallas_call(patch_kernel, in_specs=[SCALARS] * 4 + [ANYWHERE] * 7, out...  9.55 us
    all_to_all x1, waiting for transfers between devices, on_device(): residual = lax.all_to_all(copies, flat_axes, 0, 0, tiled=True)  6.16 us
    pallas_call x1, Pallas kernels, backward_sums(): pl.pallas_call(backward_kernel, in_specs=[SCALARS, ANYWHERE, ANYWHERE], o...  5.29 us
  transfers between devices with their start and end apart: 10, of which 4 were waited for; matrix products, arithmetic and copies ran while one was open for 1% of the time, Pallas kernels for 40%

profile of v9, /device:TPU:0, one launch (start us, length us, event | category | flops | bytes accessed | tf_op | source)
XLA Modules:
  0.0 103.0 jit_solution(13531442299169992339)
XLA Ops:
  0.6 0.0 copy-start.2
  0.6 0.0 copy-start
  0.7 1.2 %fusion = (f32[2,384,128]{2,1,0:T(8,128)S(1)}, f32[2,384,128]{2,1,0:T(8,128)S(1)}) fusion(f32[2,384,512]{2,1,0:T(8,128)} %bitcast.15), kind=kLoop, calls=%fused_computation.3 | loop fusion | bytes 1572864 | tf_op jit(solution)/shard_map/slice | solution.py:739
  1.9 1.3 %collective-permute-start.1 = (f32[2,384,128]{2,1,0:T(8,128)S(1)}, f32[2,384,128]{2,1,0:T(8,128)S(1)}, u32[]{:S(2)}, u32[]{:S(2)}) collective-permute-start(f32[2,384,128]{2,1,0:T(8,128)S(1)} %get-tuple-element.59), channel_id=1, source_target_pairs={{8,0},{16,8},{24,16},{9,1},{17,9},{25,17},{10,2},{18,10},{26,18},{... | collective-permute-start | bytes 1179656 | tf_op jit(solution)/shard_map/ppermute | solution.py:34
  3.2 5.5 %collective-permute-start = (f32[2,384,128]{2,1,0:T(8,128)S(1)}, f32[2,384,128]{2,1,0:T(8,128)S(1)}, u32[]{:S(2)}, u32[]{:S(2)}) collective-permute-start(f32[2,384,128]{2,1,0:T(8,128)S(1)} %get-tuple-element.60), channel_id=1, source_target_pairs={{0,8},{8,16},{16,24},{1,9},{9,17},{17,25},{2,10},{10,18},{18,26},{... | collective-permute-start | bytes 1179656 | tf_op jit(solution)/shard_map/ppermute | solution.py:34
  8.7 0.0 copy-done.2
  8.7 0.0 copy-done
  8.7 11.9 %forward.1 = f32[8,8,8,256]{3,2,1,0:T(8,128)} custom-call(s32[8]{0:T(128)S(1)} %copy-done.2, f32[16,2048]{1,0:T(8,128)S(1)} %copy-done, f32[8,256,2048]{2,1,0:T(8,128)} %volume_hbm.3, bf16[16,256,2048]{2,1,0:T(8,128)(2,1)} %weights_hbm.3), custom_call_target="tpu_custom_call" | custom-call | flops 2147483648 | bytes 25165824 | tf_op jit(solution)/shard_map/forward/pallas_call | solution.py:153
  20.6 4.2 %all-to-all-start = ((f32[8,8,8,256]{3,2,1,0:T(8,128)}), f32[8,8,8,256]{3,2,1,0:T(8,128)S(1)}, u32[]{:S(2)}, u32[]{:S(2)}) async-start(f32[8,8,8,256]{3,2,1,0:T(8,128)} %forward.1), calls=%async_computation | async-start | bytes 1048576 | tf_op jit(solution)/shard_map/all_to_all | solution.py:742
  25.4 0.0 collective-permute-done.1.right_hbm
  25.5 0.0 copy-start.5
  25.5 0.0 collective-permute-done.left_hbm
  25.5 0.0 copy-start.6
  25.5 0.7 copy-done.5
  26.2 0.1 copy-done.6
  26.3 9.5 %patches.1 = (f32[2,384,512]{2,1,0:T(8,128)}, bf16[2,384,128]{2,1,0:T(8,128)(2,1)}, bf16[2,384,128]{2,1,0:T(8,128)(2,1)}, f32[2,4,8,384]{3,2,1,0:T(8,128)}, f32[264,256]{1,0:T(8,128)}, /*index=5*/f32[264,256]{1,0:T(8,128)}) custom-call(s32[6]{0:T(128)} %bitcast.20, s32[6]{0:T(128)} %bitcast.21, s32[1]{0:T(128)} %bitcast.13.count_ref, s32[1]{0:T(128)} %bitcast.3.place_ref, ...), custom_call_target="tpu_custom_call" | custom-call | flops 3221225472 | bytes 6291456 | tf_op jit(solution)/shard_map/patches/pallas_call | solution.py:428
  35.9 0.0 copy-start.1
  35.9 0.0 all-to-all-done
  35.9 11.5 %all_to_all.25 = f32[8,8,384]{2,1,0:T(8,128)S(1)} all-to-all(f32[8,8,384]{2,1,0:T(8,128)} %bitcast.17), channel_id=1, replica_groups=mesh['tile'=4,'proj'=2,'cuts'=4] {'proj','cuts'}, dimensions={0} | all-to-all | bytes 196608 | tf_op jit(solution)/shard_map/all_to_all | solution.py:764
  47.4 0.1 collective-permute-start.3
  47.5 0.8 collective-permute-start.2
  48.4 0.0 collective-permute-done.2
  48.4 0.8 collective-permute-done.3.refs_1_
  49.2 0.7 broadcast_in_dim.13
  49.9 10.3 %all-to-all-start.2 = ((bf16[8,8,8,256]{3,2,1,0:T(8,128)(2,1)}), bf16[8,8,8,256]{3,2,1,0:T(8,128)(2,1)S(1)}, u32[]{:S(2)}, u32[]{:S(2)}) async-start(bf16[8,8,8,256]{3,2,1,0:T(8,128)(2,1)} %broadcast_in_dim.13), calls=%async_computation.2 | async-start | bytes 524288 | tf_op jit(solution)/shard_map/all_to_all | solution.py:785
  60.2 0.0 copy-done.1
  60.2 0.8 probe_parts.1
  61.0 6.2 %all-to-all-done.2.residual_hbm = bf16[8,8,8,256]{3,2,1,0:T(8,128)(2,1)S(1)} async-done(((bf16[8,8,8,256]{3,2,1,0:T(8,128)(2,1)}), bf16[8,8,8,256]{3,2,1,0:T(8,128)(2,1)S(1)}, u32[]{:S(2)}, u32[]{:S(2)}) %all-to-all-start.2) | async-done | bytes 262176 | tf_op jit(solution)/shard_map/all_to_all | solution.py:785
  67.1 3.5 %all-to-all-start.3 = ((f32[16,40,128]{2,1,0:T(8,128)}), f32[16,40,128]{2,1,0:T(8,128)S(1)}, u32[]{:S(2)}, u32[]{:S(2)}) async-start(f32[16,40,128]{2,1,0:T(8,128)} %probe_parts.1), calls=%async_computation.3 | async-start | bytes 655360 | tf_op jit(solution)/shard_map/all_to_all | solution.py:790
  70.7 0.0 copy-done.8
  70.7 3.7 %collective-permute-start.4 = (bf16[2,384,128]{2,1,0:T(8,128)(2,1)S(1)}, bf16[2,384,128]{2,1,0:T(8,128)(2,1)S(1)}, u32[]{:S(2)}, u32[]{:S(2)}) collective-permute-start(bf16[2,384,128]{2,1,0:T(8,128)(2,1)S(1)} %copy-done.8), channel_id=1, source_target_pairs={{0,8},{8,16},{16,24},{1,9},{9,17},{17,25},{2,10},{10,18},{18,26},{... | collective-permute-start | bytes 589832 | tf_op jit(solution)/shard_map/ppermute | solution.py:34
  74.5 5.3 %backward.1.sums_ref = f32[256,64]{1,0:T(8,128)S(1)} custom-call(s32[8]{0:T(128)S(1)} %copy-done.2, bf16[8,8,8,256]{3,2,1,0:T(8,128)(2,1)S(1)} %all-to-all-done.2.residual_hbm, bf16[16,256,2048]{2,1,0:T(8,128)(2,1)} %weights_hbm.3), custom_call_target="tpu_custom_call" | custom-call | flops 536870912 | bytes 8388608 | tf_op jit(solution)/shard_map/backward/pallas_call | solution.py:531
  79.7 0.0 copy-start.7
  79.8 2.5 %all-to-all-done.3.given_ref = f32[16,40,128]{2,1,0:T(8,128)S(1)} async-done(((f32[16,40,128]{2,1,0:T(8,128)}), f32[16,40,128]{2,1,0:T(8,128)S(1)}, u32[]{:S(2)}, u32[]{:S(2)}) %all-to-all-start.3) | async-done | bytes 327712 | tf_op jit(solution)/shard_map/all_to_all | solution.py:790
  82.3 1.0 probe_rows.1
  83.2 0.0 collective-permute-done.4
  83.3 2.6 %all-to-all-start.4 = ((f32[32,16,256]{2,1,0:T(8,128)}), f32[32,16,256]{2,1,0:T(8,128)S(1)}, u32[]{:S(2)}, u32[]{:S(2)}) async-start(f32[32,16,256]{2,1,0:T(8,128)} %probe_rows.1), calls=%async_computation.4 | async-start | bytes 1048576 | tf_op jit(solution)/shard_map/all_to_all | solution.py:799
  85.9 0.0 copy-done.7
  85.9 0.0 copy-start.3
  85.9 1.4 %collective-permute-start.5 = (bf16[2,384,128]{2,1,0:T(8,128)(2,1)S(1)}, bf16[2,384,128]{2,1,0:T(8,128)(2,1)S(1)}, u32[]{:S(2)}, u32[]{:S(2)}) collective-permute-start(bf16[2,384,128]{2,1,0:T(8,128)(2,1)S(1)} %copy-done.7), channel_id=1, source_target_pairs={{8,0},{16,8},{24,16},{9,1},{17,9},{25,17},{10,2},{18,10},{26,18},{... | collective-permute-start | bytes 589832 | tf_op jit(solution)/shard_map/ppermute | solution.py:34
  87.3 13.0 %update.1 = f32[8,256,2048]{2,1,0:T(8,128)} custom-call(s32[8]{0:T(128)S(1)} %copy-done.2, f32[256,64]{1,0:T(8,128)S(1)} %backward.1.sums_ref, f32[16,2048]{1,0:T(8,128)S(1)} %copy-done, f32[8,256,2048]{2,1,0:T(8,128)} %volume_hbm.3), custom_call_target="tpu_custom_call" | custom-call | flops 2147483648 | bytes 33554432 | tf_op jit(solution)/shard_map/update/pallas_call | solution.py:621
  100.4 0.0 collective-permute-done.5
  100.4 0.0 copy-done.3
  100.4 0.0 copy-start.4
  100.4 1.3 %add_bitcast_fusion = f32[1,2,384,512]{3,2,1,0:T(8,128)} fusion(f32[2,384,512]{2,1,0:T(8,128)S(1)} %copy-done.3, bf16[2,384,128]{2,1,0:T(8,128)(2,1)S(1)} %collective-permute-done.5, bf16[2,384,128]{2,1,0:T(8,128)(2,1)S(1)} %collective-permute-done.4), kind=kLoop, calls=%fused_computation | loop fusion | flops 1572864 | bytes 3538944 | tf_op jit(solution)/shard_map/broadcast_in_dim | solution.py:809
  101.7 0.4 all-to-all-done.4
  102.1 0.0 copy-done.4
  102.1 0.9 bitcast_add_fusion
  (4 shorter events, 0.1 us)
Async XLA Ops:
  0.6 8.0 %copy-start.2 = (s32[8]{0:T(128)S(1)}, s32[8]{0:T(128)}, u32[]{:S(2)}) copy-start(s32[8]{0:T(128)} %ids_ref.5) | copy-start | bytes 100
  0.6 8.0 %copy-start = (f32[16,2048]{1,0:T(8,128)S(1)}, f32[16,2048]{1,0:T(8,128)}, u32[]{:S(2)}) copy-start(f32[16,2048]{1,0:T(8,128)} %rays_hbm.3) | copy-start | bytes 393220
  1.9 23.6 %collective-permute-start.1 = (f32[2,384,128]{2,1,0:T(8,128)S(1)}, f32[2,384,128]{2,1,0:T(8,128)S(1)}, u32[]{:S(2)}, u32[]{:S(2)}) collective-permute-start(f32[2,384,128]{2,1,0:T(8,128)S(1)} %get-tuple-element.59), channel_id=1, source_target_pairs={{8,0},{16,8},{24,16},{9,1},{17,9},{25,17},{10,2},{18,10},{26,18},{... | collective-permute-start | bytes 1179656 | tf_op jit(solution)/shard_map/ppermute | solution.py:34
  3.2 22.3 %collective-permute-start = (f32[2,384,128]{2,1,0:T(8,128)S(1)}, f32[2,384,128]{2,1,0:T(8,128)S(1)}, u32[]{:S(2)}, u32[]{:S(2)}) collective-permute-start(f32[2,384,128]{2,1,0:T(8,128)S(1)} %get-tuple-element.60), channel_id=1, source_target_pairs={{0,8},{8,16},{16,24},{1,9},{9,17},{17,25},{2,10},{10,18},{18,26},{... | collective-permute-start | bytes 1179656 | tf_op jit(solution)/shard_map/ppermute | solution.py:34
  20.6 15.3 %all-to-all-start = ((f32[8,8,8,256]{3,2,1,0:T(8,128)}), f32[8,8,8,256]{3,2,1,0:T(8,128)S(1)}, u32[]{:S(2)}, u32[]{:S(2)}) async-start(f32[8,8,8,256]{3,2,1,0:T(8,128)} %forward.1), calls=%async_computation | async-start | bytes 1048576 | tf_op jit(solution)/shard_map/all_to_all | solution.py:742
  25.5 0.8 copy-start.5
  25.5 0.9 copy-start.6
  35.9 24.3 %copy-start.1 = (f32[264,256]{1,0:T(8,128)S(1)}, f32[264,256]{1,0:T(8,128)}, u32[]{:S(2)}) copy-start(f32[264,256]{1,0:T(8,128)} %get-tuple-element.43.refs_0_) | copy-start | bytes 811012
  47.4 1.8 %collective-permute-start.3 = (f32[264,256]{1,0:T(8,128)}, f32[264,256]{1,0:T(8,128)S(1)}, u32[]{:S(2)}, u32[]{:S(2)}) collective-permute-start(f32[264,256]{1,0:T(8,128)} %get-tuple-element.41), channel_id=1, source_target_pairs={{0,4},{4,0},{1,5},{5,1},{2,6},{6,2},{3,7},{7,3},{8,12},{12,8},{9,1... | collective-permute-start | bytes 811016 | tf_op jit(solution)/shard_map/ppermute | solution.py:715
  47.5 23.2 %copy-start.8 = (bf16[2,384,128]{2,1,0:T(8,128)(2,1)S(1)}, bf16[2,384,128]{2,1,0:T(8,128)(2,1)}, u32[]{:S(2)}) copy-start(bf16[2,384,128]{2,1,0:T(8,128)(2,1)} %get-tuple-element.52) | copy-start | bytes 589828
  47.5 0.8 collective-permute-start.2
  49.9 17.3 %all-to-all-start.2 = ((bf16[8,8,8,256]{3,2,1,0:T(8,128)(2,1)}), bf16[8,8,8,256]{3,2,1,0:T(8,128)(2,1)S(1)}, u32[]{:S(2)}, u32[]{:S(2)}) async-start(bf16[8,8,8,256]{3,2,1,0:T(8,128)(2,1)} %broadcast_in_dim.13), calls=%async_computation.2 | async-start | bytes 524288 | tf_op jit(solution)/shard_map/all_to_all | solution.py:785
  67.1 15.1 %all-to-all-start.3 = ((f32[16,40,128]{2,1,0:T(8,128)}), f32[16,40,128]{2,1,0:T(8,128)S(1)}, u32[]{:S(2)}, u32[]{:S(2)}) async-start(f32[16,40,128]{2,1,0:T(8,128)} %probe_parts.1), calls=%async_computation.3 | async-start | bytes 655360 | tf_op jit(solution)/shard_map/all_to_all | solution.py:790
  70.7 12.5 %collective-permute-start.4 = (bf16[2,384,128]{2,1,0:T(8,128)(2,1)S(1)}, bf16[2,384,128]{2,1,0:T(8,128)(2,1)S(1)}, u32[]{:S(2)}, u32[]{:S(2)}) collective-permute-start(bf16[2,384,128]{2,1,0:T(8,128)(2,1)S(1)} %copy-done.8), channel_id=1, source_target_pairs={{0,8},{8,16},{16,24},{1,9},{9,17},{17,25},{2,10},{10,18},{18,26},{... | collective-permute-start | bytes 589832 | tf_op jit(solution)/shard_map/ppermute | solution.py:34
  79.7 6.1 %copy-start.7 = (bf16[2,384,128]{2,1,0:T(8,128)(2,1)S(1)}, bf16[2,384,128]{2,1,0:T(8,128)(2,1)}, u32[]{:S(2)}) copy-start(bf16[2,384,128]{2,1,0:T(8,128)(2,1)} %get-tuple-element.54) | copy-start | bytes 589828
  83.3 18.9 %all-to-all-start.4 = ((f32[32,16,256]{2,1,0:T(8,128)}), f32[32,16,256]{2,1,0:T(8,128)S(1)}, u32[]{:S(2)}, u32[]{:S(2)}) async-start(f32[32,16,256]{2,1,0:T(8,128)} %probe_rows.1), calls=%async_computation.4 | async-start | bytes 1048576 | tf_op jit(solution)/shard_map/all_to_all | solution.py:799
  85.9 14.5 %copy-start.3 = (f32[2,384,512]{2,1,0:T(8,128)S(1)}, f32[2,384,512]{2,1,0:T(8,128)}, u32[]{:S(2)}) copy-start(f32[2,384,512]{2,1,0:T(8,128)} %get-tuple-element.33) | copy-start | bytes 4718596
  85.9 14.5 %collective-permute-start.5 = (bf16[2,384,128]{2,1,0:T(8,128)(2,1)S(1)}, bf16[2,384,128]{2,1,0:T(8,128)(2,1)S(1)}, u32[]{:S(2)}, u32[]{:S(2)}) collective-permute-start(bf16[2,384,128]{2,1,0:T(8,128)(2,1)S(1)} %copy-done.7), channel_id=1, source_target_pairs={{8,0},{16,8},{24,16},{9,1},{17,9},{25,17},{10,2},{18,10},{26,18},{... | collective-permute-start | bytes 589832 | tf_op jit(solution)/shard_map/ppermute | solution.py:34
  100.4 1.8 %copy-start.4 = (f32[2,256,256]{2,1,0:T(8,128)S(1)}, f32[2,256,256]{2,1,0:T(8,128)}, u32[]{:S(2)}) copy-start(f32[2,256,256]{2,1,0:T(8,128)} %probe_hbm.1) | copy-start | bytes 1572868

commit v10 on v9

--- a/solution.py
+++ b/solution.py
@@ -633,7 +633,7 @@
             pltpu.SemaphoreType.DMA((depth,)),
             pltpu.SemaphoreType.DMA((slots,)),
         ],
-        compiler_params=pltpu.CompilerParams(vmem_limit_bytes=TOMO_LIMIT),
+        compiler_params=pltpu.CompilerParams(vmem_limit_bytes=VMEM_LIMIT),
         cost_estimate=pl.CostEstimate(
             flops=8 * rows * width * sums.shape[1] * depth,
             bytes_accessed=2 * depth * rows * width * 4,

time: 104 us -> 101 us (0.971)
  starting transfers between devices: 33.5 us -> 28.7 us
  blocking collectives: 11.5 us -> 15.6 us
  Pallas kernels: 41.5 us -> 37.6 us
  waiting for transfers between devices: 9.87 us -> 11.7 us
    all_to_all x1, starting transfers between devices: 10.3 us -> 5.42 us  [on_device(): residual = lax.all_to_all(copies, flat_axes, 0, 0, tiled=True)]
    all_to_all x1, blocking collectives: 11.5 us -> 15.6 us  [on_device(): pieces = lax.all_to_all(pieces, ('proj', 'cuts'), 0, 0, tiled=True)]
    pallas_call x1, Pallas kernels: 9.55 us -> 7.01 us  [patch_updates(): pl.pallas_call(patch_kernel, in_specs=[SCALARS] * 4 + [ANYWHERE] * 7, out...]
    all_to_all x1, waiting for transfers between devices: 0.42 us -> 1.76 us  [on_device(): steps = lax.all_to_all(steps, ('proj', 'tile', 'cuts'), 0, 0, tiled=True)]
    pallas_call x1, Pallas kernels: 13 us -> 11.7 us  [volume_update(): pl.pallas_call(update_kernel, in_specs=[SCALARS, WHOLE] + [ANYWHERE] * 2,...]
    all_to_all x1, waiting for transfers between devices: 0.01 us -> 1.18 us  [on_device(): arrived = lax.all_to_all(forward, flat_axes, 0, 0, tiled=True)]
  transfers between devices with their start and end apart: 10 -> 10, of which waited for: 4 -> 5; matrix products, arithmetic and copies ran while one was open for 1% -> 1% of each run, Pallas kernels for 40% -> 37%
where the time goes in v10:
time: 101 us
  Pallas kernels  37.6 us (37%)
  starting transfers between devices  28.7 us (28%)
  blocking collectives  15.6 us (15%)
  waiting for transfers between devices  11.7 us (12%)
  local copies, waits for them, and re-layouts  3.46 us (3%)
  other arithmetic  2.24 us (2%)
  between operations  1.56 us (2%)
    all_to_all x1, blocking collectives, on_device(): pieces = lax.all_to_all(pieces, ('proj', 'cuts'), 0, 0, tiled=True)  15.6 us
    ppermute x4, starting transfers between devices, shifted(): lax.ppermute(value, axis, [(source, source + steps) for source in range(l...  11.9 us
    pallas_call x1, Pallas kernels, forward_parts(): pl.pallas_call(forward_kernel, in_specs=[SCALARS] + [ANYWHERE] * 3, out_s...  11.9 us
    pallas_call x1, Pallas kernels, volume_update(): pl.pallas_call(update_kernel, in_specs=[SCALARS, WHOLE] + [ANYWHERE] * 2,...  11.7 us
    pallas_call x1, Pallas kernels, patch_updates(): pl.pallas_call(patch_kernel, in_specs=[SCALARS] * 4 + [ANYWHERE] * 7, out...  7.01 us
    all_to_all x1, waiting for transfers between devices, on_device(): residual = lax.all_to_all(copies, flat_axes, 0, 0, tiled=True)  6.16 us
    all_to_all x1, starting transfers between devices, on_device(): residual = lax.all_to_all(copies, flat_axes, 0, 0, tiled=True)  5.42 us
    pallas_call x1, Pallas kernels, backward_sums(): pl.pallas_call(backward_kernel, in_specs=[SCALARS, ANYWHERE, ANYWHERE], o...  5.28 us
  transfers between devices with their start and end apart: 10, of which 5 were waited for; matrix products, arithmetic and copies ran while one was open for 1% of the time, Pallas kernels for 37%

profile of v10, /device:TPU:0, one launch (start us, length us, event | category | flops | bytes accessed | tf_op | source)
XLA Modules:
  0.0 100.9 jit_solution(5267829802900016066)
XLA Ops:
  0.6 0.0 copy-start.3
  0.6 0.0 copy-start
  0.7 1.2 %fusion = (f32[2,384,128]{2,1,0:T(8,128)S(1)}, f32[2,384,128]{2,1,0:T(8,128)S(1)}) fusion(f32[2,384,512]{2,1,0:T(8,128)} %bitcast.15), kind=kLoop, calls=%fused_computation.3 | loop fusion | bytes 1572864 | tf_op jit(solution)/shard_map/slice | solution.py:739
  1.9 1.3 %collective-permute-start.1 = (f32[2,384,128]{2,1,0:T(8,128)S(1)}, f32[2,384,128]{2,1,0:T(8,128)S(1)}, u32[]{:S(2)}, u32[]{:S(2)}) collective-permute-start(f32[2,384,128]{2,1,0:T(8,128)S(1)} %get-tuple-element.59), channel_id=1, source_target_pairs={{8,0},{16,8},{24,16},{9,1},{17,9},{25,17},{10,2},{18,10},{26,18},{... | collective-permute-start | bytes 1179656 | tf_op jit(solution)/shard_map/ppermute | solution.py:34
  3.2 5.5 %collective-permute-start = (f32[2,384,128]{2,1,0:T(8,128)S(1)}, f32[2,384,128]{2,1,0:T(8,128)S(1)}, u32[]{:S(2)}, u32[]{:S(2)}) collective-permute-start(f32[2,384,128]{2,1,0:T(8,128)S(1)} %get-tuple-element.60), channel_id=1, source_target_pairs={{0,8},{8,16},{16,24},{1,9},{9,17},{17,25},{2,10},{10,18},{18,26},{... | collective-permute-start | bytes 1179656 | tf_op jit(solution)/shard_map/ppermute | solution.py:34
  8.7 0.0 copy-done.3
  8.7 0.0 copy-done
  8.7 11.9 %forward.1 = f32[8,8,8,256]{3,2,1,0:T(8,128)} custom-call(s32[8]{0:T(128)S(1)} %copy-done.3, f32[16,2048]{1,0:T(8,128)S(1)} %copy-done, f32[8,256,2048]{2,1,0:T(8,128)} %volume_hbm.3, bf16[16,256,2048]{2,1,0:T(8,128)(2,1)} %weights_hbm.3), custom_call_target="tpu_custom_call" | custom-call | flops 2147483648 | bytes 25165824 | tf_op jit(solution)/shard_map/forward/pallas_call | solution.py:153
  20.6 4.2 %all-to-all-start = ((f32[8,8,8,256]{3,2,1,0:T(8,128)}), f32[8,8,8,256]{3,2,1,0:T(8,128)S(1)}, u32[]{:S(2)}, u32[]{:S(2)}) async-start(f32[8,8,8,256]{3,2,1,0:T(8,128)} %forward.1), calls=%async_computation | async-start | bytes 1048576 | tf_op jit(solution)/shard_map/all_to_all | solution.py:742
  25.4 0.0 collective-permute-done.1.right_hbm
  25.4 0.0 copy-start.6
  25.5 0.0 collective-permute-done.left_hbm
  25.5 0.0 copy-start.7
  25.5 0.7 copy-done.6
  26.2 0.1 copy-done.7
  26.3 7.0 %patches.1 = (f32[2,384,512]{2,1,0:T(8,128)}, bf16[2,384,128]{2,1,0:T(8,128)(2,1)}, bf16[2,384,128]{2,1,0:T(8,128)(2,1)}, f32[2,4,8,384]{3,2,1,0:T(8,128)}, f32[264,256]{1,0:T(8,128)}, /*index=5*/f32[264,256]{1,0:T(8,128)}) custom-call(s32[6]{0:T(128)} %bitcast.20, s32[6]{0:T(128)} %bitcast.21, s32[1]{0:T(128)} %bitcast.13.count_ref, s32[1]{0:T(128)} %bitcast.3.place_ref, ...), custom_call_target="tpu_custom_call" | custom-call | flops 3221225472 | bytes 6291456 | tf_op jit(solution)/shard_map/patches/pallas_call | solution.py:428
  33.3 0.0 copy-start.2
  33.3 1.2 %all-to-all-done = f32[8,8,8,256]{3,2,1,0:T(8,128)S(1)} async-done(((f32[8,8,8,256]{3,2,1,0:T(8,128)}), f32[8,8,8,256]{3,2,1,0:T(8,128)S(1)}, u32[]{:S(2)}, u32[]{:S(2)}) %all-to-all-start) | async-done | bytes 524320 | tf_op jit(solution)/shard_map/all_to_all | solution.py:742
  34.5 15.6 %all_to_all.25 = f32[8,8,384]{2,1,0:T(8,128)S(1)} all-to-all(f32[8,8,384]{2,1,0:T(8,128)} %bitcast.17), channel_id=1, replica_groups=mesh['tile'=4,'proj'=2,'cuts'=4] {'proj','cuts'}, dimensions={0} | all-to-all | bytes 196608 | tf_op jit(solution)/shard_map/all_to_all | solution.py:764
  50.1 0.1 collective-permute-start.3
  50.3 0.8 collective-permute-start.2
  51.1 0.0 collective-permute-done.2
  51.1 0.8 collective-permute-done.3.refs_1_
  51.9 0.7 broadcast_in_dim.13
  52.6 5.4 %all-to-all-start.2 = ((bf16[8,8,8,256]{3,2,1,0:T(8,128)(2,1)}), bf16[8,8,8,256]{3,2,1,0:T(8,128)(2,1)S(1)}, u32[]{:S(2)}, u32[]{:S(2)}) async-start(bf16[8,8,8,256]{3,2,1,0:T(8,128)(2,1)} %broadcast_in_dim.13), calls=%async_computation.2 | async-start | bytes 524288 | tf_op jit(solution)/shard_map/all_to_all | solution.py:785
  58.0 0.0 copy-done.2
  58.0 0.8 probe_parts.1
  58.8 6.2 %all-to-all-done.2.residual_hbm = bf16[8,8,8,256]{3,2,1,0:T(8,128)(2,1)S(1)} async-done(((bf16[8,8,8,256]{3,2,1,0:T(8,128)(2,1)}), bf16[8,8,8,256]{3,2,1,0:T(8,128)(2,1)S(1)}, u32[]{:S(2)}, u32[]{:S(2)}) %all-to-all-start.2) | async-done | bytes 262176 | tf_op jit(solution)/shard_map/all_to_all | solution.py:785
  65.0 3.5 %all-to-all-start.3 = ((f32[16,40,128]{2,1,0:T(8,128)}), f32[16,40,128]{2,1,0:T(8,128)S(1)}, u32[]{:S(2)}, u32[]{:S(2)}) async-start(f32[16,40,128]{2,1,0:T(8,128)} %probe_parts.1), calls=%async_computation.3 | async-start | bytes 655360 | tf_op jit(solution)/shard_map/all_to_all | solution.py:790
  68.5 0.0 copy-done.9
  68.5 3.7 %collective-permute-start.4 = (bf16[2,384,128]{2,1,0:T(8,128)(2,1)S(1)}, bf16[2,384,128]{2,1,0:T(8,128)(2,1)S(1)}, u32[]{:S(2)}, u32[]{:S(2)}) collective-permute-start(bf16[2,384,128]{2,1,0:T(8,128)(2,1)S(1)} %copy-done.9), channel_id=1, source_target_pairs={{0,8},{8,16},{16,24},{1,9},{9,17},{17,25},{2,10},{10,18},{18,26},{... | collective-permute-start | bytes 589832 | tf_op jit(solution)/shard_map/ppermute | solution.py:34
  72.3 5.3 %backward.1.sums_ref = f32[256,64]{1,0:T(8,128)S(1)} custom-call(s32[8]{0:T(128)S(1)} %copy-done.3, bf16[8,8,8,256]{3,2,1,0:T(8,128)(2,1)S(1)} %all-to-all-done.2.residual_hbm, bf16[16,256,2048]{2,1,0:T(8,128)(2,1)} %weights_hbm.3), custom_call_target="tpu_custom_call" | custom-call | flops 536870912 | bytes 8388608 | tf_op jit(solution)/shard_map/backward/pallas_call | solution.py:531
  77.6 0.0 copy-start.1
  77.6 0.6 copy-done.1
  78.2 1.9 %all-to-all-done.3.given_ref = f32[16,40,128]{2,1,0:T(8,128)S(1)} async-done(((f32[16,40,128]{2,1,0:T(8,128)}), f32[16,40,128]{2,1,0:T(8,128)S(1)}, u32[]{:S(2)}, u32[]{:S(2)}) %all-to-all-start.3) | async-done | bytes 327712 | tf_op jit(solution)/shard_map/all_to_all | solution.py:790
  80.1 1.0 probe_rows.1
  81.1 0.0 collective-permute-done.4
  81.1 2.7 %all-to-all-start.4 = ((f32[32,16,256]{2,1,0:T(8,128)}), f32[32,16,256]{2,1,0:T(8,128)S(1)}, u32[]{:S(2)}, u32[]{:S(2)}) async-start(f32[32,16,256]{2,1,0:T(8,128)} %probe_rows.1), calls=%async_computation.4 | async-start | bytes 1048576 | tf_op jit(solution)/shard_map/all_to_all | solution.py:799
  83.8 0.0 copy-done.8
  83.8 0.0 copy-start.4
  83.8 1.4 %collective-permute-start.5 = (bf16[2,384,128]{2,1,0:T(8,128)(2,1)S(1)}, bf16[2,384,128]{2,1,0:T(8,128)(2,1)S(1)}, u32[]{:S(2)}, u32[]{:S(2)}) collective-permute-start(bf16[2,384,128]{2,1,0:T(8,128)(2,1)S(1)} %copy-done.8), channel_id=1, source_target_pairs={{8,0},{16,8},{24,16},{9,1},{17,9},{25,17},{10,2},{18,10},{26,18},{... | collective-permute-start | bytes 589832 | tf_op jit(solution)/shard_map/ppermute | solution.py:34
  85.3 11.7 %update.1 = f32[8,256,2048]{2,1,0:T(8,128)} custom-call(s32[8]{0:T(128)} %ids_ref.5, f32[256,64]{1,0:T(8,128)} %copy-done.1, f32[16,2048]{1,0:T(8,128)} %rays_hbm.3, f32[8,256,2048]{2,1,0:T(8,128)} %volume_hbm.3), custom_call_target="tpu_custom_call" | custom-call | flops 2147483648 | bytes 33554432 | tf_op jit(solution)/shard_map/update/pallas_call | solution.py:621
  97.0 0.0 collective-permute-done.5
  97.0 0.0 copy-done.4
  97.0 0.0 copy-start.5
  97.0 1.3 %add_bitcast_fusion = f32[1,2,384,512]{3,2,1,0:T(8,128)} fusion(f32[2,384,512]{2,1,0:T(8,128)S(1)} %copy-done.4, bf16[2,384,128]{2,1,0:T(8,128)(2,1)S(1)} %collective-permute-done.5, bf16[2,384,128]{2,1,0:T(8,128)(2,1)S(1)} %collective-permute-done.4), kind=kLoop, calls=%fused_computation | loop fusion | flops 1572864 | bytes 3538944 | tf_op jit(solution)/shard_map/broadcast_in_dim | solution.py:809
  98.3 1.8 %all-to-all-done.4 = f32[32,16,256]{2,1,0:T(8,128)S(1)} async-done(((f32[32,16,256]{2,1,0:T(8,128)}), f32[32,16,256]{2,1,0:T(8,128)S(1)}, u32[]{:S(2)}, u32[]{:S(2)}) %all-to-all-start.4) | async-done | bytes 524320 | tf_op jit(solution)/shard_map/all_to_all | solution.py:799
  100.1 0.9 bitcast_add_fusion
  (6 shorter events, 0.1 us)
Async XLA Ops:
  0.6 8.0 %copy-start.3 = (s32[8]{0:T(128)S(1)}, s32[8]{0:T(128)}, u32[]{:S(2)}) copy-start(s32[8]{0:T(128)} %ids_ref.5) | copy-start | bytes 100
  0.6 8.0 %copy-start = (f32[16,2048]{1,0:T(8,128)S(1)}, f32[16,2048]{1,0:T(8,128)}, u32[]{:S(2)}) copy-start(f32[16,2048]{1,0:T(8,128)} %rays_hbm.3) | copy-start | bytes 393220
  1.9 23.6 %collective-permute-start.1 = (f32[2,384,128]{2,1,0:T(8,128)S(1)}, f32[2,384,128]{2,1,0:T(8,128)S(1)}, u32[]{:S(2)}, u32[]{:S(2)}) collective-permute-start(f32[2,384,128]{2,1,0:T(8,128)S(1)} %get-tuple-element.59), channel_id=1, source_target_pairs={{8,0},{16,8},{24,16},{9,1},{17,9},{25,17},{10,2},{18,10},{26,18},{... | collective-permute-start | bytes 1179656 | tf_op jit(solution)/shard_map/ppermute | solution.py:34
  3.2 22.3 %collective-permute-start = (f32[2,384,128]{2,1,0:T(8,128)S(1)}, f32[2,384,128]{2,1,0:T(8,128)S(1)}, u32[]{:S(2)}, u32[]{:S(2)}) collective-permute-start(f32[2,384,128]{2,1,0:T(8,128)S(1)} %get-tuple-element.60), channel_id=1, source_target_pairs={{0,8},{8,16},{16,24},{1,9},{9,17},{17,25},{2,10},{10,18},{18,26},{... | collective-permute-start | bytes 1179656 | tf_op jit(solution)/shard_map/ppermute | solution.py:34
  20.6 14.0 %all-to-all-start = ((f32[8,8,8,256]{3,2,1,0:T(8,128)}), f32[8,8,8,256]{3,2,1,0:T(8,128)S(1)}, u32[]{:S(2)}, u32[]{:S(2)}) async-start(f32[8,8,8,256]{3,2,1,0:T(8,128)} %forward.1), calls=%async_computation | async-start | bytes 1048576 | tf_op jit(solution)/shard_map/all_to_all | solution.py:742
  25.4 0.7 copy-start.6
  25.5 0.9 copy-start.7
  33.3 24.7 %copy-start.2 = (f32[264,256]{1,0:T(8,128)S(1)}, f32[264,256]{1,0:T(8,128)}, u32[]{:S(2)}) copy-start(f32[264,256]{1,0:T(8,128)} %get-tuple-element.43.refs_0_) | copy-start | bytes 811012
  50.1 1.8 %collective-permute-start.3 = (f32[264,256]{1,0:T(8,128)}, f32[264,256]{1,0:T(8,128)S(1)}, u32[]{:S(2)}, u32[]{:S(2)}) collective-permute-start(f32[264,256]{1,0:T(8,128)} %get-tuple-element.41), channel_id=1, source_target_pairs={{0,4},{4,0},{1,5},{5,1},{2,6},{6,2},{3,7},{7,3},{8,12},{12,8},{9,1... | collective-permute-start | bytes 811016 | tf_op jit(solution)/shard_map/ppermute | solution.py:715
  50.3 18.3 %copy-start.9 = (bf16[2,384,128]{2,1,0:T(8,128)(2,1)S(1)}, bf16[2,384,128]{2,1,0:T(8,128)(2,1)}, u32[]{:S(2)}) copy-start(bf16[2,384,128]{2,1,0:T(8,128)(2,1)} %get-tuple-element.52) | copy-start | bytes 589828
  50.3 0.8 collective-permute-start.2
  52.6 12.4 %all-to-all-start.2 = ((bf16[8,8,8,256]{3,2,1,0:T(8,128)(2,1)}), bf16[8,8,8,256]{3,2,1,0:T(8,128)(2,1)S(1)}, u32[]{:S(2)}, u32[]{:S(2)}) async-start(bf16[8,8,8,256]{3,2,1,0:T(8,128)(2,1)} %broadcast_in_dim.13), calls=%async_computation.2 | async-start | bytes 524288 | tf_op jit(solution)/shard_map/all_to_all | solution.py:785
  65.0 15.1 %all-to-all-start.3 = ((f32[16,40,128]{2,1,0:T(8,128)}), f32[16,40,128]{2,1,0:T(8,128)S(1)}, u32[]{:S(2)}, u32[]{:S(2)}) async-start(f32[16,40,128]{2,1,0:T(8,128)} %probe_parts.1), calls=%async_computation.3 | async-start | bytes 655360 | tf_op jit(solution)/shard_map/all_to_all | solution.py:790
  68.5 12.5 %collective-permute-start.4 = (bf16[2,384,128]{2,1,0:T(8,128)(2,1)S(1)}, bf16[2,384,128]{2,1,0:T(8,128)(2,1)S(1)}, u32[]{:S(2)}, u32[]{:S(2)}) collective-permute-start(bf16[2,384,128]{2,1,0:T(8,128)(2,1)S(1)} %copy-done.9), channel_id=1, source_target_pairs={{0,8},{8,16},{16,24},{1,9},{9,17},{17,25},{2,10},{10,18},{18,26},{... | collective-permute-start | bytes 589832 | tf_op jit(solution)/shard_map/ppermute | solution.py:34
  77.6 0.7 copy-start.1
  78.2 5.6 %copy-start.8 = (bf16[2,384,128]{2,1,0:T(8,128)(2,1)S(1)}, bf16[2,384,128]{2,1,0:T(8,128)(2,1)}, u32[]{:S(2)}) copy-start(bf16[2,384,128]{2,1,0:T(8,128)(2,1)} %get-tuple-element.54) | copy-start | bytes 589828
  81.1 19.0 %all-to-all-start.4 = ((f32[32,16,256]{2,1,0:T(8,128)}), f32[32,16,256]{2,1,0:T(8,128)S(1)}, u32[]{:S(2)}, u32[]{:S(2)}) async-start(f32[32,16,256]{2,1,0:T(8,128)} %probe_rows.1), calls=%async_computation.4 | async-start | bytes 1048576 | tf_op jit(solution)/shard_map/all_to_all | solution.py:799
  83.8 13.1 %copy-start.4 = (f32[2,384,512]{2,1,0:T(8,128)S(1)}, f32[2,384,512]{2,1,0:T(8,128)}, u32[]{:S(2)}) copy-start(f32[2,384,512]{2,1,0:T(8,128)} %get-tuple-element.33) | copy-start | bytes 4718596
  83.8 13.1 %collective-permute-start.5 = (bf16[2,384,128]{2,1,0:T(8,128)(2,1)S(1)}, bf16[2,384,128]{2,1,0:T(8,128)(2,1)S(1)}, u32[]{:S(2)}, u32[]{:S(2)}) collective-permute-start(bf16[2,384,128]{2,1,0:T(8,128)(2,1)S(1)} %copy-done.8), channel_id=1, source_target_pairs={{8,0},{16,8},{24,16},{9,1},{17,9},{25,17},{10,2},{18,10},{26,18},{... | collective-permute-start | bytes 589832 | tf_op jit(solution)/shard_map/ppermute | solution.py:34
  97.0 3.1 %copy-start.5 = (f32[2,256,256]{2,1,0:T(8,128)S(1)}, f32[2,256,256]{2,1,0:T(8,128)}, u32[]{:S(2)}) copy-start(f32[2,256,256]{2,1,0:T(8,128)} %probe_hbm.1) | copy-start | bytes 1572868
